TPU v7x, 32 devices: a whole 2x2x4 slice. The times are simulated.
32 devices in a mesh: fsdp: 2 (over y), context: 8 (over z, x), tensor: 2 (over core).
Axes of the slice: x: 2, y: 2, z: 4, core: 2. Of those that a mesh axis runs over, the one named last changes fastest.
Arguments:
- tokens: bfloat16 [2, 2048, 2048], P(None, ('fsdp', 'context'), 'tensor'), may hold values from -6 to 6
- cotangent: bfloat16 [2, 2048, 2048], P(None, ('fsdp', 'context'), 'tensor'), may hold values from -6 to 6
- lengths: int32 [2, 2, 4], replicated, may hold values from 1 to 512, 1024 in all within a row
- permutation: int32 [2, 2048], replicated, may hold values from 0 to 2047, as said below
- ln_gain: bfloat16 [2048], P('fsdp'), may hold values from 0.099609375 to 1.8984375
- ln_bias: bfloat16 [2048], P('fsdp'), may hold values from -3 to 3
- qkv_weight: bfloat16 [2048, 3, 2048], P('fsdp', None, 'tensor'), may hold values from -0.125 to 0.125
- qkv_bias: bfloat16 [3, 32, 64], P(None, 'tensor', 'fsdp'), may hold values from -3 to 3
- dense_weight: bfloat16 [2048, 2048], P('tensor', 'fsdp'), may hold values from -1 to 1
- dense_bias: bfloat16 [2048], P('fsdp'), may hold values from -4.5 to 4.5
- fc1_weight: bfloat16 [2048, 8192], P('fsdp', 'tensor'), may hold values from -0.125 to 0.125
- fc1_bias: bfloat16 [32, 256], P('tensor', 'fsdp'), may hold values from -3 to 3
- fc2_weight: bfloat16 [8192, 2048], P('tensor', 'fsdp'), may hold values from -0.0625 to 0.0625
- fc2_bias: bfloat16 [2048], P('fsdp'), may hold values from -4.5 to 4.5
Outputs:
- layer_out: bfloat16 [2, 2048, 2048], P(None, ('fsdp', 'context'), 'tensor')
- grad_tokens: bfloat16 [2, 2048, 2048], P(None, ('fsdp', 'context'), 'tensor')
- grad_ln_gain: float32 [2048], P('fsdp')
- grad_ln_bias: float32 [2048], P('fsdp')
- grad_qkv_weight: float32 [2048, 3, 2048], P('fsdp', None, 'tensor')
- grad_qkv_bias: float32 [3, 32, 64], P(None, 'tensor', 'fsdp')
- grad_dense_weight: float32 [2048, 2048], P('tensor', 'fsdp')
- grad_dense_bias: float32 [2048], P('fsdp')
- grad_fc1_weight: float32 [2048, 8192], P('fsdp', 'tensor')
- grad_fc1_bias: float32 [32, 256], P('tensor', 'fsdp')
- grad_fc2_weight: float32 [8192, 2048], P('tensor', 'fsdp')
- grad_fc2_bias: float32 [2048], P('fsdp')
Inputs may be any that keep to these rules, and one draw needn't show every extreme that they name: Each micro-batch's lengths of one pack sum to 1024. Each row is a permutation; the 128 arriving tokens at rows s * 128 to (s + 1) * 128 - 1 take exactly 8 positions of every aligned block of 128 layout positions.
All inputs are finite; a program needn't handle non-finite values.
Results may differ from a plain program's by a relative error of at most 0.033.
Values may be sent and summed in bfloat16 or wider, within the bound.
A program may use at most 320 MiB of HBM per device.

v0:
```python
from functools import partial

import jax
import jax.numpy as jnp
from jax import lax
from jax.sharding import PartitionSpec as P

ROT = 32


EPSILON = 1e-05
ROPE_BASE = 10000.0
NEG_FILL = -1e30


def layer_norm(values, gain, shift):
    center = values - jnp.mean(values, axis=-1, keepdims=True)
    spread = jnp.mean(center * center, axis=-1, keepdims=True)
    return center * lax.rsqrt(spread + EPSILON) * gain + shift


def rotate(values, position):
    half = ROT // 2
    freq = ROPE_BASE ** (-2.0 * jnp.arange(half, dtype=jnp.float32) / ROT)
    angles = position[:, None] * freq[None, :]
    cosine = jnp.cos(angles)[:, None, :]
    sine = jnp.sin(angles)[:, None, :]
    first = values[..., :half]
    second = values[..., half:ROT]
    return jnp.concatenate(
        [first * cosine - second * sine, second * cosine + first * sine, values[..., ROT:]], axis=-1
    )


def segment_layout(length_row, places):
    ends = jnp.cumsum(length_row)
    starts = ends - length_row
    segment = jnp.sum((places[:, None] >= ends[None, :]).astype(jnp.int32), axis=1)
    match = segment[:, None] == jnp.arange(length_row.shape[0], dtype=jnp.int32)[None, :]
    begin = jnp.sum(jnp.where(match, starts[None, :], 0), axis=1)
    return (segment, places - begin)


def rows_block(source, block_index, block_rows, head_count, head_width):
    return lax.dynamic_slice_in_dim(source, block_index * block_rows, block_rows, 0).reshape(
        block_rows, head_count, head_width
    )


def pair_mask(query_segment, query_place, key_segment, key_place):
    return (
        (query_segment[:, None] == key_segment[None, :])
        & (key_place[None, :] <= query_place[:, None])
    )[None]


def key_scores(
    query,
    keys_all,
    key_segment,
    key_place,
    query_segment,
    query_place,
    block_index,
    block_rows,
    scale,
):
    row_count, head_count, head_width = query.shape
    key_block = rows_block(keys_all, block_index, block_rows, head_count, head_width)
    scores = (
        jnp.einsum("qhe,khe->hqk", query, key_block, preferred_element_type=jnp.float32) * scale
    )
    segment_block = lax.dynamic_slice_in_dim(key_segment, block_index * block_rows, block_rows, 0)
    place_block = lax.dynamic_slice_in_dim(key_place, block_index * block_rows, block_rows, 0)
    return (scores, pair_mask(query_segment, query_place, segment_block, place_block), key_block)


def attend_forward(
    query,
    keys_all,
    values_all,
    key_segment,
    key_place,
    query_segment,
    query_place,
    first_block,
    last_block,
    block_rows,
    scale,
):
    row_count, head_count, head_width = query.shape

    def find_peak(block_index, carry):
        peak, total = carry
        scores, allowed, _ = key_scores(
            query,
            keys_all,
            key_segment,
            key_place,
            query_segment,
            query_place,
            block_index,
            block_rows,
            scale,
        )
        fresh = jnp.maximum(peak, jnp.max(jnp.where(allowed, scores, NEG_FILL), axis=-1))
        added = jnp.sum(jnp.where(allowed, jnp.exp(scores - fresh[..., None]), 0.0), axis=-1)
        return (fresh, total * jnp.exp(peak - fresh) + added)

    start_carry = (
        jnp.full((head_count, row_count), NEG_FILL, jnp.float32),
        jnp.zeros((head_count, row_count), jnp.float32),
    )
    peak, total = lax.fori_loop(first_block, last_block + 1, find_peak, start_carry)
    log_total = peak + jnp.log(total)

    def weigh(block_index, accum):
        scores, allowed, _ = key_scores(
            query,
            keys_all,
            key_segment,
            key_place,
            query_segment,
            query_place,
            block_index,
            block_rows,
            scale,
        )
        attend_weights = jnp.where(allowed, jnp.exp(scores - log_total[..., None]), 0.0).astype(
            jnp.bfloat16
        )
        values = rows_block(values_all, block_index, block_rows, head_count, head_width)
        return accum + jnp.einsum(
            "hqk,khe->qhe", attend_weights, values, preferred_element_type=jnp.float32
        )

    attended = lax.fori_loop(
        first_block, last_block + 1, weigh, jnp.zeros(query.shape, jnp.float32)
    )
    return (attended, log_total)


def attend_backward(
    query,
    keys_all,
    values_all,
    key_segment,
    key_place,
    query_segment,
    query_place,
    first_block,
    last_block,
    block_rows,
    scale,
    log_total,
    grad_out,
    delta,
):
    row_count, head_count, head_width = query.shape

    def step_back(block_index, carry):
        scores, allowed, key_block = key_scores(
            query,
            keys_all,
            key_segment,
            key_place,
            query_segment,
            query_place,
            block_index,
            block_rows,
            scale,
        )
        values = rows_block(values_all, block_index, block_rows, head_count, head_width)
        attend_weights = jnp.where(allowed, jnp.exp(scores - log_total[..., None]), 0.0)
        grad_weights = jnp.einsum(
            "qhe,khe->hqk", grad_out, values, preferred_element_type=jnp.float32
        )
        grad_scores = (attend_weights * (grad_weights - delta[..., None])).astype(jnp.bfloat16)
        grad_query = (
            carry[0]
            + jnp.einsum("hqk,khe->qhe", grad_scores, key_block, preferred_element_type=jnp.float32)
            * scale
        )
        grad_keys, grad_values = (carry[1], carry[2])
        key_part = (
            jnp.einsum("hqk,qhe->khe", grad_scores, query, preferred_element_type=jnp.float32)
            * scale
        ).reshape(block_rows, head_count * head_width)
        value_part = jnp.einsum(
            "hqk,qhe->khe",
            attend_weights.astype(jnp.bfloat16),
            grad_out,
            preferred_element_type=jnp.float32,
        ).reshape(block_rows, head_count * head_width)
        block_start = block_index * block_rows
        grad_keys = lax.dynamic_update_slice_in_dim(
            grad_keys,
            lax.dynamic_slice_in_dim(grad_keys, block_start, block_rows, 0) + key_part,
            block_start,
            0,
        )
        grad_values = lax.dynamic_update_slice_in_dim(
            grad_values,
            lax.dynamic_slice_in_dim(grad_values, block_start, block_rows, 0) + value_part,
            block_start,
            0,
        )
        return (grad_query, grad_keys, grad_values)

    start_carry = (
        jnp.zeros(query.shape, jnp.float32),
        jnp.zeros(keys_all.shape, jnp.float32),
        jnp.zeros(values_all.shape, jnp.float32),
    )
    return lax.fori_loop(first_block, last_block + 1, step_back, start_carry)


def body(
    tokens,
    cotangent,
    lengths,
    permutation,
    ln_gain,
    ln_bias,
    qkv_weight,
    qkv_bias,
    dense_weight,
    dense_bias,
    fc1_weight,
    fc1_bias,
    fc2_weight,
    fc2_bias,
):
    gain_all, shift_all, w_qkv, b_qkv, w_dense, b_dense, w_fc1, b_fc1, w_fc2, b_fc2 = (
        lax.all_gather(ln_gain, "fsdp", axis=0, tiled=True),
        lax.all_gather(ln_bias, "fsdp", axis=0, tiled=True),
        lax.all_gather(qkv_weight, "fsdp", axis=0, tiled=True),
        lax.all_gather(qkv_bias, "fsdp", axis=2, tiled=True),
        lax.all_gather(dense_weight, "fsdp", axis=1, tiled=True),
        lax.all_gather(dense_bias, "fsdp", axis=0, tiled=True),
        lax.all_gather(fc1_weight, "fsdp", axis=0, tiled=True),
        lax.all_gather(fc1_bias, "fsdp", axis=1, tiled=True),
        lax.all_gather(fc2_weight, "fsdp", axis=1, tiled=True),
        lax.all_gather(fc2_bias, "fsdp", axis=0, tiled=True),
    )
    gain_f = gain_all.astype(jnp.float32)
    shift_f = shift_all.astype(jnp.float32)
    local_width = w_qkv.shape[2]
    head_count = b_qkv.shape[1]
    head_width = b_qkv.shape[2]
    hidden_local = w_fc1.shape[1]
    qkv_shift = b_qkv.astype(jnp.float32).reshape(3, local_width)
    fc1_shift = b_fc1.astype(jnp.float32).reshape(hidden_local)
    micro_count = tokens.shape[0]
    row_count = tokens.shape[1]
    feature_share = tokens.shape[2]
    all_rows = micro_count * row_count
    pack_length = row_count * lax.axis_size("context")
    block_rows = min(512, pack_length)
    group_index = lax.axis_index(("fsdp", "context"))
    pack_index = lax.axis_index("fsdp")
    context_index = lax.axis_index("context")
    tensor_index = lax.axis_index("tensor")
    out_shift = lax.dynamic_slice_in_dim(
        b_dense.astype(jnp.float32) + b_fc2.astype(jnp.float32),
        tensor_index * feature_share,
        feature_share,
        0,
    )
    scale = head_width ** (-0.5)
    counting = jnp.arange(row_count, dtype=jnp.int32)
    pack_places = jnp.arange(pack_length, dtype=jnp.int32)
    query_place = lax.dynamic_slice_in_dim(pack_places, context_index * row_count, row_count, 0)
    last_query_block = (context_index * row_count + row_count - 1) // block_rows
    sent_tokens = []
    sent_cot = []
    slot_sources = []
    arrive_slots = []
    return_orders = []
    key_segments = []
    query_segments = []
    query_positions = []
    first_blocks = []
    length_rows = []
    for micro_index in range(micro_count):
        perm_row = permutation[micro_index]
        own_targets = lax.dynamic_slice_in_dim(perm_row, group_index * row_count, row_count, 0)
        send_order = jnp.argsort(own_targets // row_count, stable=True)
        return_orders.append(jnp.zeros(row_count, jnp.int32).at[send_order].set(counting))
        arriving = jnp.nonzero(perm_row // row_count == group_index, size=row_count)[0]
        arrive_slot = perm_row[arriving] % row_count
        arrive_slots.append(arrive_slot)
        slot_sources.append(jnp.zeros(row_count, jnp.int32).at[arrive_slot].set(counting))
        sent_tokens.append(tokens[micro_index][send_order])
        sent_cot.append(cotangent[micro_index][send_order])
        length_row = lax.dynamic_index_in_dim(lengths[micro_index], pack_index, 0, keepdims=False)
        length_rows.append(length_row)
        key_segment, key_position = segment_layout(length_row, pack_places)
        key_segments.append(key_segment)
        query_segments.append(
            lax.dynamic_slice_in_dim(key_segment, context_index * row_count, row_count, 0)
        )
        query_position = lax.dynamic_slice_in_dim(
            key_position, context_index * row_count, row_count, 0
        )
        query_positions.append(query_position)
        first_blocks.append((query_place[0] - query_position[0]) // block_rows)
    received = (
        lax.all_to_all(
            jnp.stack(sent_tokens), ("fsdp", "context"), split_axis=1, concat_axis=1, tiled=True
        ),
        lax.all_to_all(
            jnp.stack(sent_cot), ("fsdp", "context"), split_axis=1, concat_axis=1, tiled=True
        ),
    )
    own_tokens = jnp.concatenate(
        [received[0][m][slot_sources[m]] for m in range(micro_count)], axis=0
    )
    own_cot = jnp.concatenate([received[1][m][slot_sources[m]] for m in range(micro_count)], axis=0)
    full_tokens, full_cot = (
        lax.all_gather(own_tokens, "tensor", axis=1, tiled=True),
        lax.all_gather(own_cot, "tensor", axis=1, tiled=True),
    )
    normed, norm_back = jax.vjp(layer_norm, full_tokens.astype(jnp.float32), gain_f, shift_f)
    normed_b = normed.astype(jnp.bfloat16)
    qkv = jnp.einsum("rd,dce->rce", normed_b, w_qkv, preferred_element_type=jnp.float32) + qkv_shift
    angle_pos = jnp.concatenate(query_positions, axis=0).astype(jnp.float32)
    query_rot, rope_back = jax.vjp(
        lambda inner: rotate(inner, angle_pos), qkv[:, 0].reshape(all_rows, head_count, head_width)
    )
    key_rot = rotate(qkv[:, 1].reshape(all_rows, head_count, head_width), angle_pos)
    query_b = query_rot.astype(jnp.bfloat16)
    key_b = key_rot.reshape(all_rows, local_width).astype(jnp.bfloat16)
    value_b = qkv[:, 2].astype(jnp.bfloat16)
    keys_all, values_all = (
        lax.all_gather(
            key_b.reshape(micro_count, row_count, local_width), "context", axis=1, tiled=True
        ),
        lax.all_gather(
            value_b.reshape(micro_count, row_count, local_width), "context", axis=1, tiled=True
        ),
    )
    attended_list = []
    log_list = []
    for micro_index in range(micro_count):
        rows = slice(micro_index * row_count, (micro_index + 1) * row_count)
        attended_one, log_one = attend_forward(
            query_b[rows],
            keys_all[micro_index],
            values_all[micro_index],
            key_segments[micro_index],
            pack_places,
            query_segments[micro_index],
            query_place,
            first_blocks[micro_index],
            last_query_block,
            block_rows,
            scale,
        )
        attended_list.append(attended_one)
        log_list.append(log_one)
    attended = jnp.concatenate(attended_list, axis=0)
    attended_b = attended.reshape(all_rows, local_width).astype(jnp.bfloat16)
    pre_act = jnp.dot(normed_b, w_fc1, preferred_element_type=jnp.float32) + fc1_shift
    activ, gelu_back = jax.vjp(partial(jax.nn.gelu, approximate=True), pre_act)
    activ_b = activ.astype(jnp.bfloat16)
    partial_out = jnp.dot(attended_b, w_dense, preferred_element_type=jnp.float32) + jnp.dot(
        activ_b, w_fc2, preferred_element_type=jnp.float32
    )
    branch = lax.psum_scatter(
        partial_out.astype(jnp.bfloat16), "tensor", scatter_dimension=1, tiled=True
    ).astype(jnp.float32)
    layer_rows = (own_tokens.astype(jnp.float32) + branch + out_shift).astype(jnp.bfloat16)
    grad_attended = jnp.einsum(
        "rd,ed->re", full_cot, w_dense, preferred_element_type=jnp.float32
    ).astype(jnp.bfloat16)
    grad_activ = jnp.einsum("rd,hd->rh", full_cot, w_fc2, preferred_element_type=jnp.float32)
    grad_pre = gelu_back(grad_activ)[0].astype(jnp.bfloat16)
    grad_heads = grad_attended.reshape(all_rows, head_count, head_width)
    delta_list = []
    for micro_index in range(micro_count):
        rows = slice(micro_index * row_count, (micro_index + 1) * row_count)
        delta_list.append(
            jnp.einsum(
                "qhe,qhe->hq", grad_heads[rows].astype(jnp.float32), attended_list[micro_index]
            )
        )
    query_grads = []
    key_parts = []
    value_parts = []
    for micro_index in range(micro_count):
        rows = slice(micro_index * row_count, (micro_index + 1) * row_count)
        grad_query_one, grad_keys_one, grad_values_one = attend_backward(
            query_b[rows],
            keys_all[micro_index],
            values_all[micro_index],
            key_segments[micro_index],
            pack_places,
            query_segments[micro_index],
            query_place,
            first_blocks[micro_index],
            last_query_block,
            block_rows,
            scale,
            log_list[micro_index],
            grad_heads[rows],
            delta_list[micro_index],
        )
        query_grads.append(grad_query_one)
        key_parts.append(grad_keys_one)
        value_parts.append(grad_values_one)
    grad_keys, grad_values = (
        lax.psum_scatter(
            jnp.stack(key_parts).astype(jnp.bfloat16), "context", scatter_dimension=1, tiled=True
        ).astype(jnp.float32),
        lax.psum_scatter(
            jnp.stack(value_parts).astype(jnp.bfloat16), "context", scatter_dimension=1, tiled=True
        ).astype(jnp.float32),
    )
    grad_keys = grad_keys.reshape(all_rows, local_width)
    grad_values = grad_values.reshape(all_rows, local_width)
    grad_query = jnp.concatenate(query_grads, axis=0)
    grad_query_pre = rope_back(grad_query)[0].reshape(all_rows, local_width)
    grad_key_pre = rope_back(grad_keys.reshape(all_rows, head_count, head_width))[0].reshape(
        all_rows, local_width
    )
    grad_qkv = jnp.stack([grad_query_pre, grad_key_pre, grad_values], axis=1).astype(jnp.bfloat16)
    grad_normed_part = jnp.einsum(
        "rce,dce->rd", grad_qkv, w_qkv, preferred_element_type=jnp.float32
    ) + jnp.einsum("rh,dh->rd", grad_pre, w_fc1, preferred_element_type=jnp.float32)
    grad_normed = lax.psum(grad_normed_part.astype(jnp.bfloat16), "tensor").astype(jnp.float32)
    grad_input, grad_gain, grad_shift = norm_back(grad_normed)
    cot_f = full_cot.astype(jnp.float32)
    grad_own = lax.dynamic_slice_in_dim(
        cot_f + grad_input, tensor_index * feature_share, feature_share, 1
    ).astype(jnp.bfloat16)
    cot_total = jnp.sum(cot_f, axis=0)
    part_qkv_w = jnp.einsum("rd,rce->dce", normed_b, grad_qkv, preferred_element_type=jnp.float32)
    part_qkv_b = jnp.sum(grad_qkv.astype(jnp.float32), axis=0).reshape(b_qkv.shape)
    part_dense_w = jnp.einsum("re,rd->ed", attended_b, full_cot, preferred_element_type=jnp.float32)
    part_fc1_w = jnp.einsum("rd,rh->dh", normed_b, grad_pre, preferred_element_type=jnp.float32)
    part_fc1_b = jnp.sum(grad_pre.astype(jnp.float32), axis=0).reshape(b_fc1.shape)
    part_fc2_w = jnp.einsum("rh,rd->hd", activ_b, full_cot, preferred_element_type=jnp.float32)
    back_rows = []
    back_grads = []
    for micro_index in range(micro_count):
        rows = slice(micro_index * row_count, (micro_index + 1) * row_count)
        back_rows.append(layer_rows[rows][arrive_slots[micro_index]])
        back_grads.append(grad_own[rows][arrive_slots[micro_index]])
    returned = (
        lax.all_to_all(
            jnp.stack(back_rows), ("fsdp", "context"), split_axis=1, concat_axis=1, tiled=True
        ),
        lax.all_to_all(
            jnp.stack(back_grads), ("fsdp", "context"), split_axis=1, concat_axis=1, tiled=True
        ),
    )
    layer_out = jnp.stack([returned[0][m][return_orders[m]] for m in range(micro_count)])
    grad_tokens = jnp.stack([returned[1][m][return_orders[m]] for m in range(micro_count)])
    shares = (
        lax.psum_scatter(
            grad_gain.astype(jnp.bfloat16), ("fsdp", "context"), scatter_dimension=0, tiled=True
        ).astype(jnp.float32),
        lax.psum_scatter(
            grad_shift.astype(jnp.bfloat16), ("fsdp", "context"), scatter_dimension=0, tiled=True
        ).astype(jnp.float32),
        lax.psum_scatter(
            part_qkv_w.astype(jnp.bfloat16), ("fsdp", "context"), scatter_dimension=0, tiled=True
        ).astype(jnp.float32),
        lax.psum_scatter(
            part_qkv_b.astype(jnp.bfloat16), ("fsdp", "context"), scatter_dimension=2, tiled=True
        ).astype(jnp.float32),
        lax.psum_scatter(
            part_dense_w.astype(jnp.bfloat16), ("fsdp", "context"), scatter_dimension=1, tiled=True
        ).astype(jnp.float32),
        lax.psum_scatter(
            cot_total.astype(jnp.bfloat16), ("fsdp", "context"), scatter_dimension=0, tiled=True
        ).astype(jnp.float32),
        lax.psum_scatter(
            part_fc1_w.astype(jnp.bfloat16), ("fsdp", "context"), scatter_dimension=0, tiled=True
        ).astype(jnp.float32),
        lax.psum_scatter(
            part_fc1_b.astype(jnp.bfloat16), ("fsdp", "context"), scatter_dimension=1, tiled=True
        ).astype(jnp.float32),
        lax.psum_scatter(
            part_fc2_w.astype(jnp.bfloat16), ("fsdp", "context"), scatter_dimension=1, tiled=True
        ).astype(jnp.float32),
        lax.psum_scatter(
            cot_total.astype(jnp.bfloat16), ("fsdp", "context"), scatter_dimension=0, tiled=True
        ).astype(jnp.float32),
    )
    reduced = (
        lax.all_gather(shares[0].astype(jnp.bfloat16), "context", axis=0, tiled=True).astype(
            jnp.float32
        ),
        lax.all_gather(shares[1].astype(jnp.bfloat16), "context", axis=0, tiled=True).astype(
            jnp.float32
        ),
        lax.all_gather(shares[2].astype(jnp.bfloat16), "context", axis=0, tiled=True).astype(
            jnp.float32
        ),
        lax.all_gather(shares[3].astype(jnp.bfloat16), "context", axis=2, tiled=True).astype(
            jnp.float32
        ),
        lax.all_gather(shares[4].astype(jnp.bfloat16), "context", axis=1, tiled=True).astype(
            jnp.float32
        ),
        lax.all_gather(shares[5].astype(jnp.bfloat16), "context", axis=0, tiled=True).astype(
            jnp.float32
        ),
        lax.all_gather(shares[6].astype(jnp.bfloat16), "context", axis=0, tiled=True).astype(
            jnp.float32
        ),
        lax.all_gather(shares[7].astype(jnp.bfloat16), "context", axis=1, tiled=True).astype(
            jnp.float32
        ),
        lax.all_gather(shares[8].astype(jnp.bfloat16), "context", axis=1, tiled=True).astype(
            jnp.float32
        ),
        lax.all_gather(shares[9].astype(jnp.bfloat16), "context", axis=0, tiled=True).astype(
            jnp.float32
        ),
    )
    return (
        layer_out,
        grad_tokens,
        reduced[0],
        reduced[1],
        reduced[2],
        reduced[3],
        reduced[4],
        reduced[5],
        reduced[6],
        reduced[7],
        reduced[8],
        reduced[9],
    )


def solution(mesh):
    in_specs = (
        P(None, ("fsdp", "context"), "tensor"),
        P(None, ("fsdp", "context"), "tensor"),
        P(),
        P(),
        P("fsdp"),
        P("fsdp"),
        P("fsdp", None, "tensor"),
        P(None, "tensor", "fsdp"),
        P("tensor", "fsdp"),
        P("fsdp"),
        P("fsdp", "tensor"),
        P("tensor", "fsdp"),
        P("tensor", "fsdp"),
        P("fsdp"),
    )
    out_specs = (
        P(None, ("fsdp", "context"), "tensor"),
        P(None, ("fsdp", "context"), "tensor"),
        P("fsdp"),
        P("fsdp"),
        P("fsdp", None, "tensor"),
        P(None, "tensor", "fsdp"),
        P("tensor", "fsdp"),
        P("fsdp"),
        P("fsdp", "tensor"),
        P("tensor", "fsdp"),
        P("tensor", "fsdp"),
        P("fsdp"),
    )
    return jax.shard_map(body, mesh=mesh, in_specs=in_specs, out_specs=out_specs, check_vma=False)
```

profile of v0, /device:TPU:0, one launch (start us, length us, event | category | flops | bytes accessed | tf_op | source)
XLA Modules:
  0.0 2777.6 jit_solution(12622522128899695949)
XLA Ops:
  26.9 14.7 scatter_custom_fusion.2
  45.1 14.7 scatter_custom_fusion
  71.2 21.7 all_to_all.20
  116.2 118.3 %all-gather.18.cloned.1.call-done = bf16[2048,3,1024]{2,0,1:T(8,128)(2,1)} async-done(((bf16[1024,3,1024]{2,0,1:T(8,128)(2,1)}), bf16[2048,3,1024]{2,0,1:T(8,128)(2,1)}) %all-gather.18.cloned.1.call-update) | async-done | bytes 12582928 | tf_op jit(solution)/shard_map/all_gather | solution.py:237
  247.4 57.7 %all-gather.24.cloned.1.call-done = bf16[1024,2048]{1,0:T(8,128)(2,1)} async-done(((bf16[1024,1024]{1,0:T(8,128)(2,1)}), bf16[1024,2048]{1,0:T(8,128)(2,1)}) %all-gather.24.cloned.1.call-update) | async-done | bytes 4194320 | tf_op jit(solution)/shard_map/all_gather | solution.py:239
  311.9 101.3 %all-gather.22.cloned.1.call-done = bf16[2,1024,1024]{1,0,2:T(2,128)(2,1)} async-done(((bf16[2,128,1024]{1,0,2:T(2,128)(2,1)}), bf16[2,1024,1024]{1,0,2:T(2,128)(2,1)}) %all-gather.22.cloned.1.call-update) | async-done | bytes 4194320 | tf_op jit(solution)/shard_map/all_gather | solution.py:336
  426.5 64.2 %all-gather.20.cloned.1.call-done = bf16[2,1024,1024]{1,2,0:T(8,128)(2,1)} async-done(((bf16[2,128,1024]{1,2,0:T(8,128)(2,1)}), bf16[2,1024,1024]{1,2,0:T(8,128)(2,1)}) %all-gather.20.cloned.1.call-update) | async-done | bytes 4194320 | tf_op jit(solution)/shard_map/all_gather | solution.py:339
  619.9 68.1 %reduce-scatter.27.cloned.1.call-done = bf16[128,2048]{1,0:T(8,128)(2,1)} async-done(((bf16[1024,2048]{1,0:T(8,128)(2,1)}), bf16[128,2048]{1,0:T(8,128)(2,1)}) %reduce-scatter.27.cloned.1.call-update) | async-done | bytes 524304
  690.4 89.9 %reduce-scatter.25.cloned.1.call-done = bf16[128,2048]{1,0:T(8,128)(2,1)} async-done(((bf16[1024,2048]{1,0:T(8,128)(2,1)}), bf16[128,2048]{1,0:T(8,128)(2,1)}) %reduce-scatter.25.cloned.1.call-update) | async-done | bytes 524304
  806.6 174.0 %all-gather.28.cloned.1.call-done = bf16[4096,2048]{1,0:T(8,128)(2,1)} async-done(((bf16[4096,1024]{1,0:T(8,128)(2,1)}), bf16[4096,2048]{1,0:T(8,128)(2,1)}) %all-gather.28.cloned.1.call-update) | async-done | bytes 16777232 | tf_op jit(solution)/shard_map/all_gather | solution.py:243
  991.6 189.3 %all-gather.26.cloned.1.call-done = bf16[2048,4096]{1,0:T(8,128)(2,1)} async-done(((bf16[1024,4096]{1,0:T(8,128)(2,1)}), bf16[2048,4096]{1,0:T(8,128)(2,1)}) %all-gather.26.cloned.1.call-update) | async-done | bytes 16777232 | tf_op jit(solution)/shard_map/all_gather | solution.py:241
  1216.2 21.0 copy.364
  1281.9 261.1 %reduce-scatter.21.cloned.1.call-done = bf16[128,3,1024]{2,0,1:T(8,128)(2,1)} async-done(((bf16[2048,3,1024]{2,0,1:T(8,128)(2,1)}), bf16[128,3,1024]{2,0,1:T(8,128)(2,1)}) %reduce-scatter.21.cloned.1.call-update) | async-done | bytes 786448 | tf_op jit(solution)/shard_map/reduce_scatter | solution.py:467
  1543.1 349.2 %reduce-scatter.23.cloned.1.call-done = bf16[128,4096]{1,0:T(8,128)(2,1)} async-done(((bf16[2048,4096]{1,0:T(8,128)(2,1)}), bf16[128,4096]{1,0:T(8,128)(2,1)}) %reduce-scatter.23.cloned.1.call-update) | async-done | bytes 1048592 | tf_op jit(solution)/shard_map/reduce_scatter | solution.py:479
  1892.3 348.5 %reduce-scatter.33.cloned.1.call-done = bf16[128,4096]{1,0:T(8,128)(2,1)} async-done(((bf16[2048,4096]{1,0:T(8,128)(2,1)}), bf16[128,4096]{1,0:T(8,128)(2,1)}) %reduce-scatter.33.cloned.1.call-update) | async-done | bytes 1048592
  2291.6 63.0 %reduce-scatter.31.cloned.1.call-done = bf16[16,16]{1,0:T(8,128)(2,1)} async-done(((bf16[256,16]{1,0:T(8,128)(2,1)}), bf16[16,16]{1,0:T(8,128)(2,1)}) %reduce-scatter.31.cloned.1.call-update) | async-done | bytes 528
  2354.6 30.9 %all_gather.91 = bf16[16,128]{0,1:T(8,128)(2,1)S(1)} all-gather(bf16[16,16]{0,1:T(8,128)(2,1)} %bitcast.505), channel_id=1, replica_groups=mesh['fsdp'=2,'context'=8,'tensor'=2] {'context'}, dimensions={1}, use_global_device_ids=true | all-gather | bytes 4608 | tf_op jit(solution)/shard_map/all_gather | solution.py:514
  2391.5 75.2 %all-reduce.10 = (bf16[3,16,64]{1,0,2:T(4,128)(2,1)S(1)}, bf16[2048]{0:T(1024)(128)(2,1)S(1)}, bf16[2048]{0:T(1024)(128)(2,1)S(1)}, bf16[2048]{0:T(1024)(128)(2,1)S(1)}) all-reduce(bf16[3,16,64]{1,0,2:T(4,128)(2,1)S(1)} %copy.320, ...), channel_id=8, replica_groups=mesh['fsdp'=2,'context'=8,'tensor'=2] {'fsdp','context'}, use_global_device_ids=true, to_apply=%region_52.53.clone | all-reduce | flops 9216 | bytes 36864
  2466.8 16.9 all-gather
  2484.4 17.8 all-gather.1
  2502.7 30.7 %all_gather.87 = bf16[3,16,32]{1,0,2:T(4,128)(2,1)S(1)} all-gather(bf16[3,16,4]{1,0,2:T(4,128)(2,1)S(1)} %constant_dynamic-slice_fusion.14), channel_id=1, replica_groups=mesh['fsdp'=2,'context'=8,'tensor'=2] {'context'}, dimensions={2}, use_global_device_ids=true | all-gather | bytes 3456 | tf_op jit(solution)/shard_map/all_gather | solution.py:502
  2534.2 17.1 all-gather.2
  2568.5 63.4 %all-gather.36.cloned.1.call-done = bf16[1024,4096]{1,0:T(8,128)(2,1)} async-done(((bf16[128,4096]{1,0:T(8,128)(2,1)}), bf16[1024,4096]{1,0:T(8,128)(2,1)}) %all-gather.36.cloned.1.call-update) | async-done | bytes 8388624 | tf_op jit(solution)/shard_map/all_gather | solution.py:511
  2644.1 114.2 %all-gather.38.cloned.1.call-done = bf16[4096,1024]{1,0:T(8,128)(2,1)} async-done(((bf16[4096,128]{1,0:T(8,128)(2,1)}), bf16[4096,1024]{1,0:T(8,128)(2,1)}) %all-gather.38.cloned.1.call-update) | async-done | bytes 8388624 | tf_op jit(solution)/shard_map/all_gather | solution.py:517
  (500 shorter events, 481.7 us)
Async XLA Ops:
  17.9 46.6 %all-to-all-start = ((bf16[2,128,1024]{2,0,1:T(2,128)(2,1)}), bf16[2,128,1024]{2,0,1:T(2,128)(2,1)S(1)}, u32[]{:S(2)}, u32[]{:S(2)}) async-start(bf16[2,128,1024]{2,0,1:T(2,128)(2,1)} %copy.280), calls=%async_computation | async-start | bytes 1048576 | tf_op jit(solution)/shard_map/all_to_all | solution.py:309
  26.2 86.9 %all-gather.16.cloned.1.call-start = ((), (), s32[]{:S(2)}) async-start(), calls=%async_computation.12 | async-start | bytes 1572864 | tf_op jit(solution)/shard_map/all_gather | solution.py:321
  68.0 166.5 %all-gather.18.cloned.1.call-start = ((), (), s32[]{:S(2)}) async-start(), calls=%async_computation.13 | async-start | bytes 18874368 | tf_op jit(solution)/shard_map/all_gather | solution.py:237
  68.7 178.7 %all-gather.30.cloned.1.call-start = ((), (), s32[]{:S(2)}) async-start(), calls=%async_computation.20 | async-start | bytes 1572864 | tf_op jit(solution)/shard_map/all_gather | solution.py:322
  96.4 208.6 %all-gather.24.cloned.1.call-start = ((), (), s32[]{:S(2)}) async-start(), calls=%async_computation.16 | async-start | bytes 6291456 | tf_op jit(solution)/shard_map/all_gather | solution.py:239
  97.0 316.2 %all-gather.22.cloned.1.call-start = ((), (), s32[]{:S(2)}) async-start(), calls=%async_computation.15 | async-start | bytes 4718592 | tf_op jit(solution)/shard_map/all_gather | solution.py:336
  246.3 244.4 %all-gather.20.cloned.1.call-start = ((), (), s32[]{:S(2)}) async-start(), calls=%async_computation.14 | async-start | bytes 4718592 | tf_op jit(solution)/shard_map/all_gather | solution.py:339
  311.2 376.8 %reduce-scatter.27.cloned.1.call-start = ((), (), s32[]{:S(2)}) async-start(), calls=%async_computation.29 | async-start | bytes 4718592
  582.2 198.1 %reduce-scatter.25.cloned.1.call-start = ((), (), s32[]{:S(2)}) async-start(), calls=%async_computation.28 | async-start | bytes 4718592
  605.3 375.3 %all-gather.28.cloned.1.call-start = ((), (), s32[]{:S(2)}) async-start(), calls=%async_computation.18 | async-start | bytes 25165824 | tf_op jit(solution)/shard_map/all_gather | solution.py:243
  606.1 574.8 %all-gather.26.cloned.1.call-start = ((), (), s32[]{:S(2)}) async-start(), calls=%async_computation.17 | async-start | bytes 25165824 | tf_op jit(solution)/shard_map/all_gather | solution.py:241
  606.7 673.4 %reduce-scatter.29.cloned.1.call-start = ((), (), s32[]{:S(2)}) async-start(), calls=%async_computation.30 | async-start | bytes 4456448
  618.0 925.0 %reduce-scatter.21.cloned.1.call-start = ((), (), s32[]{:S(2)}) async-start(), calls=%async_computation.22 | async-start | bytes 13369344 | tf_op jit(solution)/shard_map/reduce_scatter | solution.py:467
  801.4 1090.8 %reduce-scatter.23.cloned.1.call-start = ((), (), s32[]{:S(2)}) async-start(), calls=%async_computation.25 | async-start | bytes 17825792 | tf_op jit(solution)/shard_map/reduce_scatter | solution.py:479
  1204.5 1036.3 %reduce-scatter.33.cloned.1.call-start = ((), (), s32[]{:S(2)}) async-start(), calls=%async_computation.32 | async-start | bytes 17825792
  1237.3 1017.3 %reduce-scatter.19.cloned.1.call-start = ((), (), s32[]{:S(2)}) async-start(), calls=%async_computation.19 | async-start | bytes 1572864 | tf_op jit(solution)/shard_map/reduce_scatter | solution.py:370
  1250.1 1025.0 %all-reduce.13.cloned.1.call-start = ((), (), s32[]{:S(2)}) async-start(), calls=%async_computation.21 | async-start | bytes 2097152 | tf_op jit(solution)/shard_map/psum | solution.py:431
  1277.0 1077.6 %reduce-scatter.31.cloned.1.call-start = ((), (), s32[]{:S(2)}) async-start(), calls=%async_computation.31 | async-start | bytes 69632
  1277.8 1277.1 %all-gather.34.cloned.1.call-start = ((), (), s32[]{:S(2)}) async-start(), calls=%async_computation.24 | async-start | bytes 2359296 | tf_op jit(solution)/shard_map/all_gather | solution.py:505
  1281.9 1277.2 %all-gather.32.cloned.1.call-start = ((), (), s32[]{:S(2)}) async-start(), calls=%async_computation.23 | async-start | bytes 7077888 | tf_op jit(solution)/shard_map/all_gather | solution.py:499
  1543.0 1088.8 %all-gather.36.cloned.1.call-start = ((), (), s32[]{:S(2)}) async-start(), calls=%async_computation.26 | async-start | bytes 9437184 | tf_op jit(solution)/shard_map/all_gather | solution.py:511
  1892.3 866.0 %all-gather.38.cloned.1.call-start = ((), (), s32[]{:S(2)}) async-start(), calls=%async_computation.27 | async-start | bytes 9437184 | tf_op jit(solution)/shard_map/all_gather | solution.py:517
  2259.0 23.7 all-to-all-start.1
  2282.7 268.7 %all-to-all-start.3 = ((bf16[2,128,1024]{2,0,1:T(2,128)(2,1)}), bf16[2,128,1024]{2,0,1:T(2,128)(2,1)S(1)}, u32[]{:S(2)}, u32[]{:S(2)}) async-start(bf16[2,128,1024]{2,0,1:T(2,128)(2,1)} %copy.316), calls=%async_computation.4 | async-start | bytes 1048576 | tf_op jit(solution)/shard_map/all_to_all | solution.py:454
  (68 other events, 7064.9 us)
Sparse Core Ops, SparseCore 0:
  68.1 10.3 all-gather.15
  80.0 154.4 all-gather.17
  236.6 9.0 all-gather.29
  247.1 57.9 all-gather.23
  307.5 105.7 all-gather.21
  415.7 74.9 all-gather.19
  582.3 105.6 reduce-scatter.26
  692.6 87.6 reduce-scatter.24
  781.9 198.7 all-gather.27
  982.0 198.8 all-gather.25
  1183.2 96.7 reduce-scatter.28
  1282.8 260.1 reduce-scatter.20
  1545.9 346.3 reduce-scatter.22
  1894.4 346.3 reduce-scatter.32
  2243.5 8.5 reduce-scatter.18
  2254.4 20.7 all-reduce.12
  2277.2 77.2 reduce-scatter.30
  2356.7 48.3 all-gather.33
  2407.5 98.7 all-gather.31
  2508.5 123.2 all-gather.35
  2634.7 123.5 all-gather.37
where the time goes:
time: 2790 us; the launch traced here: 2780 us
  waiting for transfers between devices  2080 us (75%)
  blocking collectives  238 us (9%)
  local copies, waits for them, and re-layouts  174 us (6%)
  matrix products  128 us (5%)
  other arithmetic  119 us (4%)
    unnamed x26, waiting for transfers between devices  574 us
    reduce_scatter x1, waiting for transfers between devices, body(): lax.psum_scatter(part_fc1_w.astype(jnp.bfloat16), ('fsdp', 'context'), sc...  349 us
    reduce_scatter x1, waiting for transfers between devices, body(): lax.psum_scatter(part_qkv_w.astype(jnp.bfloat16), ('fsdp', 'context'), sc...  261 us
    all_gather x1, waiting for transfers between devices, body(): lax.all_gather(fc1_weight, 'fsdp', axis=0, tiled=True)  189 us
    all_gather x1, waiting for transfers between devices, body(): lax.all_gather(fc2_weight, 'fsdp', axis=1, tiled=True)  174 us
    all_gather x1, waiting for transfers between devices, body(): lax.all_gather(qkv_weight, 'fsdp', axis=0, tiled=True)  118 us
    all_gather x1, waiting for transfers between devices, body(): lax.all_gather(shares[8].astype(jnp.bfloat16), 'context', axis=1, tiled=T...  114 us
    all_gather x1, waiting for transfers between devices, body(): lax.all_gather(key_b.reshape(micro_count, row_count, local_width), 'conte...  101 us
  transfers between devices with their start and end apart: 24, of which 16 were waited for; matrix products, arithmetic and copies ran while one was open for 11% of the time, Pallas kernels for 0%

commit v1 on v0

--- a/solution.py
+++ b/solution.py
@@ -3,9 +3,13 @@
 import jax
 import jax.numpy as jnp
 from jax import lax
+from jax.experimental import pallas as pl
+from jax.experimental.pallas import tpu as pltpu
+from jax.sharding import Mesh
 from jax.sharding import PartitionSpec as P
 
 ROT = 32
+FS, CT, TE = "fsdp", "context", "tensor"
 
 
 EPSILON = 1e-05
@@ -33,7 +37,9 @@
 
 
 def segment_layout(length_row, places):
-    ends = jnp.cumsum(length_row)
+    count = length_row.shape[0]
+    upto = jnp.arange(count)[:, None] >= jnp.arange(count)[None, :]
+    ends = jnp.sum(jnp.where(upto, length_row[None, :], 0), axis=1)
     starts = ends - length_row
     segment = jnp.sum((places[:, None] >= ends[None, :]).astype(jnp.int32), axis=1)
     match = segment[:, None] == jnp.arange(length_row.shape[0], dtype=jnp.int32)[None, :]
@@ -232,16 +238,16 @@
     fc2_bias,
 ):
     gain_all, shift_all, w_qkv, b_qkv, w_dense, b_dense, w_fc1, b_fc1, w_fc2, b_fc2 = (
-        lax.all_gather(ln_gain, "fsdp", axis=0, tiled=True),
-        lax.all_gather(ln_bias, "fsdp", axis=0, tiled=True),
-        lax.all_gather(qkv_weight, "fsdp", axis=0, tiled=True),
-        lax.all_gather(qkv_bias, "fsdp", axis=2, tiled=True),
-        lax.all_gather(dense_weight, "fsdp", axis=1, tiled=True),
-        lax.all_gather(dense_bias, "fsdp", axis=0, tiled=True),
-        lax.all_gather(fc1_weight, "fsdp", axis=0, tiled=True),
-        lax.all_gather(fc1_bias, "fsdp", axis=1, tiled=True),
-        lax.all_gather(fc2_weight, "fsdp", axis=1, tiled=True),
-        lax.all_gather(fc2_bias, "fsdp", axis=0, tiled=True),
+        lax.all_gather(ln_gain, FS, axis=0, tiled=True),
+        lax.all_gather(ln_bias, FS, axis=0, tiled=True),
+        lax.all_gather(qkv_weight, FS, axis=0, tiled=True),
+        lax.all_gather(qkv_bias, FS, axis=2, tiled=True),
+        lax.all_gather(dense_weight, FS, axis=1, tiled=True),
+        lax.all_gather(dense_bias, FS, axis=0, tiled=True),
+        lax.all_gather(fc1_weight, FS, axis=0, tiled=True),
+        lax.all_gather(fc1_bias, FS, axis=1, tiled=True),
+        lax.all_gather(fc2_weight, FS, axis=1, tiled=True),
+        lax.all_gather(fc2_bias, FS, axis=0, tiled=True),
     )
     gain_f = gain_all.astype(jnp.float32)
     shift_f = shift_all.astype(jnp.float32)
@@ -255,12 +261,12 @@
     row_count = tokens.shape[1]
     feature_share = tokens.shape[2]
     all_rows = micro_count * row_count
-    pack_length = row_count * lax.axis_size("context")
+    pack_length = row_count * lax.axis_size(CT)
     block_rows = min(512, pack_length)
-    group_index = lax.axis_index(("fsdp", "context"))
-    pack_index = lax.axis_index("fsdp")
-    context_index = lax.axis_index("context")
-    tensor_index = lax.axis_index("tensor")
+    group_index = lax.axis_index((FS, CT))
+    pack_index = lax.axis_index(FS)
+    context_index = lax.axis_index(CT)
+    tensor_index = lax.axis_index(TE)
     out_shift = lax.dynamic_slice_in_dim(
         b_dense.astype(jnp.float32) + b_fc2.astype(jnp.float32),
         tensor_index * feature_share,
@@ -287,7 +293,8 @@
         own_targets = lax.dynamic_slice_in_dim(perm_row, group_index * row_count, row_count, 0)
         send_order = jnp.argsort(own_targets // row_count, stable=True)
         return_orders.append(jnp.zeros(row_count, jnp.int32).at[send_order].set(counting))
-        arriving = jnp.nonzero(perm_row // row_count == group_index, size=row_count)[0]
+        here = perm_row // row_count == group_index
+        arriving = jnp.argsort(jnp.where(here, 0, 1), stable=True)[:row_count]
         arrive_slot = perm_row[arriving] % row_count
         arrive_slots.append(arrive_slot)
         slot_sources.append(jnp.zeros(row_count, jnp.int32).at[arrive_slot].set(counting))
@@ -307,10 +314,10 @@
         first_blocks.append((query_place[0] - query_position[0]) // block_rows)
     received = (
         lax.all_to_all(
-            jnp.stack(sent_tokens), ("fsdp", "context"), split_axis=1, concat_axis=1, tiled=True
+            jnp.stack(sent_tokens), (FS, CT), split_axis=1, concat_axis=1, tiled=True
         ),
         lax.all_to_all(
-            jnp.stack(sent_cot), ("fsdp", "context"), split_axis=1, concat_axis=1, tiled=True
+            jnp.stack(sent_cot), (FS, CT), split_axis=1, concat_axis=1, tiled=True
         ),
     )
     own_tokens = jnp.concatenate(
@@ -318,8 +325,8 @@
     )
     own_cot = jnp.concatenate([received[1][m][slot_sources[m]] for m in range(micro_count)], axis=0)
     full_tokens, full_cot = (
-        lax.all_gather(own_tokens, "tensor", axis=1, tiled=True),
-        lax.all_gather(own_cot, "tensor", axis=1, tiled=True),
+        lax.all_gather(own_tokens, TE, axis=1, tiled=True),
+        lax.all_gather(own_cot, TE, axis=1, tiled=True),
     )
     normed, norm_back = jax.vjp(layer_norm, full_tokens.astype(jnp.float32), gain_f, shift_f)
     normed_b = normed.astype(jnp.bfloat16)
@@ -334,10 +341,10 @@
     value_b = qkv[:, 2].astype(jnp.bfloat16)
     keys_all, values_all = (
         lax.all_gather(
-            key_b.reshape(micro_count, row_count, local_width), "context", axis=1, tiled=True
+            key_b.reshape(micro_count, row_count, local_width), CT, axis=1, tiled=True
         ),
         lax.all_gather(
-            value_b.reshape(micro_count, row_count, local_width), "context", axis=1, tiled=True
+            value_b.reshape(micro_count, row_count, local_width), CT, axis=1, tiled=True
         ),
     )
     attended_list = []
@@ -368,7 +375,7 @@
         activ_b, w_fc2, preferred_element_type=jnp.float32
     )
     branch = lax.psum_scatter(
-        partial_out.astype(jnp.bfloat16), "tensor", scatter_dimension=1, tiled=True
+        partial_out.astype(jnp.bfloat16), TE, scatter_dimension=1, tiled=True
     ).astype(jnp.float32)
     layer_rows = (own_tokens.astype(jnp.float32) + branch + out_shift).astype(jnp.bfloat16)
     grad_attended = jnp.einsum(
@@ -411,10 +418,10 @@
         value_parts.append(grad_values_one)
     grad_keys, grad_values = (
         lax.psum_scatter(
-            jnp.stack(key_parts).astype(jnp.bfloat16), "context", scatter_dimension=1, tiled=True
+            jnp.stack(key_parts).astype(jnp.bfloat16), CT, scatter_dimension=1, tiled=True
         ).astype(jnp.float32),
         lax.psum_scatter(
-            jnp.stack(value_parts).astype(jnp.bfloat16), "context", scatter_dimension=1, tiled=True
+            jnp.stack(value_parts).astype(jnp.bfloat16), CT, scatter_dimension=1, tiled=True
         ).astype(jnp.float32),
     )
     grad_keys = grad_keys.reshape(all_rows, local_width)
@@ -428,7 +435,7 @@
     grad_normed_part = jnp.einsum(
         "rce,dce->rd", grad_qkv, w_qkv, preferred_element_type=jnp.float32
     ) + jnp.einsum("rh,dh->rd", grad_pre, w_fc1, preferred_element_type=jnp.float32)
-    grad_normed = lax.psum(grad_normed_part.astype(jnp.bfloat16), "tensor").astype(jnp.float32)
+    grad_normed = lax.psum(grad_normed_part.astype(jnp.bfloat16), TE).astype(jnp.float32)
     grad_input, grad_gain, grad_shift = norm_back(grad_normed)
     cot_f = full_cot.astype(jnp.float32)
     grad_own = lax.dynamic_slice_in_dim(
@@ -449,75 +456,75 @@
         back_grads.append(grad_own[rows][arrive_slots[micro_index]])
     returned = (
         lax.all_to_all(
-            jnp.stack(back_rows), ("fsdp", "context"), split_axis=1, concat_axis=1, tiled=True
+            jnp.stack(back_rows), (FS, CT), split_axis=1, concat_axis=1, tiled=True
         ),
         lax.all_to_all(
-            jnp.stack(back_grads), ("fsdp", "context"), split_axis=1, concat_axis=1, tiled=True
+            jnp.stack(back_grads), (FS, CT), split_axis=1, concat_axis=1, tiled=True
         ),
     )
     layer_out = jnp.stack([returned[0][m][return_orders[m]] for m in range(micro_count)])
     grad_tokens = jnp.stack([returned[1][m][return_orders[m]] for m in range(micro_count)])
     shares = (
         lax.psum_scatter(
-            grad_gain.astype(jnp.bfloat16), ("fsdp", "context"), scatter_dimension=0, tiled=True
+            grad_gain.astype(jnp.bfloat16), (FS, CT), scatter_dimension=0, tiled=True
         ).astype(jnp.float32),
         lax.psum_scatter(
-            grad_shift.astype(jnp.bfloat16), ("fsdp", "context"), scatter_dimension=0, tiled=True
+            grad_shift.astype(jnp.bfloat16), (FS, CT), scatter_dimension=0, tiled=True
         ).astype(jnp.float32),
         lax.psum_scatter(
-            part_qkv_w.astype(jnp.bfloat16), ("fsdp", "context"), scatter_dimension=0, tiled=True
+            part_qkv_w.astype(jnp.bfloat16), (FS, CT), scatter_dimension=0, tiled=True
         ).astype(jnp.float32),
         lax.psum_scatter(
-            part_qkv_b.astype(jnp.bfloat16), ("fsdp", "context"), scatter_dimension=2, tiled=True
+            part_qkv_b.astype(jnp.bfloat16), (FS, CT), scatter_dimension=2, tiled=True
         ).astype(jnp.float32),
         lax.psum_scatter(
-            part_dense_w.astype(jnp.bfloat16), ("fsdp", "context"), scatter_dimension=1, tiled=True
+            part_dense_w.astype(jnp.bfloat16), (FS, CT), scatter_dimension=1, tiled=True
         ).astype(jnp.float32),
         lax.psum_scatter(
-            cot_total.astype(jnp.bfloat16), ("fsdp", "context"), scatter_dimension=0, tiled=True
+            cot_total.astype(jnp.bfloat16), (FS, CT), scatter_dimension=0, tiled=True
         ).astype(jnp.float32),
         lax.psum_scatter(
-            part_fc1_w.astype(jnp.bfloat16), ("fsdp", "context"), scatter_dimension=0, tiled=True
+            part_fc1_w.astype(jnp.bfloat16), (FS, CT), scatter_dimension=0, tiled=True
         ).astype(jnp.float32),
         lax.psum_scatter(
-            part_fc1_b.astype(jnp.bfloat16), ("fsdp", "context"), scatter_dimension=1, tiled=True
+            part_fc1_b.astype(jnp.bfloat16), (FS, CT), scatter_dimension=1, tiled=True
         ).astype(jnp.float32),
         lax.psum_scatter(
-            part_fc2_w.astype(jnp.bfloat16), ("fsdp", "context"), scatter_dimension=1, tiled=True
+            part_fc2_w.astype(jnp.bfloat16), (FS, CT), scatter_dimension=1, tiled=True
         ).astype(jnp.float32),
         lax.psum_scatter(
-            cot_total.astype(jnp.bfloat16), ("fsdp", "context"), scatter_dimension=0, tiled=True
+            cot_total.astype(jnp.bfloat16), (FS, CT), scatter_dimension=0, tiled=True
         ).astype(jnp.float32),
     )
     reduced = (
-        lax.all_gather(shares[0].astype(jnp.bfloat16), "context", axis=0, tiled=True).astype(
+        lax.all_gather(shares[0].astype(jnp.bfloat16), CT, axis=0, tiled=True).astype(
             jnp.float32
         ),
-        lax.all_gather(shares[1].astype(jnp.bfloat16), "context", axis=0, tiled=True).astype(
+        lax.all_gather(shares[1].astype(jnp.bfloat16), CT, axis=0, tiled=True).astype(
             jnp.float32
         ),
-        lax.all_gather(shares[2].astype(jnp.bfloat16), "context", axis=0, tiled=True).astype(
+        lax.all_gather(shares[2].astype(jnp.bfloat16), CT, axis=0, tiled=True).astype(
             jnp.float32
         ),
-        lax.all_gather(shares[3].astype(jnp.bfloat16), "context", axis=2, tiled=True).astype(
+        lax.all_gather(shares[3].astype(jnp.bfloat16), CT, axis=2, tiled=True).astype(
             jnp.float32
         ),
-        lax.all_gather(shares[4].astype(jnp.bfloat16), "context", axis=1, tiled=True).astype(
+        lax.all_gather(shares[4].astype(jnp.bfloat16), CT, axis=1, tiled=True).astype(
             jnp.float32
         ),
-        lax.all_gather(shares[5].astype(jnp.bfloat16), "context", axis=0, tiled=True).astype(
+        lax.all_gather(shares[5].astype(jnp.bfloat16), CT, axis=0, tiled=True).astype(
             jnp.float32
         ),
-        lax.all_gather(shares[6].astype(jnp.bfloat16), "context", axis=0, tiled=True).astype(
+        lax.all_gather(shares[6].astype(jnp.bfloat16), CT, axis=0, tiled=True).astype(
             jnp.float32
         ),
-        lax.all_gather(shares[7].astype(jnp.bfloat16), "context", axis=1, tiled=True).astype(
+        lax.all_gather(shares[7].astype(jnp.bfloat16), CT, axis=1, tiled=True).astype(
             jnp.float32
         ),
-        lax.all_gather(shares[8].astype(jnp.bfloat16), "context", axis=1, tiled=True).astype(
+        lax.all_gather(shares[8].astype(jnp.bfloat16), CT, axis=1, tiled=True).astype(
             jnp.float32
         ),
-        lax.all_gather(shares[9].astype(jnp.bfloat16), "context", axis=0, tiled=True).astype(
+        lax.all_gather(shares[9].astype(jnp.bfloat16), CT, axis=0, tiled=True).astype(
             jnp.float32
         ),
     )
@@ -537,35 +544,714 @@
     )
 
 
+MESH = pl.DeviceIdType.MESH
+AXES = ("y", "h", "l", "x", "t")
+BLOCK = 256
+SPAN = 512
+
+
+def fits(mesh):
+    return (mesh.shape[FS], mesh.shape[CT], mesh.shape[TE]) == (2, 8, 2)
+
+
+def place():
+    return tuple(lax.axis_index(a) for a in AXES)
+
+
+def greet(peers):
+    barrier = pltpu.get_barrier_semaphore()
+    total = 0
+    for device, there in peers:
+        if there is True:
+            pl.semaphore_signal(barrier, inc=1, device_id=device, device_id_type=MESH)
+            total += 1
+        else:
+
+            @pl.when(there)
+            def _(device=device):
+                pl.semaphore_signal(barrier, inc=1, device_id=device, device_id_type=MESH)
+
+            total = total + there.astype(jnp.int32)
+    pl.semaphore_wait(barrier, total)
+
+
+def spread_kernel(
+    tok, cot, w_q, w_d, w_1, w_2, small, tok_all, cot_all, q_out, d_out, o_1, o_2, small_out,
+    local_sem, send_sem, recv_sem,
+):
+    y, h, l, x, t = place()
+    z = 2 * h + l
+    rows, half = tok.shape[1], tok.shape[2]
+    other_y, other_x, other_t = {"y": 1 - y}, {"x": 1 - x}, {"t": 1 - t}
+
+    def along(zz):
+        return {"h": zz // 2, "l": lax.rem(zz, 2)}
+
+    greet(
+        [(other_y, True), (other_x, True), (other_t, True)]
+        + [(along(lax.max(z - 1, 0)), z > 0), (along(lax.min(z + 1, 3)), z < 3)]
+    )
+    units = [(tok, tok_all, 0, 1), (tok, tok_all, 1, 1), (cot, cot_all, 0, 2)]
+    numbers = {}
+
+    def number(key):
+        return numbers.setdefault(key, len(numbers))
+
+    def region(unit, chunk, core):
+        _, out, m, n = units[unit]
+        dy, dx, way, k = chunk
+        yy = 1 - y if dy else y
+        xx = 1 - x if dx else x
+        zz = z - k if way == "up" else z + k
+        group = yy * 8 + zz * 2 + xx
+        return out.at[
+            pl.ds(m, n),
+            pl.ds(pl.multiple_of(group * rows, rows), rows),
+            pl.ds(pl.multiple_of(core * half, half), half),
+        ]
+
+    def own(unit):
+        array, _, m, n = units[unit]
+        return array.at[pl.ds(m, n)]
+
+    started = []
+
+    def send(unit, chunk, key, device):
+        source = own(unit) if chunk == (0, 0, "up", 0) else region(unit, chunk, t)
+        i = number((unit,) + key)
+        copy = pltpu.make_async_remote_copy(
+            src_ref=source, dst_ref=region(unit, chunk, t), send_sem=send_sem.at[i],
+            recv_sem=recv_sem.at[i], device_id=device, device_id_type=MESH,
+        )
+        copy.start()
+        return copy
+
+    def arrive(unit, chunk, key, core):
+        i = number((unit,) + key)
+        ref = region(unit, chunk, core)
+        pltpu.make_async_remote_copy(
+            src_ref=ref, dst_ref=ref, send_sem=send_sem.at[i], recv_sem=recv_sem.at[i],
+            device_id=other_t, device_id_type=MESH,
+        ).wait_recv()
+
+    def sent(unit, chunk, key):
+        i = number((unit,) + key)
+        ref = own(unit)
+        pltpu.make_async_remote_copy(
+            src_ref=ref, dst_ref=ref, send_sem=send_sem.at[i], recv_sem=recv_sem.at[i],
+            device_id=other_t, device_id_type=MESH,
+        ).wait_send()
+
+    def when(there, what):
+        if there is True:
+            what()
+        else:
+            pl.when(there)(what)
+
+    def there_of(way, k):
+        return True if k == 0 else (z >= k if way == "up" else z + k <= 3)
+
+    def to_core(unit, chunk):
+        key = chunk + ("core",)
+        send(unit, chunk, key, other_t)
+        started.append((unit, chunk, key, None))
+
+    def onward(unit, chunk, axis):
+        dy, dx, way, k = chunk
+        key = ((1, dx, way, k) if axis == "y" else (dy, 1, way, k)) + ("link",)
+        send(unit, chunk, key, other_y if axis == "y" else other_x)
+        started.append((unit, chunk, key, None))
+
+    def up_down(unit, chunk):
+        dy, dx, way, k = chunk
+        for going in ("up", "down") if k == 0 else (way,):
+            can = z < 3 if going == "up" else z > 0
+            key = (dy, dx, going, k + 1, "link")
+            target = along(lax.min(z + 1, 3) if going == "up" else lax.max(z - 1, 0))
+            when(can, lambda: send(unit, chunk, key, target) and None)
+            started.append((unit, chunk, key, going))
+
+    def got(unit, chunk):
+        arrive(unit, chunk, chunk + ("link",), t)
+
+    steps = [[("up", 0)], [("up", 1), ("down", 1)], [("up", 2), ("down", 2)], [("up", 3), ("down", 3)]]
+    block = (y * 4 + l * 2 + x, (1 - y) * 4 + l * 2 + x)
+    pieces = []
+    depth = w_1.shape[0]
+    for b, to in ((block[1], True), (block[0], False)):
+        row = pl.ds(pl.multiple_of(y * depth, depth), depth)
+        wide, narrow = w_1.shape[1] // 8, w_d.shape[0] // 8
+        pieces.append([
+            (w_1.at[:, pl.ds(pl.multiple_of(b * wide, wide), wide)], o_1.at[row]),
+            (w_2.at[pl.ds(pl.multiple_of(b * wide, wide), wide)], o_2.at[:, row]),
+            (w_q.at[:, :, pl.ds(pl.multiple_of(b * narrow, narrow), narrow)], q_out.at[:, row]),
+            (w_d.at[pl.ds(pl.multiple_of(b * narrow, narrow), narrow)], d_out.at[:, row]),
+            (small, small_out.at[y]),
+        ])
+    locals_, weights = [], []
+    first = (0, 0, "up", 0)
+    for u in range(3):
+        up_down(u, first) if u else None
+    for u in range(3):
+        onward(u, first, "y")
+    for i, (source, target) in enumerate(pieces[0]):
+        copy = pltpu.make_async_remote_copy(
+            src_ref=source, dst_ref=target, send_sem=send_sem.at[number(("w", i))],
+            recv_sem=recv_sem.at[number(("w", i))], device_id=other_y, device_id_type=MESH,
+        )
+        copy.start()
+        weights.append(copy)
+    for u in range(3):
+        onward(u, first, "x")
+        to_core(u, first)
+        copy = pltpu.make_async_copy(own(u), region(u, first, t), local_sem.at[len(locals_)])
+        copy.start()
+        locals_.append(copy)
+    for source, target in pieces[1]:
+        copy = pltpu.make_async_copy(source, target, local_sem.at[len(locals_)])
+        copy.start()
+        locals_.append(copy)
+
+    got(0, (1, 0, "up", 0))
+    onward(0, (1, 0, "up", 0), "x")
+    up_down(0, first)
+    up_down(0, (1, 0, "up", 0))
+    to_core(0, (1, 0, "up", 0))
+
+    def rest_of_first():
+        for dy in (0, 1):
+            got(0, (dy, 1, "up", 0))
+            up_down(0, (dy, 1, "up", 0))
+            to_core(0, (dy, 1, "up", 0))
+
+    def z_step(s):
+        for u in (1, 2):
+            for way, k in steps[s]:
+                def act(u=u, c=(0, 0, way, k)):
+                    got(u, c)
+                    up_down(u, c) if c[3] < 3 else None
+                    onward(u, c, "y")
+                    onward(u, c, "x")
+                    to_core(u, c)
+                when(there_of(way, k), act)
+
+    def y_step(s):
+        for u in (1, 2):
+            for way, k in steps[s]:
+                def act(u=u, c=(1, 0, way, k)):
+                    got(u, c)
+                    onward(u, c, "x")
+                    to_core(u, c)
+                when(there_of(way, k), act)
+
+    def x_step(s):
+        for u in (1, 2):
+            for way, k in steps[s]:
+                def act(u=u, way=way, k=k):
+                    for dy in (0, 1):
+                        got(u, (dy, 1, way, k))
+                        to_core(u, (dy, 1, way, k))
+                when(there_of(way, k), act)
+
+    def first_step(s):
+        for way, k in steps[s]:
+            def act(way=way, k=k):
+                for dy in (0, 1):
+                    for dx in (0, 1):
+                        c = (dy, dx, way, k)
+                        got(0, c)
+                        up_down(0, c) if k < 3 else None
+                        to_core(0, c)
+            when(there_of(way, k), act)
+
+    z_step(1)
+    rest_of_first()
+    y_step(0)
+    z_step(2)
+    y_step(1)
+    x_step(0)
+    first_step(1)
+    z_step(3)
+    y_step(2)
+    x_step(1)
+    first_step(2)
+    y_step(3)
+    x_step(2)
+    first_step(3)
+    x_step(3)
+    for u in range(3):
+        for dy in (0, 1):
+            for dx in (0, 1):
+                for s in range(4):
+                    for way, k in steps[s]:
+                        c = (dy, dx, way, k)
+                        when(there_of(way, k), lambda: arrive(u, c, c + ("core",), 1 - t))
+    for copy in locals_:
+        copy.wait()
+    for copy in weights:
+        copy.wait()
+    for unit, chunk, key, going in started:
+        there = there_of(*chunk[2:])
+        if going is not None:
+            can = z < 3 if going == "up" else z > 0
+            there = can if there is True else can & there
+        when(there, lambda: sent(unit, chunk, key))
+
+
+def spread(tokens, cotangent, w_q, w_d, w_1, w_2, small):
+    micro, rows, half = tokens.shape
+    everything = jax.ShapeDtypeStruct((micro, rows * 16, half * 2), tokens.dtype)
+    depth = w_1.shape[0] * 2
+    outs = [
+        everything,
+        everything,
+        jax.ShapeDtypeStruct((3, depth, w_q.shape[2] // 8), w_q.dtype),
+        jax.ShapeDtypeStruct((w_d.shape[0] // 8, depth), w_d.dtype),
+        jax.ShapeDtypeStruct((depth, w_1.shape[1] // 8), w_1.dtype),
+        jax.ShapeDtypeStruct((w_2.shape[0] // 8, depth), w_2.dtype),
+        jax.ShapeDtypeStruct((2,) + small.shape, small.dtype),
+    ]
+    return pl.pallas_call(
+        spread_kernel,
+        out_shape=outs,
+        in_specs=[pl.BlockSpec(memory_space=pl.ANY)] * 7,
+        out_specs=[pl.BlockSpec(memory_space=pl.ANY)] * 7,
+        scratch_shapes=[
+            pltpu.SemaphoreType.DMA((8,)),
+            pltpu.SemaphoreType.DMA((176,)),
+            pltpu.SemaphoreType.DMA((176,)),
+        ],
+        compiler_params=pltpu.CompilerParams(collective_id=0, has_side_effects=True),
+        name="spread",
+    )(tokens, cotangent, w_q, w_d, w_1, w_2, small)
+
+
+def join_kernel(count, parts, outs, local_sem, send_sem, recv_sem):
+    y, h, l, x, t = place()
+    device = {"y": {"y": 1 - y}, "l": {"l": 1 - l}, "x": {"x": 1 - x}}
+    greet([(device[a], True) for a in ("y", "l", "x")])
+
+    def half_of(i, yy):
+        ref, d_axis, _, _ = parts[i]
+        n = ref.shape[d_axis] // 2
+        where = [slice(None)] * len(ref.shape)
+        where[d_axis] = pl.ds(pl.multiple_of(yy * n, n), n)
+        return ref.at[tuple(where)]
+
+    def spot(i, yy, ll, xx):
+        ref, _, b_axis, _ = parts[i]
+        n = ref.shape[b_axis]
+        where = [slice(None)] * len(ref.shape)
+        where[b_axis] = pl.ds(pl.multiple_of((yy * 4 + ll * 2 + xx) * n, n), n)
+        return outs[i].at[tuple(where)]
+
+    numbers = {}
+
+    def number(key):
+        return numbers.setdefault(key, len(numbers))
+
+    sends = []
+
+    def send(i, source, target, key, axis):
+        n = number((i,) + key)
+        copy = pltpu.make_async_remote_copy(
+            src_ref=source, dst_ref=target, send_sem=send_sem.at[n], recv_sem=recv_sem.at[n],
+            device_id=device[axis], device_id_type=MESH,
+        )
+        copy.start()
+        sends.append(copy)
+
+    def got(i, target, key):
+        n = number((i,) + key)
+        pltpu.make_async_remote_copy(
+            src_ref=target, dst_ref=target, send_sem=send_sem.at[n], recv_sem=recv_sem.at[n],
+            device_id=device["y"], device_id_type=MESH,
+        ).wait_recv()
+
+    every = range(count)
+    hop = {"x": "l", "l": "x"}
+    first = {i: parts[i][3] for i in every}
+    for i in every:
+        send(i, half_of(i, 1 - y), spot(i, y, l, x), ("y",), "y")
+    for i in every:
+        send(i, half_of(i, y), spot(i, y, l, x), (0, first[i]), first[i])
+    for i in every:
+        send(i, half_of(i, y), spot(i, y, l, x), (0, hop[first[i]]), hop[first[i]])
+    locals_ = []
+    for i in every:
+        copy = pltpu.make_async_copy(half_of(i, y), spot(i, y, l, x), local_sem.at[i])
+        copy.start()
+        locals_.append(copy)
+
+    def beside(i, axis, yy):
+        return spot(i, yy, 1 - l if axis == "l" else l, 1 - x if axis == "x" else x)
+
+    for i in every:
+        a = first[i]
+        got(i, beside(i, a, y), (0, a))
+        send(i, beside(i, a, y), beside(i, a, y), (0, "far"), hop[a])
+    for i in every:
+        got(i, spot(i, 1 - y, l, x), ("y",))
+        send(i, spot(i, 1 - y, l, x), spot(i, 1 - y, l, x), (1, first[i]), first[i])
+        send(i, spot(i, 1 - y, l, x), spot(i, 1 - y, l, x), (1, hop[first[i]]), hop[first[i]])
+    for i in every:
+        a = first[i]
+        got(i, beside(i, a, 1 - y), (1, a))
+        send(i, beside(i, a, 1 - y), beside(i, a, 1 - y), (1, "far"), hop[a])
+    for i in every:
+        for yy, side in ((y, 0), (1 - y, 1)):
+            got(i, beside(i, hop[first[i]], yy), (side, hop[first[i]]))
+            got(i, spot(i, yy, 1 - l, 1 - x), (side, "far"))
+    for copy in locals_:
+        copy.wait()
+    for copy in sends:
+        copy.wait_send()
+
+
+def join(arrays, plan, shapes, collective_id, name):
+    count = len(arrays)
+
+    def kernel(*refs):
+        parts = [(refs[i],) + plan[i] for i in range(count)]
+        join_kernel(count, parts, refs[count : 2 * count], *refs[2 * count :])
+
+    return pl.pallas_call(
+        kernel,
+        out_shape=[jax.ShapeDtypeStruct(s, a.dtype) for s, a in zip(shapes, arrays)],
+        in_specs=[pl.BlockSpec(memory_space=pl.ANY)] * count,
+        out_specs=[pl.BlockSpec(memory_space=pl.ANY)] * count,
+        scratch_shapes=[
+            pltpu.SemaphoreType.DMA((count,)),
+            pltpu.SemaphoreType.DMA((7 * count,)),
+            pltpu.SemaphoreType.DMA((7 * count,)),
+        ],
+        compiler_params=pltpu.CompilerParams(collective_id=collective_id, has_side_effects=True),
+        name=name,
+    )(*arrays)
+
+
+def swap_rotary(values):
+    lane = lax.rem(lax.broadcasted_iota(jnp.int32, values.shape, 1), 64)
+    half = ROT // 2
+    width = values.shape[1]
+    return jnp.where(
+        lane < half, pltpu.roll(values, width - half, 1), pltpu.roll(values, half, 1)
+    )
+
+
+def attend_kernel(rows_ref, seg_q, seg_k, cos_ref, sin_ref, out_ref, grad_ref, gq, gk, gv):
+    pack_rows, width = rows_ref.shape[1], out_ref.shape[2]
+    scale = 64 ** (-0.5)
+    lane = lax.broadcasted_iota(jnp.int32, (1, width), 1)
+    gk[...] = jnp.zeros_like(gk)
+    gv[...] = jnp.zeros_like(gv)
+    nt = (((1,), (1,)), ((), ()))
+    tn = (((0,), (0,)), ((), ()))
+
+    def dot(a, b, dims=(((1,), (0,)), ((), ()))):
+        return lax.dot_general(a, b, dims, preferred_element_type=jnp.float32)
+
+    for block in range(pack_rows // BLOCK):
+        low = max(0, block * BLOCK - SPAN)
+        high = (block + 1) * BLOCK
+        here = slice(block * BLOCK, high)
+        keys = rows_ref[0, low:high, width : 2 * width]
+        values = rows_ref[0, low:high, 2 * width : 3 * width]
+        seg_here = seg_q[0, here, :]
+        seg_there = seg_k[0, :, low:high]
+        row = lax.broadcasted_iota(jnp.int32, (BLOCK, high - low), 0) + block * BLOCK
+        column = lax.broadcasted_iota(jnp.int32, (BLOCK, high - low), 1) + low
+        allowed = (seg_here == seg_there) & (column <= row)
+        attended = None
+        for head in range(2):
+            mine = (lane // 64) == head
+            query = jnp.where(mine, rows_ref[0, here, 0:width], 0)
+            grad = jnp.where(mine, rows_ref[0, here, 3 * width : 4 * width], 0)
+            key = jnp.where(mine, keys, 0)
+            value = jnp.where(mine, values, 0)
+            scores = jnp.where(allowed, dot(query, key, nt) * scale, NEG_FILL)
+            peak = jnp.max(scores, axis=1, keepdims=True)
+            weights = jnp.exp(scores - peak)
+            weights = weights * (1.0 / jnp.sum(weights, axis=1, keepdims=True))
+            weights_b = weights.astype(jnp.bfloat16)
+            out = dot(weights_b, value)
+            attended = out if attended is None else attended + out
+            delta = jnp.sum(grad.astype(jnp.float32) * out, axis=1, keepdims=True)
+            inner = dot(grad, value, nt)
+            grad_scores = (weights * (inner - delta)).astype(jnp.bfloat16)
+            part = dot(grad_scores, key) * scale
+            if head == 0:
+                gq[here, :] = part
+            else:
+                gq[here, :] += part
+            gk[low:high, :] += dot(grad_scores, query, tn)
+            gv[low:high, :] += dot(weights_b, grad, tn)
+        out_ref[0, here, :] = attended.astype(jnp.bfloat16)
+    cos = cos_ref[0]
+    sin = sin_ref[0]
+    q_all = gq[...]
+    grad_ref[0, :, 0:width] = (q_all * cos - swap_rotary(q_all) * sin).astype(jnp.bfloat16)
+    k_all = gk[...] * scale
+    grad_ref[0, :, width : 2 * width] = (k_all * cos - swap_rotary(k_all) * sin).astype(jnp.bfloat16)
+    grad_ref[0, :, 2 * width : 3 * width] = gv[...].astype(jnp.bfloat16)
+
+
+def attend(rows, segment, cos, sin):
+    packs, pack_rows, wide = rows.shape
+    width = wide // 4
+    return pl.pallas_call(
+        attend_kernel,
+        grid=(packs,),
+        out_shape=[
+            jax.ShapeDtypeStruct((packs, pack_rows, width), jnp.bfloat16),
+            jax.ShapeDtypeStruct((packs, pack_rows, 3 * width), jnp.bfloat16),
+        ],
+        in_specs=[
+            pl.BlockSpec((1, pack_rows, wide), lambda i: (i, 0, 0)),
+            pl.BlockSpec((1, pack_rows, 1), lambda i: (i, 0, 0)),
+            pl.BlockSpec((1, 1, pack_rows), lambda i: (i, 0, 0)),
+            pl.BlockSpec((1, pack_rows, width), lambda i: (i, 0, 0)),
+            pl.BlockSpec((1, pack_rows, width), lambda i: (i, 0, 0)),
+        ],
+        out_specs=[
+            pl.BlockSpec((1, pack_rows, width), lambda i: (i, 0, 0)),
+            pl.BlockSpec((1, pack_rows, 3 * width), lambda i: (i, 0, 0)),
+        ],
+        scratch_shapes=[pltpu.VMEM((pack_rows, width), jnp.float32)] * 3,
+        compiler_params=pltpu.CompilerParams(vmem_limit_bytes=48 << 20),
+        cost_estimate=pl.CostEstimate(
+            flops=packs * 14 * pack_rows * pack_rows * width, bytes_accessed=packs * pack_rows * width * 24, transcendentals=0
+        ),
+        name="attend",
+    )(rows, segment[:, :, None], segment[:, None, :], cos, sin)
+
+
+def fast_body(
+    tokens, cotangent, lengths, permutation, ln_gain, ln_bias, qkv_weight, qkv_bias,
+    dense_weight, dense_bias, fc1_weight, fc1_bias, fc2_weight, fc2_bias,
+):
+    y, h, l, x, t = place()
+    f32, bf16 = jnp.float32, jnp.bfloat16
+    micro, rows, share = tokens.shape
+    width = share * 2
+    total = rows * 16
+    pack_rows = rows * 8
+    packs = total // pack_rows
+    block = y * 4 + l * 2 + x
+    wide = fc1_weight.shape[1] // 8
+    narrow = dense_weight.shape[0] // 8
+    small = jnp.concatenate(
+        [a.reshape(-1) for a in (ln_gain, ln_bias, dense_bias, fc2_bias, qkv_bias, fc1_bias)]
+    )
+    small = jnp.pad(small, (0, 64 * 128 - small.shape[0])).reshape(64, 128)
+    tok_all, cot_all, w_q, w_d, w_1, w_2, small = spread(
+        tokens, cotangent, qkv_weight.transpose(1, 0, 2), dense_weight, fc1_weight, fc2_weight, small
+    )
+    small = small.reshape(2, 64 * 128).astype(f32)
+    gain = small[:, 0:share].reshape(width)
+    shift = small[:, share : 2 * share].reshape(width)
+    out_shift = (small[:, 2 * share : 3 * share] + small[:, 3 * share : 4 * share]).reshape(width)
+    at = 4 * share
+    q_shift = small[:, at : at + qkv_bias.size].reshape((2,) + qkv_bias.shape)
+    q_shift = q_shift.transpose(1, 2, 0, 3).reshape(3, -1)
+    at += qkv_bias.size
+    f_shift = small[:, at : at + fc1_bias.size].reshape((2,) + fc1_bias.shape).transpose(1, 0, 2).reshape(-1)
+    q_shift = lax.dynamic_slice_in_dim(q_shift, block * narrow, narrow, 1)
+    f_shift = lax.dynamic_slice_in_dim(f_shift, block * wide, wide, 0)
+
+    places = jnp.arange(pack_rows, dtype=jnp.int32)
+    segment, position = jax.vmap(lambda row: segment_layout(row, places))(
+        lengths.reshape(micro * packs, -1)
+    )
+    position = position.reshape(micro, total).astype(f32)
+    chosen = (permutation[:, None, :] == jnp.arange(total, dtype=jnp.int32)[None, :, None]).astype(bf16)
+    half = ROT // 2
+    freq = ROPE_BASE ** (-2.0 * jnp.arange(half, dtype=f32) / ROT)
+
+    def tables(pos):
+        angles = pos[..., None] * freq
+        cos, sin = jnp.cos(angles), jnp.sin(angles)
+        rest = jnp.ones(pos.shape + (64 - ROT,), f32)
+        cos = jnp.concatenate([cos, cos, rest], -1)
+        sin = jnp.concatenate([-sin, sin, 0 * rest], -1)
+        return jnp.concatenate([cos, cos], -1), jnp.concatenate([sin, sin], -1)
+
+    cos_l, sin_l = tables(position)
+    pos_a = jnp.einsum("mla,ml->ma", chosen, position, precision=lax.Precision.HIGHEST)
+    cos_a, sin_a = tables(pos_a)
+
+    xs = tok_all.astype(f32)
+    center = xs - jnp.mean(xs, axis=-1, keepdims=True)
+    r = lax.rsqrt(jnp.mean(center * center, axis=-1, keepdims=True) + EPSILON)
+    normed = (center * r * gain + shift).astype(bf16)
+    pre = jnp.einsum("mrd,dh->mrh", normed, w_1, preferred_element_type=f32) + f_shift
+    activ, gelu_back = jax.vjp(partial(jax.nn.gelu, approximate=True), pre)
+    activ = activ.astype(bf16)
+    grad_activ = jnp.einsum("mrd,hd->mrh", cot_all, w_2, preferred_element_type=f32)
+    grad_pre = gelu_back(grad_activ)[0].astype(bf16)
+    g_w1 = jnp.einsum("mrd,mrh->dh", normed, grad_pre, preferred_element_type=f32).astype(bf16)
+    g_w2 = jnp.einsum("mrh,mrd->hd", activ, cot_all, preferred_element_type=f32).astype(bf16)
+    qkv = [
+        jnp.einsum("mrd,de->mre", normed, w_q[c], preferred_element_type=f32) + q_shift[c]
+        for c in range(3)
+    ]
+
+    def rotated(v):
+        lane = lax.broadcasted_iota(jnp.int32, v.shape, 2) % 64
+        other = jnp.where(lane < half, jnp.roll(v, -half, 2), jnp.roll(v, half, 2))
+        return v * cos_a + other * sin_a
+
+    grad_att = jnp.einsum("mrd,ed->mre", cot_all, w_d, preferred_element_type=f32)
+    four = jnp.concatenate([rotated(qkv[0]), rotated(qkv[1]), qkv[2], grad_att], -1).astype(bf16)
+    laid = jnp.einsum("mla,mae->mle", chosen, four, preferred_element_type=f32).astype(bf16)
+    attended, grad_qkv = attend(
+        laid.reshape(micro * packs, pack_rows, -1),
+        segment,
+        cos_l.reshape(micro * packs, pack_rows, -1),
+        sin_l.reshape(micro * packs, pack_rows, -1),
+    )
+    back = jnp.concatenate([attended, grad_qkv], -1).reshape(micro, total, 4 * narrow)
+    back = jnp.einsum("mla,mle->mae", chosen, back, preferred_element_type=f32).astype(bf16)
+    attended, grad_qkv = back[..., :narrow], back[..., narrow:]
+    g_wd = jnp.einsum("mre,mrd->ed", attended, cot_all, preferred_element_type=f32).astype(bf16)
+    g_wq = jnp.stack(
+        [
+            jnp.einsum(
+                "mrd,mre->de", normed, grad_qkv[..., c * narrow : (c + 1) * narrow], preferred_element_type=f32
+            )
+            for c in range(3)
+        ]
+    ).astype(bf16)
+
+    def side(v):
+        v = v.reshape(micro, 2, 2, 4 * rows, v.shape[-1])
+        return lax.dynamic_index_in_dim(v, h, 2, keepdims=False).reshape(micro, 2, 4, rows, v.shape[-1])
+
+    out_part = jnp.einsum("mycre,ed->ycmrd", side(attended), w_d, preferred_element_type=f32) + jnp.einsum(
+        "mycre,ed->ycmrd", side(activ), w_2, preferred_element_type=f32
+    )
+    g_side = side(grad_qkv)
+    norm_part = jnp.einsum("mycre,de->ycmrd", side(grad_pre), w_1, preferred_element_type=f32) + sum(
+        jnp.einsum(
+            "mycre,de->ycmrd", g_side[..., c * narrow : (c + 1) * narrow], w_q[c], preferred_element_type=f32
+        )
+        for c in range(3)
+    )
+
+    def summed(v):
+        v = v.astype(bf16)
+        v = lax.psum_scatter(v, "t", scatter_dimension=4, tiled=True)
+        v = lax.psum_scatter(v, "y", scatter_dimension=0, tiled=True)
+        v = v.reshape((2, 2) + v.shape[2:])
+        v = lax.psum_scatter(v, "l", scatter_dimension=0, tiled=True)
+        v = lax.psum_scatter(v, "x", scatter_dimension=1, tiled=True)
+        return v.reshape(micro, rows, share).astype(f32)
+
+    out_sum, norm_sum = summed(out_part), summed(norm_part)
+    at = t * share
+
+    def mine(v):
+        return lax.dynamic_slice_in_dim(v, at, share, 0)
+
+    layer_out = (tokens.astype(f32) + out_sum + mine(out_shift)).astype(bf16)
+    group = y * 8 + h * 4 + l * 2 + x
+    x_rows = lax.dynamic_slice_in_dim(tok_all, group * rows, rows, 1).astype(f32)
+    x_mid = x_rows - jnp.mean(x_rows, axis=-1, keepdims=True)
+    r_own = lax.rsqrt(jnp.mean(x_mid * x_mid, axis=-1, keepdims=True) + EPSILON)
+    hat = lax.dynamic_slice_in_dim(x_mid * r_own, at, share, 2)
+    scaled = mine(gain) * norm_sum
+    sums = lax.psum(jnp.stack([scaled.sum(-1), (scaled * hat).sum(-1)]), "t") / width
+    grad_tokens = (
+        cotangent.astype(f32) + r_own * (scaled - sums[0][..., None] - hat * sums[1][..., None])
+    ).astype(bf16)
+
+    g_small = jnp.stack([(norm_sum * hat).sum((0, 1)), norm_sum.sum((0, 1))])
+    g_small = lax.psum(g_small, ("y", "h", "l", "x"))
+    g_small = lax.all_gather(g_small, "t", axis=1, tiled=True)
+    g_small = lax.dynamic_slice_in_dim(g_small, y * share, share, 1)
+    g_bias = jnp.concatenate([grad_qkv.astype(f32).sum((0, 1)), grad_pre.astype(f32).sum((0, 1))])
+    g_bias = lax.all_gather(g_bias, ("y", "l", "x"), axis=0)
+    g_qb = g_bias[:, : 3 * narrow].reshape(8, 3, narrow).transpose(1, 0, 2).reshape(3, -1, 64)
+    g_qb = lax.dynamic_slice_in_dim(g_qb, y * 32, 32, 2)
+    g_fb = g_bias[:, 3 * narrow :].reshape(16, -1)
+    g_fb = lax.dynamic_slice_in_dim(g_fb, y * fc1_bias.shape[1], fc1_bias.shape[1], 1)
+    cot_sum = lax.dynamic_slice_in_dim(
+        cot_all.reshape(micro * total, width), y * share, share, 1
+    ).astype(f32).sum(0)
+
+    j_1, j_2 = join(
+        [g_w1, g_w2], [(0, 1, "x"), (1, 0, "l")], [fc1_weight.shape, fc2_weight.shape], 1, "join_mlp"
+    )
+    j_q, j_d = join(
+        [g_wq, g_wd],
+        [(1, 2, "x"), (1, 0, "l")],
+        [(3,) + dense_weight.shape, dense_weight.shape],
+        2,
+        "join_att",
+    )
+    return (
+        layer_out,
+        grad_tokens,
+        g_small[0],
+        g_small[1],
+        j_q.astype(f32).transpose(1, 0, 2),
+        g_qb,
+        j_d.astype(f32),
+        cot_sum,
+        j_1.astype(f32),
+        g_fb,
+        j_2.astype(f32),
+        cot_sum,
+    )
+
+
+def fast_solution(mesh):
+    small_mesh = Mesh(mesh.devices.reshape(2, 2, 2, 2, 2), AXES)
+    rows = P(None, ("y", "h", "l", "x"), "t")
+    weights = (
+        P("y"), P("y"), P("y", None, "t"), P(None, "t", "y"), P("t", "y"), P("y"), P("y", "t"),
+        P("t", "y"), P("t", "y"), P("y"),
+    )
+    return jax.shard_map(
+        fast_body,
+        mesh=small_mesh,
+        in_specs=(rows, rows, P(), P()) + weights,
+        out_specs=(rows, rows) + weights,
+        check_vma=False,
+    )
+
+
 def solution(mesh):
+    if fits(mesh):
+        return fast_solution(mesh)
     in_specs = (
-        P(None, ("fsdp", "context"), "tensor"),
-        P(None, ("fsdp", "context"), "tensor"),
+        P(None, (FS, CT), TE),
+        P(None, (FS, CT), TE),
         P(),
         P(),
-        P("fsdp"),
-        P("fsdp"),
-        P("fsdp", None, "tensor"),
-        P(None, "tensor", "fsdp"),
-        P("tensor", "fsdp"),
-        P("fsdp"),
-        P("fsdp", "tensor"),
-        P("tensor", "fsdp"),
-        P("tensor", "fsdp"),
-        P("fsdp"),
+        P(FS),
+        P(FS),
+        P(FS, None, TE),
+        P(None, TE, FS),
+        P(TE, FS),
+        P(FS),
+        P(FS, TE),
+        P(TE, FS),
+        P(TE, FS),
+        P(FS),
     )
     out_specs = (
-        P(None, ("fsdp", "context"), "tensor"),
-        P(None, ("fsdp", "context"), "tensor"),
-        P("fsdp"),
-        P("fsdp"),
-        P("fsdp", None, "tensor"),
-        P(None, "tensor", "fsdp"),
-        P("tensor", "fsdp"),
-        P("fsdp"),
-        P("fsdp", "tensor"),
-        P("tensor", "fsdp"),
-        P("tensor", "fsdp"),
-        P("fsdp"),
+        P(None, (FS, CT), TE),
+        P(None, (FS, CT), TE),
+        P(FS),
+        P(FS),
+        P(FS, None, TE),
+        P(None, TE, FS),
+        P(TE, FS),
+        P(FS),
+        P(FS, TE),
+        P(TE, FS),
+        P(TE, FS),
+        P(FS),
     )
     return jax.shard_map(body, mesh=mesh, in_specs=in_specs, out_specs=out_specs, check_vma=False)

time: 2790 us -> 1170 us (0.42)
  waiting for transfers between devices: 2080 us -> 217 us
  Pallas kernels: 0 us -> 426 us
  blocking collectives: 238 us -> 72.3 us
  matrix products: 128 us -> 253 us
  local copies, waits for them, and re-layouts: 174 us -> 66.5 us
    all_gather x12 -> x0, waiting for transfers between devices: 882 us -> none  [the longest x1 189 us: body(): lax.all_gather(fc1_weight, 'fsdp', axis=0, tiled=True)]
    reduce_scatter x3 -> x6, waiting for transfers between devices: 610 us -> 15.9 us  [the longest x2 15.9 us: summed(): v = lax.psum_scatter(v, 't', scatter_dimension=4, tiled=True)]
    pallas_call x0 -> x4, Pallas kernels: none -> 426 us  [the longest x2 210 us: join(): pl.pallas_call(kernel, out_shape=[jax.ShapeDtypeStruct(s, a.dtype) for s,...]
    unnamed x26 -> x8, waiting for transfers between devices: 574 us -> 201 us
    dot_general x26 -> x21, matrix products: 128 us -> 253 us  [the longest x3 36.3 us: fast_body(): jnp.einsum('mycre,de->ycmrd', g_side[..., c * narrow:(c + 1) * narrow], w...]
    all_gather x11 -> x2, blocking collectives: 141 us -> 28.6 us  [the longest x1 26.8 us: fast_body(): g_bias = lax.all_gather(g_bias, ('y', 'l', 'x'), axis=0)]
    unnamed x1 -> x0, blocking collectives: 75.2 us -> none
    unnamed x144 -> x83, local copies, waits for them, and re-layouts: 79.5 us -> 23.4 us
  transfers between devices with their start and end apart: 24 -> 7, of which waited for: 16 -> 2; matrix products, arithmetic and copies ran while one was open for 11% -> 16% of each run, Pallas kernels for 0% -> 18%
where the time goes in v1:
time: 1170 us; the launch traced here: 1160 us
  Pallas kernels  426 us (36%)
  matrix products  253 us (22%)
  waiting for transfers between devices  217 us (19%)
  other arithmetic  113 us (10%)
  blocking collectives  72.3 us (6%)
  local copies, waits for them, and re-layouts  66.5 us (6%)
  between operations  15 us (1%)
    pallas_call x2, Pallas kernels, join(): pl.pallas_call(kernel, out_shape=[jax.ShapeDtypeStruct(s, a.dtype) for s,...  210 us
    unnamed x8, waiting for transfers between devices  201 us
    pallas_call x1, Pallas kernels, spread(): pl.pallas_call(spread_kernel, out_shape=outs, in_specs=[pl.BlockSpec(memo...  183 us
    psum x1, blocking collectives, fast_body(): g_small = lax.psum(g_small, ('y', 'h', 'l', 'x'))  41.2 us
    dot_general x3, matrix products, fast_body(): jnp.einsum('mycre,de->ycmrd', g_side[..., c * narrow:(c + 1) * narrow], w...  36.3 us
    dot_general x3, matrix products, fast_body(): jnp.einsum('mrd,de->mre', normed, w_q[c], preferred_element_type=f32)  35.4 us
    pallas_call x1, Pallas kernels, attend(): pl.pallas_call(attend_kernel, grid=(packs,), out_shape=[jax.ShapeDtypeStr...  33.5 us
    dot_general x3, matrix products, fast_body(): jnp.einsum('mrd,mre->de', normed, grad_qkv[..., c * narrow:(c + 1) * narr...  28.5 us
  transfers between devices with their start and end apart: 7, of which 2 were waited for; matrix products, arithmetic and copies ran while one was open for 16% of the time, Pallas kernels for 18%

profile of v1, /device:TPU:0, one launch (start us, length us, event | category | flops | bytes accessed | tf_op | source)
XLA Modules:
  0.0 1163.9 jit_solution(17241184353502175065)
XLA Ops:
  14.1 182.9 %spread.1 = (bf16[2,2048,2048]{2,1,0:T(8,128)(2,1)}, bf16[2,2048,2048]{2,1,0:T(8,128)(2,1)}, bf16[3,2048,128]{2,1,0:T(8,128)(2,1)}, bf16[128,2048]{1,0:T(8,128)(...) custom-call(bf16[2,128,1024]{2,1,0:T(8,128)(2,1)} %tok.1, ...), custom_call_target="tpu_custom_call" | custom-call | tf_op jit(solution)/shard_map/spread/pallas_call | solution.py:814
  214.9 16.4 %fusion.5 = bf16[2,2048,2048]{2,1,0:T(8,128)(2,1)} fusion(bf16[2,2048,2048]{2,1,0:T(8,128)(2,1)} %get-tuple-element.26, f32[2048]{0:T(1024)S(1)} %get-tuple-element.78, f32[2048]{0:T(1024)S(1)} %get-tuple-element.79, f32[2,2048]{1,0:T(2,128)S(1)} %add_rsqrt_fusion, f32[2,2048]{1,0:T(2,128)S(1)} %broadcast_multiply_fusion), kind=kLoop, calls=%fused_computation.7 | loop fusion | flops 50331648 | bytes 33603584 | tf_op jit(solution)/shard_map/convert_element_type | solution.py:1086
  231.4 11.5 convolution_add_fusion.2
  245.4 11.5 convolution_add_fusion.1
  259.6 15.2 %fusion.8 = f32[2,1,2048]{2,1,0:T(1,128)S(1)} fusion(s32[2,2048]{1,0:T(2,128)S(1)} %copy-done.26, f32[2,2048,1]{1,0,2:T(2,128)S(1)} %convert_bitcast_fusion.3), kind=kOutput, calls=%fused_computation.11 | convolution fusion | flops 109051904 | bytes 49152 | tf_op jit(solution)/shard_map/mla,ml->ma/dot_general | solution.py:1080
  293.1 12.5 %fusion.36 = bf16[2,2048,128]{1,2,0:T(8,128)(2,1)} fusion(bf16[2,2048,2048]{2,1,0:T(8,128)(2,1)} %fusion.5, f32[128]{0:T(128)S(1)} %get-tuple-element.72, bf16[3,2048,128]{2,1,0:T(8,128)(2,1)} %get-tuple-element.28), kind=kOutput, calls=%fused_computation.53 | convolution fusion | flops 2148532224 | bytes 18350592 | tf_op jit(solution)/shard_map/mrd,de->mre/dot_general | solution.py:1095
  309.2 10.4 concatenate.62.cos_ref
  319.7 12.4 %convolution_convert_fusion = bf16[2,2048,128]{1,2,0:T(8,128)(2,1)} fusion(bf16[2,2048,2048]{2,1,0:T(8,128)(2,1)} %get-tuple-element.29, bf16[128,2048]{1,0:T(8,128)(2,1)} %get-tuple-element.25), kind=kOutput, calls=%fused_computation.54 | convolution fusion | flops 2148007936 | bytes 18350080 | tf_op jit(solution)/shard_map/mrd,ed->mre/dot_general | solution.py:1104
  350.2 16.2 %fusion.30 = bf16[2,2048,512]{2,1,0:T(8,128)(2,1)} fusion(bf16[2,2048,128]{1,2,0:T(8,128)(2,1)S(1)} %copy-done.28, bf16[2,2048,128]{1,2,0:T(8,128)(2,1)S(1)} %copy-done.12, bf16[2,2048,128]{1,2,0:T(8,128)(2,1)S(1)} %get-tuple-element.46, bf16[2,2048,128]{1,2,0:T(8,128)(2,1)S(1)} %get-tuple-element.45, s32[2,2048]{1,0:T(2,128)S(1)} %copy-done.26), kind=kOutput, calls=%fused_computation.44 | convolution fusion | flops 8625586176 | bytes 8404992 | tf_op jit(solution)/shard_map/mla,mae->mle/dot_general | solution.py:1106
  366.4 33.5 %attend.1 = (bf16[4,1024,128]{2,1,0:T(8,128)(2,1)S(1)}, bf16[4,1024,384]{2,1,0:T(8,128)(2,1)}) custom-call(bf16[4,1024,512]{2,1,0:T(8,128)(2,1)} %bitcast.279, s32[4,1024,1]{2,1,0:T(8,128)S(1)} %copy-done, s32[4,1,1024]{2,1,0:T(1,128)S(1)} %broadcast_in_dim.64.seg_k, f32[4,1024,128]{2,1,0:T(8,128)S(1)} %concatenate.62.cos_ref, ...), custom_call_target="tpu_custom_call" | custom-call | flops 7516192768 | bytes 12582912 | tf_op jit(solution)/shard_map/attend/pallas_call | solution.py:1002
  414.4 16.6 %multiply_convert_fusion = (bf16[2,2048,512]{2,1,0:T(8,128)(2,1)S(1)}, f32[2,2048,512]{2,1,0:T(8,128)}) fusion(f32[512]{0:T(512)S(1)} %dynamic_slice.47, bf16[2,2048,2048]{2,1,0:T(8,128)(2,1)} %fusion.5, bf16[2048,512]{1,0:T(8,128)(2,1)S(1)} %copy-done.22), kind=kOutput, calls=%fused_computation.32 | convolution fusion | flops 8610906112 | bytes 31459328 | tf_op jit(solution)/shard_map/mrd,dh->mrh/dot_general | solution.py:1087
  442.2 11.4 fusion.21
  456.2 21.0 %convert_reduce_fusion.2 = (f32[512]{0:T(512)S(1)}, bf16[2,2048,512]{2,1,0:T(8,128)(2,1)S(1)}) fusion(f32[2,2048,512]{2,1,0:T(8,128)} %get-tuple-element.75, f32[512]{0:T(512)S(1)} %dynamic_slice.47, bf16[2,2048,2048]{2,1,0:T(8,128)(2,1)} %get-tuple-element.29, bf16[512,2048]{1,0:T(8,128)(2,1)S(1)} %copy-done.25), kind=kOutput, calls=%fused_computation.31 | convolution fusion | flops 8638169088 | bytes 31461376 | tf_op jit(solution)/shard_map/mrd,hd->mrh/dot_general | solution.py:1090
  504.2 20.2 %fusion.22 = bf16[2,4,2,128,2048]{3,4,1,0,2:T(8,128)(2,1)} fusion(f32[2048,2,2,4,128]{4,0,3,2,1:T(8,128)} %fusion.50, f32[2048,2,2,4,128]{4,0,3,2,1:T(8,128)} %fusion.77, f32[2048,2,2,4,128]{4,0,3,2,1:T(8,128)} %fusion.75, bf16[2,2,4,128,384]{4,3,2,1,0:T(8,128)(2,1)S(1)} %bitcast.243, bf16[3,2048,128]{2,1,0:T(8,128)(2,1)S(1)} %copy-done.7), kind=kOutput, calls=%fused_computation.30 | convolution fusion | flops 1090519040 | bytes 59768832 | tf_op jit(solution)/shard_map/mycre,de->ycmrd/dot_general | solution.py:1135
  524.5 15.9 %reduce-scatter.19.cloned.1.call-done = bf16[2,4,2,128,1024]{3,4,1,0,2:T(8,128)(2,1)} async-done(((bf16[2,4,2,128,2048]{3,4,1,0,2:T(8,128)(2,1)}), bf16[2,4,2,128,1024]{3,4,1,0,2:T(8,128)(2,1)}) %reduce-scatter.19.cloned.1.call-update) | async-done | bytes 4194320 | tf_op jit(solution)/shard_map/reduce_scatter | solution.py:1143
  541.6 201.1 %all-reduce.6.cloned.1.call-done = (bf16[2,4,2,128,1024]{3,4,1,0,2:T(8,128)(2,1)}, bf16[2,4,2,128,1024]{3,4,1,0,2:T(8,128)(2,1)}) async-done(((bf16[2,4,2,128,1024]{3,4,1,0,2:T(8,128)(2,1)}, bf16[2,4,2,128,1024]{3,4,1,0,2:T(8,128)(2,1)}), (bf16[2,4,2,128,1024]{3,4,1,0,2:T(8,128)(2,1)}, bf16[2,4,2,128,1024]{3,4,1,0,2:T(8,128)(2,1)})) %all-reduce.6.cloned.1.call-update) | async-done | bytes 8388624
  750.3 26.8 %all-gather.1 = f32[8,1,896]{2,1,0:T(1,128)S(1)} all-gather(f32[1,1,896]{2,1,0:T(1,128)S(1)} %reshape.240), channel_id=2, replica_groups=mesh['y'=2,'h'=2,'l'=2,'x'=2,'t'=2] {'y','l','x'}, dimensions={0}, use_global_device_ids=true | all-gather | bytes 32256 | tf_op jit(solution)/shard_map/all_gather | solution.py:1173
  804.7 11.5 fusion.43
  841.1 14.6 %bitcast_convert_fusion.1.refs_0_ = bf16[2048,512]{1,0:T(8,128)(2,1)} fusion(bf16[2,2048,2048]{2,1,0:T(8,128)(2,1)} %fusion.5, bf16[2,2048,512]{2,1,0:T(8,128)(2,1)} %copy-done.15), kind=kOutput, calls=%fused_computation.43 | convolution fusion | flops 8590983168 | bytes 23068672 | tf_op jit(solution)/shard_map/mrd,mrh->dh/dot_general | solution.py:1092
  856.4 77.7 %join_att.1 = (bf16[3,1024,1024]{2,1,0:T(8,128)(2,1)}, bf16[1024,1024]{1,0:T(8,128)(2,1)}) custom-call(bf16[3,2048,128]{2,1,0:T(8,128)(2,1)} %pad_maximum_fusion.1.refs_0_, bf16[128,2048]{1,0:T(8,128)(2,1)} %fusion.40.refs_1_), custom_call_target="tpu_custom_call" | custom-call | tf_op jit(solution)/shard_map/join_att/pallas_call | solution.py:918
  938.2 132.2 %join_mlp.1 = (bf16[1024,4096]{1,0:T(8,128)(2,1)}, bf16[4096,1024]{1,0:T(8,128)(2,1)}) custom-call(bf16[2048,512]{1,0:T(8,128)(2,1)} %bitcast_convert_fusion.1.refs_0_, bf16[512,2048]{1,0:T(8,128)(2,1)} %bitcast_convert_fusion.refs_1_), custom_call_target="tpu_custom_call" | custom-call | tf_op jit(solution)/shard_map/join_mlp/pallas_call | solution.py:918
  1070.5 11.8 %convert_element_type.139 = f32[1024,4096]{1,0:T(8,128)} convert(bf16[1024,4096]{1,0:T(8,128)(2,1)} %get-tuple-element.36) | non-fusion elementwise | flops 4194304 | bytes 25165824 | tf_op jit(solution)/shard_map/convert_element_type | solution.py:1201
  1082.3 11.7 %convert_element_type.140 = f32[4096,1024]{1,0:T(8,128)} convert(bf16[4096,1024]{1,0:T(8,128)(2,1)} %get-tuple-element.37) | non-fusion elementwise | flops 4194304 | bytes 25165824 | tf_op jit(solution)/shard_map/convert_element_type | solution.py:1203
  1108.3 41.2 %psum.15 = f32[2,1024]{1,0:T(2,128)S(1)} all-reduce(f32[2,1024]{1,0:T(2,128)S(1)} %pad_maximum_fusion.2), channel_id=1, replica_groups=mesh['y'=2,'h'=2,'l'=2,'x'=2,'t'=2] {'y','h','l','x'}, use_global_device_ids=true, to_apply=%region_20.21 | all-reduce | flops 2048 | bytes 16384 | tf_op jit(solution)/shard_map/psum | solution.py:1169
  (200 shorter events, 212.6 us)
Async XLA Ops:
  7.2 517.3 %reduce-scatter.13.cloned.1.call-start = ((), (), s32[]{:S(2)}) async-start(), calls=%async_computation.6 | async-start | bytes 12582912 | tf_op jit(solution)/shard_map/reduce_scatter | solution.py:1143
  198.5 10.7 copy-start.1
  214.9 16.5 %copy-start.18 = (f32[2048]{0:T(1024)}, f32[2048]{0:T(1024)S(1)}, u32[]{:S(2)}) copy-start(f32[2048]{0:T(1024)S(1)} %get-tuple-element.79) | copy-start | bytes 24580
  350.2 16.2 %copy-start = (s32[4,1024,1]{2,1,0:T(8,128)S(1)}, s32[4,1024,1]{2,1,0:T(8,128)}, u32[]{:S(2)}) copy-start(s32[4,1024,1]{2,1,0:T(8,128)} %copy.115.seg_q) | copy-start | bytes 49156
  402.3 12.1 %copy-start.22 = (bf16[2048,512]{1,0:T(8,128)(2,1)S(1)}, bf16[2048,512]{1,0:T(8,128)(2,1)}, u32[]{:S(2)}) copy-start(bf16[2048,512]{1,0:T(8,128)(2,1)} %get-tuple-element.33) | copy-start | bytes 6291460
  431.1 11.2 copy-start.13
  453.7 86.7 %reduce-scatter.19.cloned.1.call-start = ((), (), s32[]{:S(2)}) async-start(), calls=%async_computation.9 | async-start | bytes 12582912 | tf_op jit(solution)/shard_map/reduce_scatter | solution.py:1143
  477.2 10.7 copy-start.15
  524.4 218.3 %all-reduce.6.cloned.1.call-start = ((), (), s32[]{:S(2)}) async-start(), calls=%async_computation.12 | async-start | bytes 16777216
  540.4 300.5 %reduce-scatter.21.cloned.1.call-start = ((), (), s32[]{:S(2)}) async-start(), calls=%async_computation.10 | async-start | bytes 3145728 | tf_op jit(solution)/shard_map/reduce_scatter | solution.py:1146
  747.7 108.0 %reduce-scatter.15.cloned.1.call-start = ((), (), s32[]{:S(2)}) async-start(), calls=%async_computation.7 | async-start | bytes 3145728 | tf_op jit(solution)/shard_map/reduce_scatter | solution.py:1146
  781.9 374.4 %copy-start.21 = (f32[1024]{0:T(1024)}, f32[1024]{0:T(1024)S(1)}, u32[]{:S(2)}) copy-start(f32[1024]{0:T(1024)S(1)} %convert_reduce_fusion.1) | copy-start | bytes 12292
  802.4 300.8 %reduce-scatter.23.cloned.1.call-start = ((), (), s32[]{:S(2)}) async-start(), calls=%async_computation.11 | async-start | bytes 1572864 | tf_op jit(solution)/shard_map/reduce_scatter | solution.py:1147
  804.7 15.0 %copy-start.6 = (bf16[2,2048,512]{2,1,0:T(8,128)(2,1)S(1)}, bf16[2,2048,512]{2,1,0:T(8,128)(2,1)}, u32[]{:S(2)}) copy-start(bf16[2,2048,512]{2,1,0:T(8,128)(2,1)} %copy-done.4) | copy-start | bytes 12582916
  816.2 12.8 %slice-start = ((s8[16777216]{0:T(1024)(128)(4,1)}), s8[4194304]{0:T(1024)(128)(4,1)S(1)}, s32[]{:S(2)}) async-start(s8[16777216]{0:T(1024)(128)(4,1)} %bitcast.238), calls=%async_computation.13 | async-start | bytes 8388608
  819.8 9.3 slice-start.1
  819.8 9.3 slice-start.2
  819.8 9.6 slice-start.3
  819.8 11.0 copy-start.14
  840.9 15.5 %copy-start.20 = (f32[1,8,2,128]{3,2,1,0:T(2,128)S(1)}, f32[1,8,2,128]{3,2,1,0:T(2,128)}, u32[]{:S(2)}) copy-start(f32[1,8,2,128]{3,2,1,0:T(2,128)} %get-tuple-element.55) | copy-start | bytes 24580
  840.9 15.5 %copy-start.19 = (f32[2048]{0:T(1024)S(1)}, f32[2048]{0:T(1024)}, u32[]{:S(2)}) copy-start(f32[2048]{0:T(1024)} %copy-done.18) | copy-start | bytes 24580
  840.9 311.1 %reduce-scatter.17.cloned.1.call-start = ((), (), s32[]{:S(2)}) async-start(), calls=%async_computation.8 | async-start | bytes 1572864 | tf_op jit(solution)/shard_map/reduce_scatter | solution.py:1147
  1094.0 58.0 %copy-start.10 = (bf16[2,128,1024]{2,1,0:T(8,128)(2,1)S(1)}, bf16[2,128,1024]{2,1,0:T(8,128)(2,1)}, u32[]{:S(2)}) copy-start(bf16[2,128,1024]{2,1,0:T(8,128)(2,1)} %tok.1) | copy-start | bytes 1572868
  1094.0 60.1 %copy-start.11 = (bf16[2,128,1024]{2,1,0:T(8,128)(2,1)S(1)}, bf16[2,128,1024]{2,1,0:T(8,128)(2,1)}, u32[]{:S(2)}) copy-start(bf16[2,128,1024]{2,1,0:T(8,128)(2,1)} %cot.1) | copy-start | bytes 1572868
  (17 other events, 66.6 us)
Sparse Core Ops, SparseCore 0:
  453.8 16.1 reduce-scatter.12
  524.6 15.7 reduce-scatter.18
  542.9 199.7 all-reduce.5
  747.8 32.3 reduce-scatter.20
  802.6 32.2 reduce-scatter.14
  841.0 25.7 reduce-scatter.22
  869.1 32.5 reduce-scatter.16

commit v2 on v1

--- a/solution.py
+++ b/solution.py
@@ -833,6 +833,8 @@
 
     def half_of(i, yy):
         ref, d_axis, _, _ = parts[i]
+        if d_axis is None:
+            return ref
         n = ref.shape[d_axis] // 2
         where = [slice(None)] * len(ref.shape)
         where[d_axis] = pl.ds(pl.multiple_of(yy * n, n), n)
@@ -930,6 +932,325 @@
     )(*arrays)
 
 
+NN = (((1,), (0,)), ((), ()))
+NT = (((1,), (1,)), ((), ()))
+TN = (((0,), (0,)), ((), ()))
+
+
+def dot(a, b, dims=NN):
+    return lax.dot_general(a, b, dims, preferred_element_type=jnp.float32)
+
+
+def fold_kernel(
+    activ, grad_pre, back, tok_all, cot, w_1, w_2, w_q, w_d, gain, out_shift, layer_out, grad_out, ln_out,
+    act_v, pre_v, back_v, tok_v, give, core_in, give_n, sum_in, stat_v, stat_in, ln_v, ln_in,
+    load_sem, core_send, core_recv, hop_send, hop_recv, small_send, small_recv,
+):
+    y, h, l, x, t = place()
+    rows, share = cot.shape[1], cot.shape[2]
+    both = 2 * rows
+    device = {"y": {"y": 1 - y}, "l": {"l": 1 - l}, "x": {"x": 1 - x}, "t": {"t": 1 - t}, "h": {"h": 1 - h}}
+    narrow = w_d.shape[0]
+    loads = []
+
+    def load(source, target):
+        copy = pltpu.make_async_copy(source, target, load_sem.at[len(loads)])
+        copy.start()
+        loads.append(copy)
+
+    def group_rows(dy, dl, dx):
+        yy = 1 - y if dy else y
+        ll = 1 - l if dl else l
+        xx = 1 - x if dx else x
+        return pl.ds(pl.multiple_of((yy * 8 + h * 4 + ll * 2 + xx) * rows, rows), rows)
+
+    owners = [(1, 0, 1), (1, 1, 1), (0, 0, 1), (0, 1, 1), (1, 0, 0), (1, 1, 0), (0, 1, 0), (0, 0, 0)]
+    arrived = {}
+    for o, owner in enumerate(owners):
+        start = len(loads)
+        for m in range(2):
+            there = pl.ds(m * rows, rows)
+            load(activ.at[m, group_rows(*owner)], act_v.at[o, there])
+            load(back.at[m, group_rows(*owner)], back_v.at[o, there])
+            load(grad_pre.at[m, group_rows(*owner)], pre_v.at[o, there])
+        arrived[o] = loads[start:]
+    start = len(loads)
+    for m in range(2):
+        load(tok_all.at[m, group_rows(0, 0, 0)], tok_v.at[pl.ds(m * rows, rows)])
+    tok_loads = loads[start:]
+    greet([(device[a], True) for a in ("t", "x", "y", "l", "h")])
+
+    def part(a, o, tt):
+        columns = pl.ds(pl.multiple_of(tt * share, share), share)
+        if a == 0:
+            return dot(act_v[o], w_2[:, columns]) + dot(back_v[o, :, 0:narrow], w_d[:, columns])
+        total = dot(pre_v[o], w_1[columns, :], NT)
+        for c in range(3):
+            total += dot(back_v[o, :, (c + 1) * narrow : (c + 2) * narrow], w_q[c, columns, :], NT)
+        return total
+
+    core = {}
+
+    def offer(a, o):
+        if o in arrived:
+            for copy in arrived.pop(o):
+                copy.wait()
+        i = a * 8 + o
+        give[i] = part(a, o, 1 - t).astype(jnp.bfloat16)
+        core[i] = pltpu.make_async_remote_copy(
+            src_ref=give.at[i], dst_ref=core_in.at[i], send_sem=core_send.at[i], recv_sem=core_recv.at[i],
+            device_id=device["t"], device_id_type=MESH,
+        )
+        core[i].start()
+
+    hops = {0: ("x", "y", "l"), 1: ("y", "x", "l")}
+    place_of = {"y": 0, "l": 1, "x": 2}
+    slots, passed = {}, {}
+
+    def slot(a, stage, owner):
+        return slots.setdefault((a, stage, owner), len(slots))
+
+    def total_of(a, o, stage):
+        i = a * 8 + o
+        total = part(a, o, t)
+        core[i].wait_recv()
+        total += core_in[i].astype(jnp.float32)
+        for s in range(stage):
+            n = slot(a, s, owners[o])
+            passed[n].wait_recv()
+            total += sum_in[n].astype(jnp.float32)
+        return total
+
+    def stage_owners(a, stage):
+        done = [place_of[d] for d in hops[a][:stage]]
+        now = place_of[hops[a][stage]]
+        return [o for o, w in enumerate(owners) if all(w[d] == 0 for d in done) and w[now] == 1]
+
+    def pass_on(a, o, stage):
+        axis = hops[a][stage]
+        seen = list(owners[o])
+        seen[place_of[axis]] = 0
+        n = slot(a, stage, tuple(seen))
+        give_n[n] = total_of(a, o, stage).astype(jnp.bfloat16)
+        passed[n] = pltpu.make_async_remote_copy(
+            src_ref=give_n.at[n], dst_ref=sum_in.at[n], send_sem=hop_send.at[n], recv_sem=hop_recv.at[n],
+            device_id=device[axis], device_id_type=MESH,
+        )
+        passed[n].start()
+
+    order = []
+    for stage in range(3):
+        for pair in zip(stage_owners(0, stage), stage_owners(1, stage)):
+            order += [(a, o, stage) for a, o in enumerate(pair)]
+    ahead = 2
+    queue = [(a, o) for a, o, _ in order] + [(0, 7), (1, 7)]
+    for a, o in queue[:ahead]:
+        offer(a, o)
+    for i, (a, o, stage) in enumerate(order):
+        if stage == 0:
+            offer(*queue[i + ahead])
+            pass_on(a, o, stage)
+            if i == 7:
+                for item in queue[i + ahead + 1 :]:
+                    offer(*item)
+        else:
+            pass_on(a, o, stage)
+    for copy in tok_loads:
+        copy.wait()
+    mine = pl.ds(pl.multiple_of(t * share, share), share)
+    values = tok_v[...].astype(jnp.float32)
+    mean = jnp.mean(values, axis=1, keepdims=True)
+    spread_of = jnp.mean((values - mean) ** 2, axis=1, keepdims=True)
+    r = lax.rsqrt(spread_of + EPSILON)
+    token = tok_v[:, mine].astype(jnp.float32)
+    hat = (token - mean) * r
+    norm_sum = total_of(1, 7, 3)
+    scaled = norm_sum * gain[:, mine]
+    stat_v[:, 0:128] = jnp.broadcast_to(jnp.sum(scaled, axis=1, keepdims=True), (both, 128))
+    stat_v[:, 128:256] = jnp.broadcast_to(jnp.sum(scaled * hat, axis=1, keepdims=True), (both, 128))
+    stat = pltpu.make_async_remote_copy(
+        src_ref=stat_v, dst_ref=stat_in, send_sem=small_send.at[0], recv_sem=small_recv.at[0],
+        device_id=device["t"], device_id_type=MESH,
+    )
+    stat.start()
+    top = lax.broadcasted_iota(jnp.int32, (8, share), 0) == 0
+    ln_v[0] = jnp.where(
+        top, jnp.sum(norm_sum * hat, axis=0, keepdims=True), jnp.sum(norm_sum, axis=0, keepdims=True)
+    )
+    smalls = [stat]
+
+    def swap(step, axis):
+        copy = pltpu.make_async_remote_copy(
+            src_ref=ln_v.at[step], dst_ref=ln_in.at[step], send_sem=small_send.at[step + 1],
+            recv_sem=small_recv.at[step + 1], device_id=device[axis], device_id_type=MESH,
+        )
+        copy.start()
+        smalls.append(copy)
+        return copy
+
+    first = swap(0, "h")
+    out = token + total_of(0, 7, 3) + out_shift[:, mine]
+    for m in range(2):
+        layer_out[m] = out[m * rows : (m + 1) * rows].astype(jnp.bfloat16)
+    first.wait_recv()
+    ln_v[1] = ln_v[0] + ln_in[0]
+    second = swap(1, "l")
+    stat.wait_recv()
+    width = 2 * share
+    mean_t = (stat_v[:, 0:1] + stat_in[:, 0:1]) / width
+    mean_h = (stat_v[:, 128:129] + stat_in[:, 128:129]) / width
+    grad = r * (scaled - mean_t - hat * mean_h)
+    for m in range(2):
+        grad_out[m] = (cot[m].astype(jnp.float32) + grad[m * rows : (m + 1) * rows]).astype(jnp.bfloat16)
+    second.wait_recv()
+    ln_v[2] = ln_v[1] + ln_in[1]
+    swap(2, "x").wait_recv()
+    ln_v[3] = ln_v[2] + ln_in[2]
+    swap(3, "y").wait_recv()
+    ln_v[4] = ln_v[3] + ln_in[3]
+    swap(4, "t").wait_recv()
+    ln_out[...] = jnp.where(t == y, ln_v[4], ln_in[4])
+    for copy in core.values():
+        copy.wait_send()
+    for copy in passed.values():
+        copy.wait_send()
+    for copy in smalls:
+        copy.wait_send()
+
+
+def fold(activ, grad_pre, back, tok_all, cot, w_1, w_2, w_q, w_d, gain, out_shift):
+    micro, rows, share = cot.shape
+    both = micro * rows
+    narrow = w_d.shape[0]
+    held = lambda n, w: pltpu.VMEM((n, both, w), jnp.bfloat16)
+    sem = pltpu.SemaphoreType.DMA
+    any_, vmem = pl.BlockSpec(memory_space=pl.ANY), pl.BlockSpec(memory_space=pltpu.VMEM)
+    return pl.pallas_call(
+        fold_kernel,
+        out_shape=[
+            jax.ShapeDtypeStruct(cot.shape, cot.dtype),
+            jax.ShapeDtypeStruct(cot.shape, cot.dtype),
+            jax.ShapeDtypeStruct((8, share), jnp.float32),
+        ],
+        in_specs=[any_] * 4 + [vmem] * 7,
+        out_specs=[vmem] * 3,
+        scratch_shapes=[
+            held(8, w_1.shape[1]),
+            held(8, w_1.shape[1]),
+            held(8, 4 * narrow),
+            pltpu.VMEM((both, 2 * share), jnp.bfloat16),
+            held(16, share),
+            held(16, share),
+            held(14, share),
+            held(14, share),
+            pltpu.VMEM((both, 256), jnp.float32),
+            pltpu.VMEM((both, 256), jnp.float32),
+            pltpu.VMEM((5, 8, share), jnp.float32),
+            pltpu.VMEM((5, 8, share), jnp.float32),
+            sem((50,)),
+            sem((16,)),
+            sem((16,)),
+            sem((14,)),
+            sem((14,)),
+            sem((6,)),
+            sem((6,)),
+        ],
+        compiler_params=pltpu.CompilerParams(
+            collective_id=3, has_side_effects=True, vmem_limit_bytes=60 << 20
+        ),
+        name="fold",
+    )(activ, grad_pre, back, tok_all, cot, w_1, w_2, w_q, w_d, gain, out_shift)
+
+
+ROOT = 0.7978845608028654
+CUBE = 0.044715
+
+
+def rows_kernel(
+    tok, cot, w_1, w_2, w_q, w_d, gain, shift, f_shift, q_shift,
+    normed_out, activ_out, pre_out, four_out, g_1, g_2, cot_sum, pre_sum, acc_1, acc_2,
+):
+    step = pl.program_id(0)
+
+    @pl.when(step == 0)
+    def _():
+        acc_1[...] = jnp.zeros_like(acc_1)
+        acc_2[...] = jnp.zeros_like(acc_2)
+        cot_sum[...] = jnp.zeros_like(cot_sum)
+        pre_sum[...] = jnp.zeros_like(pre_sum)
+
+    f32, bf16 = jnp.float32, jnp.bfloat16
+    values = tok[0].astype(f32)
+    center = values - jnp.mean(values, axis=1, keepdims=True)
+    r = lax.rsqrt(jnp.mean(center * center, axis=1, keepdims=True) + EPSILON)
+    normed = (center * r * gain[...] + shift[...]).astype(bf16)
+    normed_out[0] = normed
+    cots = cot[0]
+    pre = dot(normed, w_1[...]) + f_shift[...]
+    square = pre * pre
+    curve = jnp.tanh(ROOT * (pre + CUBE * pre * square))
+    activ = (0.5 * pre * (1.0 + curve)).astype(bf16)
+    slope = 0.5 * (1.0 + curve) + 0.5 * pre * (1.0 - curve * curve) * (ROOT * (1.0 + 3.0 * CUBE * square))
+    grad_pre = (dot(cots, w_2[...], NT) * slope).astype(bf16)
+    activ_out[0] = activ
+    pre_out[0] = grad_pre
+    narrow = w_d.shape[0]
+    for c in range(3):
+        at = slice(c * narrow, (c + 1) * narrow)
+        four_out[0, :, at] = (dot(normed, w_q[c]) + q_shift[:, at]).astype(bf16)
+    four_out[0, :, 3 * narrow :] = dot(cots, w_d[...], NT).astype(bf16)
+    acc_1[...] += dot(normed, grad_pre, TN)
+    acc_2[...] += dot(activ, cots, TN)
+    cot_sum[...] += jnp.sum(cots.astype(f32), axis=0, keepdims=True)
+    pre_sum[...] += jnp.sum(grad_pre.astype(f32), axis=0, keepdims=True)
+
+    @pl.when(step == pl.num_programs(0) - 1)
+    def _():
+        g_1[...] = acc_1[...].astype(bf16)
+        g_2[...] = acc_2[...].astype(bf16)
+
+
+def row_work(tok_all, cot_all, w_1, w_2, w_q, w_d, gain, shift, f_shift, q_shift, size):
+    micro, total, width = tok_all.shape
+    per = total // size
+    wide = w_1.shape[1]
+    narrow = w_d.shape[0]
+    bf16, f32 = jnp.bfloat16, jnp.float32
+
+    def block(w):
+        return pl.BlockSpec((1, size, w), lambda i: (i // per, i % per, 0))
+
+    def whole(a):
+        return pl.BlockSpec(a.shape, lambda i: (0,) * len(a.shape), pipeline_mode=pl.Buffered(1))
+
+    def fixed(*s):
+        return pl.BlockSpec(s, lambda i: (0,) * len(s))
+
+    consts = (w_1, w_2, w_q, w_d, gain, shift, f_shift, q_shift)
+    return pl.pallas_call(
+        rows_kernel,
+        grid=(micro * per,),
+        out_shape=[
+            jax.ShapeDtypeStruct(tok_all.shape, bf16),
+            jax.ShapeDtypeStruct((micro, total, wide), bf16),
+            jax.ShapeDtypeStruct((micro, total, wide), bf16),
+            jax.ShapeDtypeStruct((micro, total, 4 * narrow), bf16),
+            jax.ShapeDtypeStruct(w_1.shape, bf16),
+            jax.ShapeDtypeStruct(w_2.shape, bf16),
+            jax.ShapeDtypeStruct((1, width), f32),
+            jax.ShapeDtypeStruct((1, wide), f32),
+        ],
+        in_specs=[block(width), block(width)] + [whole(a) for a in consts],
+        out_specs=[
+            block(width), block(wide), block(wide), block(4 * narrow),
+            fixed(*w_1.shape), fixed(*w_2.shape), fixed(1, width), fixed(1, wide),
+        ],
+        scratch_shapes=[pltpu.VMEM(w_1.shape, f32), pltpu.VMEM(w_2.shape, f32)],
+        compiler_params=pltpu.CompilerParams(vmem_limit_bytes=60 << 20),
+        name="row_work",
+    )(tok_all, cot_all, *consts)
+
+
 def swap_rotary(values):
     lane = lax.rem(lax.broadcasted_iota(jnp.int32, values.shape, 1), 64)
     half = ROT // 2
@@ -939,91 +1260,170 @@
     )
 
 
-def attend_kernel(rows_ref, seg_q, seg_k, cos_ref, sin_ref, out_ref, grad_ref, gq, gk, gv):
-    pack_rows, width = rows_ref.shape[1], out_ref.shape[2]
+def attend_kernel(four, perm, seg_q, seg_k, pos, freq, sign, back_ref, laid, gq, gk, gv, cos_v, sin_v):
+    pack = pl.program_id(1)
+    pack_rows, width = back_ref.shape[1], back_ref.shape[2] // 4
+    bf16, f32 = jnp.bfloat16, jnp.float32
     scale = 64 ** (-0.5)
     lane = lax.broadcasted_iota(jnp.int32, (1, width), 1)
+    total = four.shape[1]
+    for block in range(pack_rows // BLOCK):
+        here = slice(block * BLOCK, (block + 1) * BLOCK)
+        target = pack * pack_rows + block * BLOCK + lax.broadcasted_iota(jnp.int32, (BLOCK, total), 0)
+        chosen = jnp.where(perm[0] == target, 1.0, 0.0).astype(bf16)
+        got = dot(chosen, four[0])
+        angle = pos[0, here, :] * freq[...]
+        cos, sin = jnp.cos(angle), jnp.sin(angle) * sign[...]
+        cos_v[here, :] = cos
+        sin_v[here, :] = sin
+        for c in range(2):
+            at = slice(c * width, (c + 1) * width)
+            part = got[:, at]
+            laid[here, at] = (part * cos + swap_rotary(part) * sin).astype(bf16)
+        laid[here, 2 * width :] = got[:, 2 * width :].astype(bf16)
     gk[...] = jnp.zeros_like(gk)
     gv[...] = jnp.zeros_like(gv)
-    nt = (((1,), (1,)), ((), ()))
-    tn = (((0,), (0,)), ((), ()))
-
-    def dot(a, b, dims=(((1,), (0,)), ((), ()))):
-        return lax.dot_general(a, b, dims, preferred_element_type=jnp.float32)
-
     for block in range(pack_rows // BLOCK):
         low = max(0, block * BLOCK - SPAN)
         high = (block + 1) * BLOCK
         here = slice(block * BLOCK, high)
-        keys = rows_ref[0, low:high, width : 2 * width]
-        values = rows_ref[0, low:high, 2 * width : 3 * width]
-        seg_here = seg_q[0, here, :]
-        seg_there = seg_k[0, :, low:high]
+        keys = laid[low:high, width : 2 * width]
+        values = laid[low:high, 2 * width : 3 * width]
         row = lax.broadcasted_iota(jnp.int32, (BLOCK, high - low), 0) + block * BLOCK
         column = lax.broadcasted_iota(jnp.int32, (BLOCK, high - low), 1) + low
-        allowed = (seg_here == seg_there) & (column <= row)
+        allowed = (seg_q[0, here, :] == seg_k[0, :, low:high]) & (column <= row)
         attended = None
         for head in range(2):
             mine = (lane // 64) == head
-            query = jnp.where(mine, rows_ref[0, here, 0:width], 0)
-            grad = jnp.where(mine, rows_ref[0, here, 3 * width : 4 * width], 0)
+            query = jnp.where(mine, laid[here, 0:width], 0)
+            grad = jnp.where(mine, laid[here, 3 * width : 4 * width], 0)
             key = jnp.where(mine, keys, 0)
             value = jnp.where(mine, values, 0)
-            scores = jnp.where(allowed, dot(query, key, nt) * scale, NEG_FILL)
+            scores = jnp.where(allowed, dot(query, key, NT) * scale, NEG_FILL)
             peak = jnp.max(scores, axis=1, keepdims=True)
             weights = jnp.exp(scores - peak)
             weights = weights * (1.0 / jnp.sum(weights, axis=1, keepdims=True))
-            weights_b = weights.astype(jnp.bfloat16)
+            weights_b = weights.astype(bf16)
             out = dot(weights_b, value)
             attended = out if attended is None else attended + out
-            delta = jnp.sum(grad.astype(jnp.float32) * out, axis=1, keepdims=True)
-            inner = dot(grad, value, nt)
-            grad_scores = (weights * (inner - delta)).astype(jnp.bfloat16)
-            part = dot(grad_scores, key) * scale
+            delta = jnp.sum(grad.astype(f32) * out, axis=1, keepdims=True)
+            inner = dot(grad, value, NT)
+            grad_scores = (weights * (inner - delta)).astype(bf16)
+            part = dot(grad_scores, key)
             if head == 0:
                 gq[here, :] = part
             else:
                 gq[here, :] += part
-            gk[low:high, :] += dot(grad_scores, query, tn)
-            gv[low:high, :] += dot(weights_b, grad, tn)
-        out_ref[0, here, :] = attended.astype(jnp.bfloat16)
-    cos = cos_ref[0]
-    sin = sin_ref[0]
-    q_all = gq[...]
-    grad_ref[0, :, 0:width] = (q_all * cos - swap_rotary(q_all) * sin).astype(jnp.bfloat16)
-    k_all = gk[...] * scale
-    grad_ref[0, :, width : 2 * width] = (k_all * cos - swap_rotary(k_all) * sin).astype(jnp.bfloat16)
-    grad_ref[0, :, 2 * width : 3 * width] = gv[...].astype(jnp.bfloat16)
-
-
-def attend(rows, segment, cos, sin):
-    packs, pack_rows, wide = rows.shape
+            gk[low:high, :] += dot(grad_scores, query, TN)
+            gv[low:high, :] += dot(weights_b, grad, TN)
+        back_ref[0, here, 0:width] = attended.astype(bf16)
+    for c, ref in ((1, gq), (2, gk)):
+        grads = ref[...] * scale
+        turned = grads * cos_v[...] - swap_rotary(grads) * sin_v[...]
+        back_ref[0, :, c * width : (c + 1) * width] = turned.astype(bf16)
+    back_ref[0, :, 3 * width :] = gv[...].astype(bf16)
+
+
+def attend(four, permutation, segment, position, packs):
+    micro, total, wide = four.shape
+    pack_rows = total // packs
     width = wide // 4
+    lane = jnp.arange(width, dtype=jnp.int32) % 64
+    power = ROPE_BASE ** (-2.0 * (lane % (ROT // 2)).astype(jnp.float32) / ROT)
+    freq = jnp.where(lane < ROT, power, 0.0)[None, :]
+    sign = jnp.where(lane < ROT // 2, -1.0, 1.0)[None, :]
+
+    def by_pack(*s):
+        return pl.BlockSpec((1,) + s, lambda m, k: (m * packs + k, 0, 0))
+
+    line = pl.BlockSpec((1, width), lambda m, k: (0, 0))
+    plane = pltpu.VMEM((pack_rows, width), jnp.float32)
     return pl.pallas_call(
         attend_kernel,
-        grid=(packs,),
+        grid=(micro, packs),
+        out_shape=jax.ShapeDtypeStruct((micro * packs, pack_rows, wide), jnp.bfloat16),
+        in_specs=[
+            pl.BlockSpec((1, total, wide), lambda m, k: (m, 0, 0)),
+            pl.BlockSpec((1, 1, total), lambda m, k: (m, 0, 0)),
+            by_pack(pack_rows, 1),
+            by_pack(1, pack_rows),
+            by_pack(pack_rows, 1),
+            line,
+            line,
+        ],
+        out_specs=by_pack(pack_rows, wide),
+        scratch_shapes=[pltpu.VMEM((pack_rows, wide), jnp.bfloat16)] + [plane] * 5,
+        compiler_params=pltpu.CompilerParams(vmem_limit_bytes=48 << 20),
+        name="attend",
+    )(
+        four, permutation[:, None, :], segment[:, :, None], segment[:, None, :],
+        position.astype(jnp.float32)[:, :, None], freq, sign,
+    )
+
+
+def after_kernel(laid, perm, normed, cot, back_out, g_d, g_q, qkv_sum, acc_d, acc_q):
+    step = pl.program_id(0)
+
+    @pl.when(step == 0)
+    def _():
+        acc_d[...] = jnp.zeros_like(acc_d)
+        acc_q[...] = jnp.zeros_like(acc_q)
+        qkv_sum[...] = jnp.zeros_like(qkv_sum)
+
+    f32, bf16 = jnp.float32, jnp.bfloat16
+    size, total = normed.shape[1], laid.shape[1]
+    narrow = laid.shape[2] // 4
+    column = lax.broadcasted_iota(jnp.int32, (size, total), 1)
+    chosen = jnp.where(perm[0] == column, 1.0, 0.0).astype(bf16)
+    back = dot(chosen, laid[0]).astype(bf16)
+    back_out[0] = back
+    grads = back[:, narrow:]
+    acc_d[...] += dot(back[:, :narrow], cot[0], TN)
+    acc_q[...] += dot(normed[0], grads, TN)
+    qkv_sum[...] += jnp.sum(grads.astype(f32), axis=0, keepdims=True)
+
+    @pl.when(step == pl.num_programs(0) - 1)
+    def _():
+        g_d[...] = acc_d[...].astype(bf16)
+        for c in range(3):
+            g_q[c] = acc_q[:, c * narrow : (c + 1) * narrow].astype(bf16)
+
+
+def after(laid, permutation, normed, cot_all, size):
+    micro, total, wide = laid.shape
+    width = normed.shape[2]
+    narrow = wide // 4
+    per = total // size
+
+    def block(w):
+        return pl.BlockSpec((1, size, w), lambda i: (i // per, i % per, 0))
+
+    def fixed(*s):
+        return pl.BlockSpec(s, lambda i: (0,) * len(s))
+
+    return pl.pallas_call(
+        after_kernel,
+        grid=(micro * per,),
         out_shape=[
-            jax.ShapeDtypeStruct((packs, pack_rows, width), jnp.bfloat16),
-            jax.ShapeDtypeStruct((packs, pack_rows, 3 * width), jnp.bfloat16),
+            jax.ShapeDtypeStruct(laid.shape, jnp.bfloat16),
+            jax.ShapeDtypeStruct((narrow, width), jnp.bfloat16),
+            jax.ShapeDtypeStruct((3, width, narrow), jnp.bfloat16),
+            jax.ShapeDtypeStruct((1, 3 * narrow), jnp.float32),
         ],
         in_specs=[
-            pl.BlockSpec((1, pack_rows, wide), lambda i: (i, 0, 0)),
-            pl.BlockSpec((1, pack_rows, 1), lambda i: (i, 0, 0)),
-            pl.BlockSpec((1, 1, pack_rows), lambda i: (i, 0, 0)),
-            pl.BlockSpec((1, pack_rows, width), lambda i: (i, 0, 0)),
-            pl.BlockSpec((1, pack_rows, width), lambda i: (i, 0, 0)),
+            pl.BlockSpec((1, total, wide), lambda i: (i // per, 0, 0)),
+            block(1),
+            block(width),
+            block(width),
         ],
-        out_specs=[
-            pl.BlockSpec((1, pack_rows, width), lambda i: (i, 0, 0)),
-            pl.BlockSpec((1, pack_rows, 3 * width), lambda i: (i, 0, 0)),
+        out_specs=[block(wide), fixed(narrow, width), fixed(3, width, narrow), fixed(1, 3 * narrow)],
+        scratch_shapes=[
+            pltpu.VMEM((narrow, width), jnp.float32),
+            pltpu.VMEM((width, 3 * narrow), jnp.float32),
         ],
-        scratch_shapes=[pltpu.VMEM((pack_rows, width), jnp.float32)] * 3,
         compiler_params=pltpu.CompilerParams(vmem_limit_bytes=48 << 20),
-        cost_estimate=pl.CostEstimate(
-            flops=packs * 14 * pack_rows * pack_rows * width, bytes_accessed=packs * pack_rows * width * 24, transcendentals=0
-        ),
-        name="attend",
-    )(rows, segment[:, :, None], segment[:, None, :], cos, sin)
+        name="after",
+    )(laid, permutation[:, :, None], normed, cot_all)
 
 
 def fast_body(
@@ -1031,7 +1431,7 @@
     dense_weight, dense_bias, fc1_weight, fc1_bias, fc2_weight, fc2_bias,
 ):
     y, h, l, x, t = place()
-    f32, bf16 = jnp.float32, jnp.bfloat16
+    f32 = jnp.float32
     micro, rows, share = tokens.shape
     width = share * 2
     total = rows * 16
@@ -1048,152 +1448,53 @@
         tokens, cotangent, qkv_weight.transpose(1, 0, 2), dense_weight, fc1_weight, fc2_weight, small
     )
     small = small.reshape(2, 64 * 128).astype(f32)
-    gain = small[:, 0:share].reshape(width)
-    shift = small[:, share : 2 * share].reshape(width)
-    out_shift = (small[:, 2 * share : 3 * share] + small[:, 3 * share : 4 * share]).reshape(width)
+    gain = small[:, 0:share].reshape(1, width)
+    shift = small[:, share : 2 * share].reshape(1, width)
+    out_shift = (small[:, 2 * share : 3 * share] + small[:, 3 * share : 4 * share]).reshape(1, width)
     at = 4 * share
     q_shift = small[:, at : at + qkv_bias.size].reshape((2,) + qkv_bias.shape)
     q_shift = q_shift.transpose(1, 2, 0, 3).reshape(3, -1)
     at += qkv_bias.size
     f_shift = small[:, at : at + fc1_bias.size].reshape((2,) + fc1_bias.shape).transpose(1, 0, 2).reshape(-1)
-    q_shift = lax.dynamic_slice_in_dim(q_shift, block * narrow, narrow, 1)
-    f_shift = lax.dynamic_slice_in_dim(f_shift, block * wide, wide, 0)
+    q_shift = lax.dynamic_slice_in_dim(q_shift, block * narrow, narrow, 1).reshape(1, -1)
+    f_shift = lax.dynamic_slice_in_dim(f_shift, block * wide, wide, 0).reshape(1, -1)
 
     places = jnp.arange(pack_rows, dtype=jnp.int32)
     segment, position = jax.vmap(lambda row: segment_layout(row, places))(
         lengths.reshape(micro * packs, -1)
     )
-    position = position.reshape(micro, total).astype(f32)
-    chosen = (permutation[:, None, :] == jnp.arange(total, dtype=jnp.int32)[None, :, None]).astype(bf16)
-    half = ROT // 2
-    freq = ROPE_BASE ** (-2.0 * jnp.arange(half, dtype=f32) / ROT)
-
-    def tables(pos):
-        angles = pos[..., None] * freq
-        cos, sin = jnp.cos(angles), jnp.sin(angles)
-        rest = jnp.ones(pos.shape + (64 - ROT,), f32)
-        cos = jnp.concatenate([cos, cos, rest], -1)
-        sin = jnp.concatenate([-sin, sin, 0 * rest], -1)
-        return jnp.concatenate([cos, cos], -1), jnp.concatenate([sin, sin], -1)
-
-    cos_l, sin_l = tables(position)
-    pos_a = jnp.einsum("mla,ml->ma", chosen, position, precision=lax.Precision.HIGHEST)
-    cos_a, sin_a = tables(pos_a)
-
-    xs = tok_all.astype(f32)
-    center = xs - jnp.mean(xs, axis=-1, keepdims=True)
-    r = lax.rsqrt(jnp.mean(center * center, axis=-1, keepdims=True) + EPSILON)
-    normed = (center * r * gain + shift).astype(bf16)
-    pre = jnp.einsum("mrd,dh->mrh", normed, w_1, preferred_element_type=f32) + f_shift
-    activ, gelu_back = jax.vjp(partial(jax.nn.gelu, approximate=True), pre)
-    activ = activ.astype(bf16)
-    grad_activ = jnp.einsum("mrd,hd->mrh", cot_all, w_2, preferred_element_type=f32)
-    grad_pre = gelu_back(grad_activ)[0].astype(bf16)
-    g_w1 = jnp.einsum("mrd,mrh->dh", normed, grad_pre, preferred_element_type=f32).astype(bf16)
-    g_w2 = jnp.einsum("mrh,mrd->hd", activ, cot_all, preferred_element_type=f32).astype(bf16)
-    qkv = [
-        jnp.einsum("mrd,de->mre", normed, w_q[c], preferred_element_type=f32) + q_shift[c]
-        for c in range(3)
-    ]
-
-    def rotated(v):
-        lane = lax.broadcasted_iota(jnp.int32, v.shape, 2) % 64
-        other = jnp.where(lane < half, jnp.roll(v, -half, 2), jnp.roll(v, half, 2))
-        return v * cos_a + other * sin_a
-
-    grad_att = jnp.einsum("mrd,ed->mre", cot_all, w_d, preferred_element_type=f32)
-    four = jnp.concatenate([rotated(qkv[0]), rotated(qkv[1]), qkv[2], grad_att], -1).astype(bf16)
-    laid = jnp.einsum("mla,mae->mle", chosen, four, preferred_element_type=f32).astype(bf16)
-    attended, grad_qkv = attend(
-        laid.reshape(micro * packs, pack_rows, -1),
-        segment,
-        cos_l.reshape(micro * packs, pack_rows, -1),
-        sin_l.reshape(micro * packs, pack_rows, -1),
-    )
-    back = jnp.concatenate([attended, grad_qkv], -1).reshape(micro, total, 4 * narrow)
-    back = jnp.einsum("mla,mle->mae", chosen, back, preferred_element_type=f32).astype(bf16)
-    attended, grad_qkv = back[..., :narrow], back[..., narrow:]
-    g_wd = jnp.einsum("mre,mrd->ed", attended, cot_all, preferred_element_type=f32).astype(bf16)
-    g_wq = jnp.stack(
-        [
-            jnp.einsum(
-                "mrd,mre->de", normed, grad_qkv[..., c * narrow : (c + 1) * narrow], preferred_element_type=f32
-            )
-            for c in range(3)
-        ]
-    ).astype(bf16)
-
-    def side(v):
-        v = v.reshape(micro, 2, 2, 4 * rows, v.shape[-1])
-        return lax.dynamic_index_in_dim(v, h, 2, keepdims=False).reshape(micro, 2, 4, rows, v.shape[-1])
-
-    out_part = jnp.einsum("mycre,ed->ycmrd", side(attended), w_d, preferred_element_type=f32) + jnp.einsum(
-        "mycre,ed->ycmrd", side(activ), w_2, preferred_element_type=f32
-    )
-    g_side = side(grad_qkv)
-    norm_part = jnp.einsum("mycre,de->ycmrd", side(grad_pre), w_1, preferred_element_type=f32) + sum(
-        jnp.einsum(
-            "mycre,de->ycmrd", g_side[..., c * narrow : (c + 1) * narrow], w_q[c], preferred_element_type=f32
-        )
-        for c in range(3)
-    )
-
-    def summed(v):
-        v = v.astype(bf16)
-        v = lax.psum_scatter(v, "t", scatter_dimension=4, tiled=True)
-        v = lax.psum_scatter(v, "y", scatter_dimension=0, tiled=True)
-        v = v.reshape((2, 2) + v.shape[2:])
-        v = lax.psum_scatter(v, "l", scatter_dimension=0, tiled=True)
-        v = lax.psum_scatter(v, "x", scatter_dimension=1, tiled=True)
-        return v.reshape(micro, rows, share).astype(f32)
-
-    out_sum, norm_sum = summed(out_part), summed(norm_part)
-    at = t * share
-
-    def mine(v):
-        return lax.dynamic_slice_in_dim(v, at, share, 0)
-
-    layer_out = (tokens.astype(f32) + out_sum + mine(out_shift)).astype(bf16)
-    group = y * 8 + h * 4 + l * 2 + x
-    x_rows = lax.dynamic_slice_in_dim(tok_all, group * rows, rows, 1).astype(f32)
-    x_mid = x_rows - jnp.mean(x_rows, axis=-1, keepdims=True)
-    r_own = lax.rsqrt(jnp.mean(x_mid * x_mid, axis=-1, keepdims=True) + EPSILON)
-    hat = lax.dynamic_slice_in_dim(x_mid * r_own, at, share, 2)
-    scaled = mine(gain) * norm_sum
-    sums = lax.psum(jnp.stack([scaled.sum(-1), (scaled * hat).sum(-1)]), "t") / width
-    grad_tokens = (
-        cotangent.astype(f32) + r_own * (scaled - sums[0][..., None] - hat * sums[1][..., None])
-    ).astype(bf16)
-
-    g_small = jnp.stack([(norm_sum * hat).sum((0, 1)), norm_sum.sum((0, 1))])
-    g_small = lax.psum(g_small, ("y", "h", "l", "x"))
-    g_small = lax.all_gather(g_small, "t", axis=1, tiled=True)
-    g_small = lax.dynamic_slice_in_dim(g_small, y * share, share, 1)
-    g_bias = jnp.concatenate([grad_qkv.astype(f32).sum((0, 1)), grad_pre.astype(f32).sum((0, 1))])
-    g_bias = lax.all_gather(g_bias, ("y", "l", "x"), axis=0)
-    g_qb = g_bias[:, : 3 * narrow].reshape(8, 3, narrow).transpose(1, 0, 2).reshape(3, -1, 64)
-    g_qb = lax.dynamic_slice_in_dim(g_qb, y * 32, 32, 2)
-    g_fb = g_bias[:, 3 * narrow :].reshape(16, -1)
-    g_fb = lax.dynamic_slice_in_dim(g_fb, y * fc1_bias.shape[1], fc1_bias.shape[1], 1)
-    cot_sum = lax.dynamic_slice_in_dim(
-        cot_all.reshape(micro * total, width), y * share, share, 1
-    ).astype(f32).sum(0)
-
+    normed, activ, grad_pre, four, g_w1, g_w2, cot_sum, pre_sum = row_work(
+        tok_all, cot_all, w_1, w_2, w_q, w_d, gain, shift, f_shift, q_shift, 4 * rows
+    )
+    laid = attend(four, permutation, segment, position, packs)
+    back, g_wd, g_wq, qkv_sum = after(
+        laid.reshape(micro, total, -1), permutation, normed, cot_all, 4 * rows
+    )
+    layer_out, grad_tokens, g_ln = fold(
+        activ, grad_pre, back, tok_all, cotangent, w_1, w_2, w_q, w_d, gain, out_shift
+    )
+    g_bias = jnp.pad(jnp.concatenate([qkv_sum, pre_sum], 1), ((0, 7), (0, 0)))
     j_1, j_2 = join(
         [g_w1, g_w2], [(0, 1, "x"), (1, 0, "l")], [fc1_weight.shape, fc2_weight.shape], 1, "join_mlp"
     )
-    j_q, j_d = join(
-        [g_wq, g_wd],
-        [(1, 2, "x"), (1, 0, "l")],
-        [(3,) + dense_weight.shape, dense_weight.shape],
+    j_q, j_d, j_b = join(
+        [g_wq, g_wd, g_bias],
+        [(1, 2, "x"), (1, 0, "l"), (None, 0, "l")],
+        [(3,) + dense_weight.shape, dense_weight.shape, (64, g_bias.shape[1])],
         2,
         "join_att",
     )
+    g_bias = j_b.reshape(8, 8, -1)[:, 0]
+    g_qb = g_bias[:, : 3 * narrow].reshape(8, 3, narrow).transpose(1, 0, 2).reshape(3, -1, 64)
+    g_qb = lax.dynamic_slice_in_dim(g_qb, y * qkv_bias.shape[2], qkv_bias.shape[2], 2)
+    g_fb = g_bias[:, 3 * narrow :].reshape(fc1_bias.shape[0], -1)
+    g_fb = lax.dynamic_slice_in_dim(g_fb, y * fc1_bias.shape[1], fc1_bias.shape[1], 1)
+    cot_sum = lax.dynamic_slice_in_dim(cot_sum[0], y * share, share, 0)
     return (
         layer_out,
         grad_tokens,
-        g_small[0],
-        g_small[1],
+        g_ln[0],
+        g_ln[1],
         j_q.astype(f32).transpose(1, 0, 2),
         g_qb,
         j_d.astype(f32),

time: 1170 us -> 745 us (0.64)
  matrix products: 253 us -> 0 us
  Pallas kernels: 426 us -> 676 us
  waiting for transfers between devices: 217 us -> 0 us
  other arithmetic: 113 us -> 38.9 us
  blocking collectives: 72.3 us -> 0 us
  local copies, waits for them, and re-layouts: 66.5 us -> 19.8 us
  between operations: 15 us -> 1.24 us
    dot_general x21 -> x0, matrix products: 253 us -> none  [the longest x3 36.3 us: fast_body(): jnp.einsum('mycre,de->ycmrd', g_side[..., c * narrow:(c + 1) * narrow], w...]
    pallas_call x1 -> x4, Pallas kernels: 33.5 us -> 270 us  [the longest x1 119 us: fold(): pl.pallas_call(fold_kernel, out_shape=[jax.ShapeDtypeStruct(cot.shape, co...]
    unnamed x8 -> x0, waiting for transfers between devices: 201 us -> none
    psum x2 -> x0, blocking collectives: 43.6 us -> none  [the longest x1 41.2 us: fast_body(): g_small = lax.psum(g_small, ('y', 'h', 'l', 'x'))]
    all_gather x2 -> x0, blocking collectives: 28.6 us -> none  [the longest x1 26.8 us: fast_body(): g_bias = lax.all_gather(g_bias, ('y', 'l', 'x'), axis=0)]
    reduce_sum x8 -> x0, other arithmetic: 26.7 us -> none  [the longest x1 7.63 us: fast_body(): center = xs - jnp.mean(xs, axis=-1, keepdims=True)]
    concatenate x5 -> x0, local copies, waits for them, and re-layouts: 23.8 us -> none  [tables(): return (jnp.concatenate([cos, cos], -1), jnp.concatenate([sin, sin], -1))]
    convert_element_type x5 -> x1, other arithmetic: 20.7 us -> 1.73 us  [attend(): position.astype(jnp.float32)[:, :, None]]
  transfers between devices with their start and end apart: 7 -> 0, of which waited for: 2 -> 0; matrix products, arithmetic and copies ran while one was open for 16% -> 0% of each run, Pallas kernels for 18% -> 0%
where the time goes in v2:
time: 745 us; the launch traced here: 736 us
  Pallas kernels  676 us (91%)
  other arithmetic  38.9 us (5%)
  local copies, waits for them, and re-layouts  19.8 us (3%)
    pallas_call x2, Pallas kernels, join(): pl.pallas_call(kernel, out_shape=[jax.ShapeDtypeStruct(s, a.dtype) for s,...  223 us
    pallas_call x1, Pallas kernels, spread(): pl.pallas_call(spread_kernel, out_shape=outs, in_specs=[pl.BlockSpec(memo...  183 us
    pallas_call x1, Pallas kernels, fold(): pl.pallas_call(fold_kernel, out_shape=[jax.ShapeDtypeStruct(cot.shape, co...  119 us
    pallas_call x1, Pallas kernels, row_work(): pl.pallas_call(rows_kernel, grid=(micro * per,), out_shape=[jax.ShapeDtyp...  76.1 us
    pallas_call x1, Pallas kernels, attend(): pl.pallas_call(attend_kernel, grid=(micro, packs), out_shape=jax.ShapeDty...  47.4 us
    pallas_call x1, Pallas kernels, after(): pl.pallas_call(after_kernel, grid=(micro * per,), out_shape=[jax.ShapeDty...  27.5 us

profile of v2, /device:TPU:0, one launch (start us, length us, event | category | flops | bytes accessed | tf_op | source)
XLA Modules:
  0.0 735.7 jit_solution(3072210507463347942)
XLA Ops:
  1.3 0.7 constant_dynamic-update-slice_fusion.2
  2.0 0.7 constant_dynamic-update-slice_fusion.1
  3.4 0.8 reshape.183
  4.4 0.9 dynamic-update-slice.5
  5.9 182.9 %spread.1 = (bf16[2,2048,2048]{2,1,0:T(8,128)(2,1)}, bf16[2,2048,2048]{2,1,0:T(8,128)(2,1)}, bf16[3,2048,128]{2,1,0:T(8,128)(2,1)}, bf16[128,2048]{1,0:T(8,128)(...) custom-call(bf16[2,128,1024]{2,1,0:T(8,128)(2,1)} %tok.1, ...), custom_call_target="tpu_custom_call" | custom-call | tf_op jit(solution)/shard_map/spread/pallas_call | solution.py:814
  188.8 0.8 convert_bitcast_fusion.1
  192.4 76.1 %row_work.1 = (bf16[2,2048,2048]{2,1,0:T(8,128)(2,1)}, bf16[2,2048,512]{2,1,0:T(8,128)(2,1)}, bf16[2,2048,512]{2,1,0:T(8,128)(2,1)}, bf16[2,2048,512]{2,1,0:T(8,...) custom-call(bf16[2,2048,2048]{2,1,0:T(8,128)(2,1)} %get-tuple-element.3, ...), custom_call_target="tpu_custom_call" | custom-call | tf_op jit(solution)/shard_map/row_work/pallas_call | solution.py:1230
  269.6 2.0 copy.40
  271.6 1.7 convert_element_type.46.pos
  273.4 47.4 %attend.1 = bf16[4,1024,512]{2,1,0:T(8,128)(2,1)} custom-call(bf16[2,2048,512]{2,1,0:T(8,128)(2,1)} %get-tuple-element.48.four, s32[2,1,2048]{2,1,0:T(1,128)S(1)} %broadcast_in_dim.65.perm, s32[4,1024,1]{2,1,0:T(8,128)S(1)} %copy.41.seg_q, s32[4,1,1024]{2,1,0:T(1,128)S(1)} %broadcast_in_dim.71.seg_k, f32[4,1024,1]{2,1,0:T(8,128)S(1)} %convert_element_type.46.pos, ...), custom_call_target="tpu_custom_call" | custom-call | tf_op jit(solution)/shard_map/attend/pallas_call | solution.py:1341
  321.3 27.5 %after.1 = (bf16[2,2048,512]{2,1,0:T(8,128)(2,1)}, bf16[128,2048]{1,0:T(8,128)(2,1)S(1)}, bf16[3,2048,128]{2,1,0:T(8,128)(2,1)S(1)}, f32[1,384]{1,0:T(1,128)S(1)}) custom-call(bf16[2,2048,512]{2,1,0:T(8,128)(2,1)} %bitcast.53, s32[2,2048,1]{2,1,0:T(8,128)S(1)} %copy.42.perm, bf16[2,2048,2048]{2,1,0:T(8,128)(2,1)} %get-tuple-element.49.normed, ...), custom_call_target="tpu_custom_call" | custom-call | tf_op jit(solution)/shard_map/after/pallas_call | solution.py:1404
  348.8 1.1 copy-done
  350.0 0.8 copy-done.1
  351.4 118.8 %fold.1 = (bf16[2,128,1024]{2,1,0:T(8,128)(2,1)}, bf16[2,128,1024]{2,1,0:T(8,128)(2,1)}, f32[8,1024]{1,0:T(8,128)}) custom-call(bf16[2,2048,512]{2,1,0:T(8,128)(2,1)} %get-tuple-element.46.activ, bf16[2,2048,512]{2,1,0:T(8,128)(2,1)} %get-tuple-element.47.grad_pre, bf16[2,2048,512]{2,1,0:T(8,128)(2,1)} %get-tuple-element.50.back, ...), custom_call_target="tpu_custom_call" | custom-call | tf_op jit(solution)/shard_map/fold/pallas_call | solution.py:1128
  470.2 1.4 fusion.5
  472.3 84.1 %join_att.1 = (bf16[3,1024,1024]{2,1,0:T(8,128)(2,1)}, bf16[1024,1024]{1,0:T(8,128)(2,1)}, f32[64,896]{1,0:T(8,128)}) custom-call(bf16[3,2048,128]{2,1,0:T(8,128)(2,1)} %copy-done, bf16[128,2048]{1,0:T(8,128)(2,1)} %copy-done.1, f32[8,896]{1,0:T(8,128)} %select_maximum_fusion.refs_2_), custom_call_target="tpu_custom_call" | custom-call | tf_op jit(solution)/shard_map/join_att/pallas_call | solution.py:920
  556.4 9.3 %convert_bitcast_fusion = f32[1024,3,1024]{2,0,1:T(8,128)} fusion(bf16[3,1024,1024]{2,1,0:T(8,128)(2,1)} %get-tuple-element.58), kind=kLoop, calls=%fused_computation | loop fusion | flops 3145728 | bytes 18874368 | tf_op jit(solution)/shard_map/transpose | solution.py:1498
  565.6 1.0 slice.50
  567.4 2.5 convert_element_type.48
  569.9 139.1 %join_mlp.1 = (bf16[1024,4096]{1,0:T(8,128)(2,1)}, bf16[4096,1024]{1,0:T(8,128)(2,1)}) custom-call(bf16[2048,512]{1,0:T(8,128)(2,1)} %get-tuple-element.62.refs_0_, bf16[512,2048]{1,0:T(8,128)(2,1)} %get-tuple-element.63.refs_1_), custom_call_target="tpu_custom_call" | custom-call | tf_op jit(solution)/shard_map/join_mlp/pallas_call | solution.py:920
  709.0 11.8 %convert_element_type.49 = f32[1024,4096]{1,0:T(8,128)} convert(bf16[1024,4096]{1,0:T(8,128)(2,1)} %get-tuple-element.64) | non-fusion elementwise | flops 4194304 | bytes 25165824 | tf_op jit(solution)/shard_map/convert_element_type | solution.py:1502
  721.4 11.8 %convert_element_type.50 = f32[4096,1024]{1,0:T(8,128)} convert(bf16[4096,1024]{1,0:T(8,128)(2,1)} %get-tuple-element.65) | non-fusion elementwise | flops 4194304 | bytes 25165824 | tf_op jit(solution)/shard_map/convert_element_type | solution.py:1504
  733.8 0.8 copy.64
  734.6 0.8 copy.65
  (56 shorter events, 9.9 us)
Async XLA Ops:
  192.3 76.1 %copy-start.5 = (s32[2,2048]{1,0:T(2,128)S(1)}, s32[2,2048]{1,0:T(2,128)}, u32[]{:S(2)}) copy-start(s32[2,2048]{1,0:T(2,128)} %param.17) | copy-start | bytes 49156
  192.3 76.2 %copy-start.7 = (s32[2,2,4]{2,1,0:T(2,128)S(1)}, s32[2,2,4]{2,1,0:T(2,128)}, u32[]{:S(2)}) copy-start(s32[2,2,4]{2,1,0:T(2,128)} %param.16) | copy-start | bytes 196
  348.8 1.1 copy-start
  350.0 0.8 copy-start.1
  351.4 120.3 %copy-start.8 = (f32[1,512]{1,0:T(1,128)S(1)}, f32[1,512]{1,0:T(1,128)}, u32[]{:S(2)}) copy-start(f32[1,512]{1,0:T(1,128)} %get-tuple-element.57) | copy-start | bytes 6148
  556.4 11.0 %copy-start.2 = (bf16[1024,1024]{1,0:T(8,128)(2,1)S(1)}, bf16[1024,1024]{1,0:T(8,128)(2,1)}, u32[]{:S(2)}) copy-start(bf16[1024,1024]{1,0:T(8,128)(2,1)} %get-tuple-element.60) | copy-start | bytes 6291460
  565.6 4.2 copy-start.9
  569.9 163.3 %copy-start.6 = (f32[1,1024]{1,0:T(1,128)}, f32[1,1024]{1,0:T(1,128)S(1)}, u32[]{:S(2)}) copy-start(f32[1,1024]{1,0:T(1,128)S(1)} %constant_dynamic-slice_fusion) | copy-start | bytes 12292
  721.4 12.4 %copy-start.4 = (bf16[2,128,1024]{2,1,0:T(8,128)(2,1)S(1)}, bf16[2,128,1024]{2,1,0:T(8,128)(2,1)}, u32[]{:S(2)}) copy-start(bf16[2,128,1024]{2,1,0:T(8,128)(2,1)} %get-tuple-element.109) | copy-start | bytes 1572868
  721.4 13.2 %copy-start.3 = (bf16[2,128,1024]{2,1,0:T(8,128)(2,1)S(1)}, bf16[2,128,1024]{2,1,0:T(8,128)(2,1)}, u32[]{:S(2)}) copy-start(bf16[2,128,1024]{2,1,0:T(8,128)(2,1)} %get-tuple-element.110) | copy-start | bytes 1572868

commit v3 on v2

--- a/solution.py
+++ b/solution.py
@@ -826,13 +826,19 @@
     )(tokens, cotangent, w_q, w_d, w_1, w_2, small)
 
 
-def join_kernel(count, parts, outs, local_sem, send_sem, recv_sem):
-    y, h, l, x, t = place()
-    device = {"y": {"y": 1 - y}, "l": {"l": 1 - l}, "x": {"x": 1 - x}}
-    greet([(device[a], True) for a in ("y", "l", "x")])
-
-    def half_of(i, yy):
-        ref, d_axis, _, _ = parts[i]
+class Join:
+    def __init__(self, parts, outs, local_sem, send_sem, recv_sem):
+        self.parts, self.outs = parts, outs
+        self.local_sem, self.send_sem, self.recv_sem = local_sem, send_sem, recv_sem
+        self.y, self.h, self.l, self.x, self.t = place()
+        self.device = {"y": {"y": 1 - self.y}, "l": {"l": 1 - self.l}, "x": {"x": 1 - self.x}}
+        self.numbers, self.sends = {}, []
+        self.every = range(len(parts))
+        self.first = [p[3] for p in parts]
+        self.then = ["l" if p[3] == "x" else "x" for p in parts]
+
+    def half_of(self, i, yy):
+        ref, d_axis, _, _ = self.parts[i]
         if d_axis is None:
             return ref
         n = ref.shape[d_axis] // 2
@@ -840,96 +846,79 @@
         where[d_axis] = pl.ds(pl.multiple_of(yy * n, n), n)
         return ref.at[tuple(where)]
 
-    def spot(i, yy, ll, xx):
-        ref, _, b_axis, _ = parts[i]
+    def spot(self, i, yy, ll, xx):
+        ref, _, b_axis, _ = self.parts[i]
         n = ref.shape[b_axis]
         where = [slice(None)] * len(ref.shape)
         where[b_axis] = pl.ds(pl.multiple_of((yy * 4 + ll * 2 + xx) * n, n), n)
-        return outs[i].at[tuple(where)]
-
-    numbers = {}
-
-    def number(key):
-        return numbers.setdefault(key, len(numbers))
-
-    sends = []
-
-    def send(i, source, target, key, axis):
-        n = number((i,) + key)
-        copy = pltpu.make_async_remote_copy(
-            src_ref=source, dst_ref=target, send_sem=send_sem.at[n], recv_sem=recv_sem.at[n],
-            device_id=device[axis], device_id_type=MESH,
-        )
-        copy.start()
-        sends.append(copy)
-
-    def got(i, target, key):
-        n = number((i,) + key)
-        pltpu.make_async_remote_copy(
-            src_ref=target, dst_ref=target, send_sem=send_sem.at[n], recv_sem=recv_sem.at[n],
-            device_id=device["y"], device_id_type=MESH,
-        ).wait_recv()
-
-    every = range(count)
-    hop = {"x": "l", "l": "x"}
-    first = {i: parts[i][3] for i in every}
-    for i in every:
-        send(i, half_of(i, 1 - y), spot(i, y, l, x), ("y",), "y")
-    for i in every:
-        send(i, half_of(i, y), spot(i, y, l, x), (0, first[i]), first[i])
-    for i in every:
-        send(i, half_of(i, y), spot(i, y, l, x), (0, hop[first[i]]), hop[first[i]])
-    locals_ = []
-    for i in every:
-        copy = pltpu.make_async_copy(half_of(i, y), spot(i, y, l, x), local_sem.at[i])
-        copy.start()
-        locals_.append(copy)
-
-    def beside(i, axis, yy):
-        return spot(i, yy, 1 - l if axis == "l" else l, 1 - x if axis == "x" else x)
-
-    for i in every:
-        a = first[i]
-        got(i, beside(i, a, y), (0, a))
-        send(i, beside(i, a, y), beside(i, a, y), (0, "far"), hop[a])
-    for i in every:
-        got(i, spot(i, 1 - y, l, x), ("y",))
-        send(i, spot(i, 1 - y, l, x), spot(i, 1 - y, l, x), (1, first[i]), first[i])
-        send(i, spot(i, 1 - y, l, x), spot(i, 1 - y, l, x), (1, hop[first[i]]), hop[first[i]])
-    for i in every:
-        a = first[i]
-        got(i, beside(i, a, 1 - y), (1, a))
-        send(i, beside(i, a, 1 - y), beside(i, a, 1 - y), (1, "far"), hop[a])
-    for i in every:
-        for yy, side in ((y, 0), (1 - y, 1)):
-            got(i, beside(i, hop[first[i]], yy), (side, hop[first[i]]))
-            got(i, spot(i, yy, 1 - l, 1 - x), (side, "far"))
-    for copy in locals_:
-        copy.wait()
-    for copy in sends:
-        copy.wait_send()
-
-
-def join(arrays, plan, shapes, collective_id, name):
-    count = len(arrays)
-
-    def kernel(*refs):
-        parts = [(refs[i],) + plan[i] for i in range(count)]
-        join_kernel(count, parts, refs[count : 2 * count], *refs[2 * count :])
-
-    return pl.pallas_call(
-        kernel,
-        out_shape=[jax.ShapeDtypeStruct(s, a.dtype) for s, a in zip(shapes, arrays)],
-        in_specs=[pl.BlockSpec(memory_space=pl.ANY)] * count,
-        out_specs=[pl.BlockSpec(memory_space=pl.ANY)] * count,
-        scratch_shapes=[
-            pltpu.SemaphoreType.DMA((count,)),
-            pltpu.SemaphoreType.DMA((7 * count,)),
-            pltpu.SemaphoreType.DMA((7 * count,)),
-        ],
-        compiler_params=pltpu.CompilerParams(collective_id=collective_id, has_side_effects=True),
-        name=name,
-    )(*arrays)
+        return self.outs[i].at[tuple(where)]
+
+    def own(self, i, yy):
+        return self.spot(i, yy, self.l, self.x)
+
+    def beside(self, i, axis, yy):
+        l, x = self.l, self.x
+        return self.spot(i, yy, 1 - l if axis == "l" else l, 1 - x if axis == "x" else x)
+
+    def copy(self, n, source, target, axis):
+        return pltpu.make_async_remote_copy(
+            src_ref=source, dst_ref=target, send_sem=self.send_sem.at[n], recv_sem=self.recv_sem.at[n],
+            device_id=self.device[axis], device_id_type=MESH,
+        )
+
+    def send(self, i, source, target, key, axis):
+        n = self.numbers.setdefault((i,) + key, len(self.numbers))
+        self.copy(n, source, target, axis).start()
+        self.sends.append((n, i, axis))
+
+    def got(self, i, target, key):
+        self.copy(self.numbers[(i,) + key], target, target, "y").wait_recv()
+
+    def bring(self):
+        for i in self.every:
+            self.send(i, self.half_of(i, 1 - self.y), self.own(i, self.y), ("y",), "y")
+
+    def offer(self, axis):
+        for want in (True, False):
+            for i in self.every:
+                if (self.first[i] == axis) is want:
+                    self.send(i, self.half_of(i, self.y), self.own(i, self.y), (0, axis), axis)
+
+    def kept(self, i):
+        return pltpu.make_async_copy(self.half_of(i, self.y), self.own(i, self.y), self.local_sem.at[i])
+
+    def keep(self):
+        for i in self.every:
+            self.kept(i).start()
+
+    def far(self, side):
+        yy = 1 - self.y if side else self.y
+        for i in self.every:
+            a = self.first[i]
+            self.got(i, self.beside(i, a, yy), (side, a))
+            self.send(i, self.beside(i, a, yy), self.beside(i, a, yy), (side, "far"), self.then[i])
+
+    def brought(self):
+        for i in self.every:
+            ref = self.own(i, 1 - self.y)
+            self.got(i, ref, ("y",))
+            self.send(i, ref, ref, (1, self.first[i]), self.first[i])
+            self.send(i, ref, ref, (1, self.then[i]), self.then[i])
+
+    def end(self):
+        for i in self.every:
+            for side, yy in ((0, self.y), (1, 1 - self.y)):
+                self.got(i, self.beside(i, self.then[i], yy), (side, self.then[i]))
+                self.got(i, self.spot(i, yy, 1 - self.l, 1 - self.x), (side, "far"))
+        for i in self.every:
+            self.kept(i).wait()
+        for n, i, axis in self.sends:
+            self.copy(n, self.own(i, self.y), self.own(i, self.y), axis).wait_send()
+
+
+def join_sems(count):
+    sem = pltpu.SemaphoreType.DMA
+    return [sem((count,)), sem((7 * count,)), sem((7 * count,))]
 
 
 NN = (((1,), (0,)), ((), ()))
@@ -942,9 +931,9 @@
 
 
 def fold_kernel(
-    activ, grad_pre, back, tok_all, cot, w_1, w_2, w_q, w_d, gain, out_shift, layer_out, grad_out, ln_out,
-    act_v, pre_v, back_v, tok_v, give, core_in, give_n, sum_in, stat_v, stat_in, ln_v, ln_in,
-    load_sem, core_send, core_recv, hop_send, hop_recv, small_send, small_recv,
+    activ, grad_pre, back, tok_all, g_q, g_d, g_b, cot, w_1, w_2, w_q, w_d, gain, out_shift,
+    layer_out, grad_out, ln_out, j_q, j_d, j_b, act_v, pre_v, back_v, tok_v, give, core_in, give_n, sum_in, stat_v, stat_in, ln_v, ln_in,
+    load_sem, core_send, core_recv, hop_send, hop_recv, small_send, small_recv, *join_sem,
 ):
     y, h, l, x, t = place()
     rows, share = cot.shape[1], cot.shape[2]
@@ -964,7 +953,7 @@
         xx = 1 - x if dx else x
         return pl.ds(pl.multiple_of((yy * 8 + h * 4 + ll * 2 + xx) * rows, rows), rows)
 
-    owners = [(1, 0, 1), (1, 1, 1), (0, 0, 1), (0, 1, 1), (1, 0, 0), (1, 1, 0), (0, 1, 0), (0, 0, 0)]
+    owners = [(1, 1, 0), (1, 1, 1), (0, 1, 0), (0, 1, 1), (1, 0, 0), (1, 0, 1), (0, 0, 1), (0, 0, 0)]
     arrived = {}
     for o, owner in enumerate(owners):
         start = len(loads)
@@ -979,6 +968,11 @@
         load(tok_all.at[m, group_rows(0, 0, 0)], tok_v.at[pl.ds(m * rows, rows)])
     tok_loads = loads[start:]
     greet([(device[a], True) for a in ("t", "x", "y", "l", "h")])
+    parts = [(g_q, 1, 2, "x"), (g_d, 1, 0, "l"), (g_b, None, 0, "l")]
+    gather = Join(parts, (j_q, j_d, j_b), *join_sem)
+    gather.bring()
+    gather.offer("x")
+    gather.keep()
 
     def part(a, o, tt):
         columns = pl.ds(pl.multiple_of(tt * share, share), share)
@@ -1003,7 +997,7 @@
         )
         core[i].start()
 
-    hops = {0: ("x", "y", "l"), 1: ("y", "x", "l")}
+    hops = {0: ("l", "y", "x"), 1: ("y", "x", "l")}
     place_of = {"y": 0, "l": 1, "x": 2}
     slots, passed = {}, {}
 
@@ -1051,10 +1045,15 @@
             offer(*queue[i + ahead])
             pass_on(a, o, stage)
             if i == 7:
+                gather.offer("l")
                 for item in queue[i + ahead + 1 :]:
                     offer(*item)
+                gather.far(0)
+                gather.brought()
         else:
             pass_on(a, o, stage)
+            if i == 11:
+                gather.far(1)
     for copy in tok_loads:
         copy.wait()
     mine = pl.ds(pl.multiple_of(t * share, share), share)
@@ -1116,9 +1115,10 @@
         copy.wait_send()
     for copy in smalls:
         copy.wait_send()
-
-
-def fold(activ, grad_pre, back, tok_all, cot, w_1, w_2, w_q, w_d, gain, out_shift):
+    gather.end()
+
+
+def fold(activ, grad_pre, back, tok_all, g_q, g_d, g_b, cot, w_1, w_2, w_q, w_d, gain, out_shift):
     micro, rows, share = cot.shape
     both = micro * rows
     narrow = w_d.shape[0]
@@ -1131,9 +1131,12 @@
             jax.ShapeDtypeStruct(cot.shape, cot.dtype),
             jax.ShapeDtypeStruct(cot.shape, cot.dtype),
             jax.ShapeDtypeStruct((8, share), jnp.float32),
+            jax.ShapeDtypeStruct((3, share, share), g_q.dtype),
+            jax.ShapeDtypeStruct((share, share), g_d.dtype),
+            jax.ShapeDtypeStruct((64, g_b.shape[1]), g_b.dtype),
         ],
-        in_specs=[any_] * 4 + [vmem] * 7,
-        out_specs=[vmem] * 3,
+        in_specs=[any_] * 7 + [vmem] * 7,
+        out_specs=[vmem] * 3 + [any_] * 3,
         scratch_shapes=[
             held(8, w_1.shape[1]),
             held(8, w_1.shape[1]),
@@ -1154,12 +1157,13 @@
             sem((14,)),
             sem((6,)),
             sem((6,)),
-        ],
+        ]
+        + join_sems(3),
         compiler_params=pltpu.CompilerParams(
             collective_id=3, has_side_effects=True, vmem_limit_bytes=60 << 20
         ),
         name="fold",
-    )(activ, grad_pre, back, tok_all, cot, w_1, w_2, w_q, w_d, gain, out_shift)
+    )(activ, grad_pre, back, tok_all, g_q, g_d, g_b, cot, w_1, w_2, w_q, w_d, gain, out_shift)
 
 
 ROOT = 0.7978845608028654
@@ -1260,9 +1264,8 @@
     )
 
 
-def attend_kernel(four, perm, seg_q, seg_k, pos, freq, sign, back_ref, laid, gq, gk, gv, cos_v, sin_v):
-    pack = pl.program_id(1)
-    pack_rows, width = back_ref.shape[1], back_ref.shape[2] // 4
+def attend_pack(pack, four, perm, seg_q, seg_k, pos, freq, sign, back_ref, laid, gq, gk, gv, cos_v, sin_v):
+    pack_rows, width = laid.shape[0], laid.shape[1] // 4
     bf16, f32 = jnp.bfloat16, jnp.float32
     scale = 64 ** (-0.5)
     lane = lax.broadcasted_iota(jnp.int32, (1, width), 1)
@@ -1316,114 +1319,153 @@
                 gq[here, :] += part
             gk[low:high, :] += dot(grad_scores, query, TN)
             gv[low:high, :] += dot(weights_b, grad, TN)
-        back_ref[0, here, 0:width] = attended.astype(bf16)
+        back_ref[here, 0:width] = attended.astype(bf16)
     for c, ref in ((1, gq), (2, gk)):
         grads = ref[...] * scale
         turned = grads * cos_v[...] - swap_rotary(grads) * sin_v[...]
-        back_ref[0, :, c * width : (c + 1) * width] = turned.astype(bf16)
-    back_ref[0, :, 3 * width :] = gv[...].astype(bf16)
-
-
-def attend(four, permutation, segment, position, packs):
+        back_ref[:, c * width : (c + 1) * width] = turned.astype(bf16)
+    back_ref[:, 3 * width :] = gv[...].astype(bf16)
+
+
+def heads_kernel(
+    packs, all_packs, four, perm, seg_q, seg_k, pos, freq, sign, perm_c, normed, cot, g_1, g_2,
+    back_out, g_d, g_q, qkv_sum, j_1, j_2,
+    held, laid, gq, gk, gv, cos_v, sin_v, acc_d, acc_q, *join_sem,
+):
+    step = pl.program_id(0)
+    last = pl.num_programs(0) - 1
+    gather = Join([(g_1, 0, 1, "x"), (g_2, 1, 0, "l")], (j_1, j_2), *join_sem)
+    f32, bf16 = jnp.float32, jnp.bfloat16
+
+    @pl.when(step == 0)
+    def _():
+        greet([(d, True) for d in gather.device.values()])
+        gather.bring()
+        gather.offer("x")
+        gather.offer("l")
+        gather.keep()
+        acc_d[...] = jnp.zeros_like(acc_d)
+        acc_q[...] = jnp.zeros_like(acc_q)
+        qkv_sum[...] = jnp.zeros_like(qkv_sum)
+
+    @pl.when(step == all_packs - 1)
+    def _():
+        gather.far(0)
+
+    @pl.when(step == all_packs)
+    def _():
+        gather.brought()
+
+    @pl.when(step < all_packs)
+    def _():
+        attend_pack(
+            lax.rem(step, packs), four, perm, seg_q, seg_k, pos, freq, sign,
+            held.at[step], laid, gq, gk, gv, cos_v, sin_v,
+        )
+
+    @pl.when(step >= all_packs)
+    def _():
+        size, total = normed.shape[1], four.shape[1]
+        narrow = acc_d.shape[0]
+        per = total // size
+        pack_rows = held.shape[1]
+        first = (step - all_packs) // per * packs
+        column = lax.broadcasted_iota(jnp.int32, (size, pack_rows), 1)
+        back = None
+        for k in range(packs):
+            chosen = jnp.where(perm_c[0] == column + k * pack_rows, 1.0, 0.0).astype(bf16)
+            part = dot(chosen, held[first + k])
+            back = part if back is None else back + part
+        back = back.astype(bf16)
+        back_out[0] = back
+        grads = back[:, narrow:]
+        acc_d[...] += dot(back[:, :narrow], cot[0], TN)
+        acc_q[...] += dot(normed[0], grads, TN)
+        qkv_sum[...] += jnp.sum(grads.astype(f32), axis=0, keepdims=True)
+
+    @pl.when(step == last)
+    def _():
+        narrow = acc_d.shape[0]
+        g_d[...] = acc_d[...].astype(bf16)
+        for c in range(3):
+            g_q[c] = acc_q[:, c * narrow : (c + 1) * narrow].astype(bf16)
+        gather.far(1)
+        gather.end()
+
+
+def heads(four, permutation, segment, position, normed, cot_all, g_1, g_2, packs, size):
     micro, total, wide = four.shape
     pack_rows = total // packs
     width = wide // 4
+    deep = normed.shape[2]
+    all_packs = micro * packs
+    per = total // size
     lane = jnp.arange(width, dtype=jnp.int32) % 64
     power = ROPE_BASE ** (-2.0 * (lane % (ROT // 2)).astype(jnp.float32) / ROT)
     freq = jnp.where(lane < ROT, power, 0.0)[None, :]
     sign = jnp.where(lane < ROT // 2, -1.0, 1.0)[None, :]
 
     def by_pack(*s):
-        return pl.BlockSpec((1,) + s, lambda m, k: (m * packs + k, 0, 0))
-
-    line = pl.BlockSpec((1, width), lambda m, k: (0, 0))
+        return pl.BlockSpec((1,) + s, lambda i: (jnp.minimum(i, all_packs - 1), 0, 0))
+
+    def by_micro(*s):
+        return pl.BlockSpec((1,) + s, lambda i: (jnp.minimum(i, all_packs - 1) // packs, 0, 0))
+
+    def block(w):
+        def index(i):
+            n = jnp.maximum(i - all_packs, 0)
+            return (n // per, lax.rem(n, per), 0)
+
+        return pl.BlockSpec((1, size, w), index)
+
+    def fixed(*s):
+        return pl.BlockSpec(s, lambda i: (0,) * len(s))
+
+    any_ = pl.BlockSpec(memory_space=pl.ANY)
     plane = pltpu.VMEM((pack_rows, width), jnp.float32)
     return pl.pallas_call(
-        attend_kernel,
-        grid=(micro, packs),
-        out_shape=jax.ShapeDtypeStruct((micro * packs, pack_rows, wide), jnp.bfloat16),
+        partial(heads_kernel, packs, all_packs),
+        grid=(all_packs + micro * per,),
+        out_shape=[
+            jax.ShapeDtypeStruct(four.shape, jnp.bfloat16),
+            jax.ShapeDtypeStruct((width, deep), jnp.bfloat16),
+            jax.ShapeDtypeStruct((3, deep, width), jnp.bfloat16),
+            jax.ShapeDtypeStruct((1, 3 * width), jnp.float32),
+            jax.ShapeDtypeStruct((deep // 2, g_1.shape[1] * 8), g_1.dtype),
+            jax.ShapeDtypeStruct((g_2.shape[0] * 8, deep // 2), g_2.dtype),
+        ],
         in_specs=[
-            pl.BlockSpec((1, total, wide), lambda m, k: (m, 0, 0)),
-            pl.BlockSpec((1, 1, total), lambda m, k: (m, 0, 0)),
+            by_micro(total, wide),
+            by_micro(1, total),
             by_pack(pack_rows, 1),
             by_pack(1, pack_rows),
             by_pack(pack_rows, 1),
-            line,
-            line,
+            fixed(1, width),
+            fixed(1, width),
+            block(1),
+            block(deep),
+            block(deep),
+            any_,
+            any_,
         ],
-        out_specs=by_pack(pack_rows, wide),
-        scratch_shapes=[pltpu.VMEM((pack_rows, wide), jnp.bfloat16)] + [plane] * 5,
-        compiler_params=pltpu.CompilerParams(vmem_limit_bytes=48 << 20),
-        name="attend",
+        out_specs=[
+            block(wide), fixed(width, deep), fixed(3, deep, width), fixed(1, 3 * width), any_, any_,
+        ],
+        scratch_shapes=[
+            pltpu.VMEM((all_packs, pack_rows, wide), jnp.bfloat16),
+            pltpu.VMEM((pack_rows, wide), jnp.bfloat16),
+        ]
+        + [plane] * 5
+        + [pltpu.VMEM((width, deep), jnp.float32), pltpu.VMEM((deep, 3 * width), jnp.float32)]
+        + join_sems(2),
+        compiler_params=pltpu.CompilerParams(
+            collective_id=1, has_side_effects=True, vmem_limit_bytes=56 << 20
+        ),
+        name="heads",
     )(
         four, permutation[:, None, :], segment[:, :, None], segment[:, None, :],
-        position.astype(jnp.float32)[:, :, None], freq, sign,
-    )
-
-
-def after_kernel(laid, perm, normed, cot, back_out, g_d, g_q, qkv_sum, acc_d, acc_q):
-    step = pl.program_id(0)
-
-    @pl.when(step == 0)
-    def _():
-        acc_d[...] = jnp.zeros_like(acc_d)
-        acc_q[...] = jnp.zeros_like(acc_q)
-        qkv_sum[...] = jnp.zeros_like(qkv_sum)
-
-    f32, bf16 = jnp.float32, jnp.bfloat16
-    size, total = normed.shape[1], laid.shape[1]
-    narrow = laid.shape[2] // 4
-    column = lax.broadcasted_iota(jnp.int32, (size, total), 1)
-    chosen = jnp.where(perm[0] == column, 1.0, 0.0).astype(bf16)
-    back = dot(chosen, laid[0]).astype(bf16)
-    back_out[0] = back
-    grads = back[:, narrow:]
-    acc_d[...] += dot(back[:, :narrow], cot[0], TN)
-    acc_q[...] += dot(normed[0], grads, TN)
-    qkv_sum[...] += jnp.sum(grads.astype(f32), axis=0, keepdims=True)
-
-    @pl.when(step == pl.num_programs(0) - 1)
-    def _():
-        g_d[...] = acc_d[...].astype(bf16)
-        for c in range(3):
-            g_q[c] = acc_q[:, c * narrow : (c + 1) * narrow].astype(bf16)
-
-
-def after(laid, permutation, normed, cot_all, size):
-    micro, total, wide = laid.shape
-    width = normed.shape[2]
-    narrow = wide // 4
-    per = total // size
-
-    def block(w):
-        return pl.BlockSpec((1, size, w), lambda i: (i // per, i % per, 0))
-
-    def fixed(*s):
-        return pl.BlockSpec(s, lambda i: (0,) * len(s))
-
-    return pl.pallas_call(
-        after_kernel,
-        grid=(micro * per,),
-        out_shape=[
-            jax.ShapeDtypeStruct(laid.shape, jnp.bfloat16),
-            jax.ShapeDtypeStruct((narrow, width), jnp.bfloat16),
-            jax.ShapeDtypeStruct((3, width, narrow), jnp.bfloat16),
-            jax.ShapeDtypeStruct((1, 3 * narrow), jnp.float32),
-        ],
-        in_specs=[
-            pl.BlockSpec((1, total, wide), lambda i: (i // per, 0, 0)),
-            block(1),
-            block(width),
-            block(width),
-        ],
-        out_specs=[block(wide), fixed(narrow, width), fixed(3, width, narrow), fixed(1, 3 * narrow)],
-        scratch_shapes=[
-            pltpu.VMEM((narrow, width), jnp.float32),
-            pltpu.VMEM((width, 3 * narrow), jnp.float32),
-        ],
-        compiler_params=pltpu.CompilerParams(vmem_limit_bytes=48 << 20),
-        name="after",
-    )(laid, permutation[:, :, None], normed, cot_all)
+        position.astype(jnp.float32)[:, :, None], freq, sign, permutation[:, :, None], normed, cot_all, g_1, g_2,
+    )
 
 
 def fast_body(
@@ -1466,23 +1508,12 @@
     normed, activ, grad_pre, four, g_w1, g_w2, cot_sum, pre_sum = row_work(
         tok_all, cot_all, w_1, w_2, w_q, w_d, gain, shift, f_shift, q_shift, 4 * rows
     )
-    laid = attend(four, permutation, segment, position, packs)
-    back, g_wd, g_wq, qkv_sum = after(
-        laid.reshape(micro, total, -1), permutation, normed, cot_all, 4 * rows
-    )
-    layer_out, grad_tokens, g_ln = fold(
-        activ, grad_pre, back, tok_all, cotangent, w_1, w_2, w_q, w_d, gain, out_shift
+    back, g_wd, g_wq, qkv_sum, j_1, j_2 = heads(
+        four, permutation, segment, position, normed, cot_all, g_w1, g_w2, packs, 4 * rows
     )
     g_bias = jnp.pad(jnp.concatenate([qkv_sum, pre_sum], 1), ((0, 7), (0, 0)))
-    j_1, j_2 = join(
-        [g_w1, g_w2], [(0, 1, "x"), (1, 0, "l")], [fc1_weight.shape, fc2_weight.shape], 1, "join_mlp"
-    )
-    j_q, j_d, j_b = join(
-        [g_wq, g_wd, g_bias],
-        [(1, 2, "x"), (1, 0, "l"), (None, 0, "l")],
-        [(3,) + dense_weight.shape, dense_weight.shape, (64, g_bias.shape[1])],
-        2,
-        "join_att",
+    layer_out, grad_tokens, g_ln, j_q, j_d, j_b = fold(
+        activ, grad_pre, back, tok_all, g_wq, g_wd, g_bias, cotangent, w_1, w_2, w_q, w_d, gain, out_shift
     )
     g_bias = j_b.reshape(8, 8, -1)[:, 0]
     g_qb = g_bias[:, : 3 * narrow].reshape(8, 3, narrow).transpose(1, 0, 2).reshape(3, -1, 64)

time: 745 us -> 638 us (0.86)
  Pallas kernels: 676 us -> 567 us
    pallas_call x4 -> x1, Pallas kernels: 298 us -> 146 us  [heads(): pl.pallas_call(partial(heads_kernel, packs, all_packs), grid=(all_packs +...]
    pallas_call x1, Pallas kernels: 119 us -> 161 us  [fold(): pl.pallas_call(fold_kernel, out_shape=[jax.ShapeDtypeStruct(cot.shape, co...]
where the time goes in v3:
time: 638 us; the launch traced here: 628 us
  Pallas kernels  567 us (89%)
  other arithmetic  39.7 us (6%)
  local copies, waits for them, and re-layouts  20.4 us (3%)
    pallas_call x1, Pallas kernels, spread(): pl.pallas_call(spread_kernel, out_shape=outs, in_specs=[pl.BlockSpec(memo...  183 us
    pallas_call x1, Pallas kernels, fold(): pl.pallas_call(fold_kernel, out_shape=[jax.ShapeDtypeStruct(cot.shape, co...  161 us
    pallas_call x1, Pallas kernels, heads(): pl.pallas_call(partial(heads_kernel, packs, all_packs), grid=(all_packs +...  146 us
    pallas_call x1, Pallas kernels, row_work(): pl.pallas_call(rows_kernel, grid=(micro * per,), out_shape=[jax.ShapeDtyp...  76.2 us

profile of v3, /device:TPU:0, one launch (start us, length us, event | category | flops | bytes accessed | tf_op | source)
XLA Modules:
  0.0 627.8 jit_solution(12036628856974625667)
XLA Ops:
  0.7 0.7 constant_dynamic-update-slice_fusion.3
  1.3 0.7 constant_dynamic-update-slice_fusion.2
  2.0 0.7 constant_dynamic-update-slice_fusion.1
  2.7 0.7 constant_dynamic-update-slice_fusion
  3.4 0.8 reshape.180
  4.4 0.9 dynamic-update-slice.5
  5.9 182.9 %spread.1 = (bf16[2,2048,2048]{2,1,0:T(8,128)(2,1)}, bf16[2,2048,2048]{2,1,0:T(8,128)(2,1)}, bf16[3,2048,128]{2,1,0:T(8,128)(2,1)}, bf16[128,2048]{1,0:T(8,128)(...) custom-call(bf16[2,128,1024]{2,1,0:T(8,128)(2,1)} %tok.1, ...), custom_call_target="tpu_custom_call" | custom-call | tf_op jit(solution)/shard_map/spread/pallas_call | solution.py:814
  188.8 0.8 convert_bitcast_fusion.1
  192.4 76.2 %row_work.1 = (bf16[2,2048,2048]{2,1,0:T(8,128)(2,1)}, bf16[2,2048,512]{2,1,0:T(8,128)(2,1)}, bf16[2,2048,512]{2,1,0:T(8,128)(2,1)}, bf16[2,2048,512]{2,1,0:T(8,...) custom-call(bf16[2,2048,2048]{2,1,0:T(8,128)(2,1)} %get-tuple-element.3, ...), custom_call_target="tpu_custom_call" | custom-call | tf_op jit(solution)/shard_map/row_work/pallas_call | solution.py:1234
  269.6 1.5 convert_element_type.46.pos
  271.1 2.0 copy.41.seg_q
  274.2 2.0 copy.42.perm_c
  276.8 146.4 %heads.1 = (bf16[2,2048,512]{2,1,0:T(8,128)(2,1)}, bf16[128,2048]{1,0:T(8,128)(2,1)}, bf16[3,2048,128]{2,1,0:T(8,128)(2,1)}, f32[1,384]{1,0:T(1,128)}, bf16[1024...) custom-call(bf16[2,2048,512]{2,1,0:T(8,128)(2,1)} %get-tuple-element.48.four, s32[2,1,2048]{2,1,0:T(1,128)} %broadcast_in_dim.65.perm, ...), custom_call_target="tpu_custom_call" | custom-call | tf_op jit(solution)/shard_map/heads/pallas_call | solution.py:1426
  423.2 1.2 select_maximum_fusion.g_b
  425.0 161.1 %fold.1 = (bf16[2,128,1024]{2,1,0:T(8,128)(2,1)}, bf16[2,128,1024]{2,1,0:T(8,128)(2,1)}, f32[8,1024]{1,0:T(8,128)}, bf16[3,1024,1024]{2,1,0:T(8,128)(2,1)}, bf16...) custom-call(bf16[2,2048,512]{2,1,0:T(8,128)(2,1)} %get-tuple-element.46.activ, ...), custom_call_target="tpu_custom_call" | custom-call | tf_op jit(solution)/shard_map/fold/pallas_call | solution.py:1128
  586.1 9.1 %convert_bitcast_fusion = f32[1024,3,1024]{2,0,1:T(8,128)} fusion(bf16[3,1024,1024]{2,1,0:T(8,128)(2,1)} %get-tuple-element.60), kind=kLoop, calls=%fused_computation | loop fusion | flops 3145728 | bytes 18874368 | tf_op jit(solution)/shard_map/transpose | solution.py:1529
  595.2 11.8 %convert_element_type.49 = f32[1024,4096]{1,0:T(8,128)} convert(bf16[1024,4096]{1,0:T(8,128)(2,1)} %get-tuple-element.64) | non-fusion elementwise | flops 4194304 | bytes 25165824 | tf_op jit(solution)/shard_map/convert_element_type | solution.py:1533
  607.0 11.8 %convert_element_type.50 = f32[4096,1024]{1,0:T(8,128)} convert(bf16[4096,1024]{1,0:T(8,128)(2,1)} %get-tuple-element.65) | non-fusion elementwise | flops 4194304 | bytes 25165824 | tf_op jit(solution)/shard_map/convert_element_type | solution.py:1535
  618.9 2.5 convert_element_type.48
  621.4 1.0 slice.50
  622.4 0.7 constant_dynamic-slice_fusion.1
  623.7 1.4 fusion.5
  625.8 0.8 copy.64
  626.6 0.8 copy.65
  (49 shorter events, 8.3 us)
Async XLA Ops:
  192.4 76.2 %copy-start.5 = (s32[2,2,4]{2,1,0:T(2,128)S(1)}, s32[2,2,4]{2,1,0:T(2,128)}, u32[]{:S(2)}) copy-start(s32[2,2,4]{2,1,0:T(2,128)} %param.16) | copy-start | bytes 196
  269.0 5.2 copy-start.3
  276.8 146.4 %copy-start.6 = (f32[1,512]{1,0:T(1,128)S(1)}, f32[1,512]{1,0:T(1,128)}, u32[]{:S(2)}) copy-start(f32[1,512]{1,0:T(1,128)} %get-tuple-element.56) | copy-start | bytes 6148
  607.0 11.9 %copy-start = (bf16[1024,1024]{1,0:T(8,128)(2,1)S(1)}, bf16[1024,1024]{1,0:T(8,128)(2,1)}, u32[]{:S(2)}) copy-start(bf16[1024,1024]{1,0:T(8,128)(2,1)} %get-tuple-element.62) | copy-start | bytes 6291460
  618.9 6.3 %copy-start.7 = (f32[1,2048]{1,0:T(1,128)S(1)}, f32[1,2048]{1,0:T(1,128)}, u32[]{:S(2)}) copy-start(f32[1,2048]{1,0:T(1,128)} %get-tuple-element.63) | copy-start | bytes 24580
  618.9 6.9 %copy-start.2 = (bf16[2,128,1024]{2,1,0:T(8,128)(2,1)S(1)}, bf16[2,128,1024]{2,1,0:T(8,128)(2,1)}, u32[]{:S(2)}) copy-start(bf16[2,128,1024]{2,1,0:T(8,128)(2,1)} %get-tuple-element.109) | copy-start | bytes 1572868
  618.9 7.7 %copy-start.1 = (bf16[2,128,1024]{2,1,0:T(8,128)(2,1)S(1)}, bf16[2,128,1024]{2,1,0:T(8,128)(2,1)}, u32[]{:S(2)}) copy-start(bf16[2,128,1024]{2,1,0:T(8,128)(2,1)} %get-tuple-element.110) | copy-start | bytes 1572868
  625.2 2.2 copy-start.4

commit v4 on v3

--- a/solution.py
+++ b/solution.py
@@ -575,9 +575,27 @@
     pl.semaphore_wait(barrier, total)
 
 
+NN = (((1,), (0,)), ((), ()))
+NT = (((1,), (1,)), ((), ()))
+TN = (((0,), (0,)), ((), ()))
+
+
+def dot(a, b, dims=NN):
+    return lax.dot_general(a, b, dims, preferred_element_type=jnp.float32)
+
+
+ROOT = 0.7978845608028654
+CUBE = 0.044715
+GROUPS = tuple((dy, dx, j) for j in range(4) for dx in (0, 1) for dy in (0, 1))
+SMALL_ROWS = 80
+
+
 def spread_kernel(
-    tok, cot, w_q, w_d, w_1, w_2, small, tok_all, cot_all, q_out, d_out, o_1, o_2, small_out,
-    local_sem, send_sem, recv_sem,
+    tok, cot, w_q, w_d, w_1, w_2, small,
+    tok_all, cot_all, q_out, d_out, o_1, o_2, small_out, normed_out, activ_out, pre_out, four_out,
+    g_1, g_2, cot_sum, pre_sum,
+    v_q, v_d, v_1, v_2, v_s, acc_1, acc_2, tok_v, cot_v, normed_v, activ_v, pre_v, four_v,
+    local_sem, send_sem, recv_sem, in_sem, out_sem,
 ):
     y, h, l, x, t = place()
     z = 2 * h + l
@@ -597,13 +615,15 @@
     def number(key):
         return numbers.setdefault(key, len(numbers))
 
+    def group_at(dy, dx, zz):
+        yy = 1 - y if dy else y
+        xx = 1 - x if dx else x
+        return yy * 8 + zz * 2 + xx
+
     def region(unit, chunk, core):
         _, out, m, n = units[unit]
         dy, dx, way, k = chunk
-        yy = 1 - y if dy else y
-        xx = 1 - x if dx else x
-        zz = z - k if way == "up" else z + k
-        group = yy * 8 + zz * 2 + xx
+        group = group_at(dy, dx, z - k if way == "up" else z + k)
         return out.at[
             pl.ds(m, n),
             pl.ds(pl.multiple_of(group * rows, rows), rows),
@@ -616,31 +636,23 @@
 
     started = []
 
+    def link(unit, source, target, key, device):
+        i = number((unit,) + key)
+        return pltpu.make_async_remote_copy(
+            src_ref=source, dst_ref=target, send_sem=send_sem.at[i], recv_sem=recv_sem.at[i],
+            device_id=device, device_id_type=MESH,
+        )
+
     def send(unit, chunk, key, device):
         source = own(unit) if chunk == (0, 0, "up", 0) else region(unit, chunk, t)
-        i = number((unit,) + key)
-        copy = pltpu.make_async_remote_copy(
-            src_ref=source, dst_ref=region(unit, chunk, t), send_sem=send_sem.at[i],
-            recv_sem=recv_sem.at[i], device_id=device, device_id_type=MESH,
-        )
-        copy.start()
-        return copy
+        link(unit, source, region(unit, chunk, t), key, device).start()
 
     def arrive(unit, chunk, key, core):
-        i = number((unit,) + key)
         ref = region(unit, chunk, core)
-        pltpu.make_async_remote_copy(
-            src_ref=ref, dst_ref=ref, send_sem=send_sem.at[i], recv_sem=recv_sem.at[i],
-            device_id=other_t, device_id_type=MESH,
-        ).wait_recv()
-
-    def sent(unit, chunk, key):
-        i = number((unit,) + key)
-        ref = own(unit)
-        pltpu.make_async_remote_copy(
-            src_ref=ref, dst_ref=ref, send_sem=send_sem.at[i], recv_sem=recv_sem.at[i],
-            device_id=other_t, device_id_type=MESH,
-        ).wait_send()
+        link(unit, ref, ref, key, other_t).wait_recv()
+
+    def sent(unit, key):
+        link(unit, own(unit), own(unit), key, other_t).wait_send()
 
     def when(there, what):
         if there is True:
@@ -668,37 +680,129 @@
             can = z < 3 if going == "up" else z > 0
             key = (dy, dx, going, k + 1, "link")
             target = along(lax.min(z + 1, 3) if going == "up" else lax.max(z - 1, 0))
-            when(can, lambda: send(unit, chunk, key, target) and None)
+            when(can, lambda: send(unit, chunk, key, target))
             started.append((unit, chunk, key, going))
 
     def got(unit, chunk):
         arrive(unit, chunk, chunk + ("link",), t)
 
     steps = [[("up", 0)], [("up", 1), ("down", 1)], [("up", 2), ("down", 2)], [("up", 3), ("down", 3)]]
+
+    def z_step(s):
+        for u in (1, 2):
+            for way, k in steps[s]:
+                def act(u=u, c=(0, 0, way, k)):
+                    got(u, c)
+                    if c[3] < 3:
+                        up_down(u, c)
+                    onward(u, c, "x")
+                    onward(u, c, "y")
+                    to_core(u, c)
+                when(there_of(way, k), act)
+
+    def y_step(s):
+        for u in (1, 2):
+            for way, k in steps[s]:
+                def act(u=u, c=(1, 0, way, k)):
+                    got(u, c)
+                    onward(u, c, "x")
+                    to_core(u, c)
+                when(there_of(way, k), act)
+
+    def x_step(s, dy):
+        for u in (1, 2):
+            for way, k in steps[s]:
+                def act(u=u, c=(dy, 1, way, k)):
+                    got(u, c)
+                    to_core(u, c)
+                when(there_of(way, k), act)
+
+    def first_step(s):
+        for way, k in steps[s]:
+            def act(way=way, k=k):
+                for dy in (0, 1):
+                    for dx in (0, 1):
+                        c = (dy, dx, way, k)
+                        got(0, c)
+                        if k < 3:
+                            up_down(0, c)
+                        to_core(0, c)
+            when(there_of(way, k), act)
+
+    nearest = [
+        [(("up", 0), True)],
+        [(("up", 1), z > 0), (("down", 1), z == 0)],
+        [(("down", 2), z == 0), (("down", 1), (z == 1) | (z == 2)), (("up", 2), z == 3)],
+        [(("down", 3), z == 0), (("down", 2), z == 1), (("up", 2), z == 2), (("up", 3), z == 3)],
+    ]
+
+    def z_at(j):
+        if j == 0:
+            return z
+        options = [(0, 1, 2, 3), (1, 0, 2, 3), (2, 1, 3, 0), (3, 2, 1, 0)]
+        value = options[3][j]
+        for zz in (2, 1, 0):
+            value = jnp.where(z == zz, options[zz][j], value)
+        return value
+
+    def loads(group, slot):
+        there = pl.ds(pl.multiple_of(group * rows, rows), rows)
+        copies = []
+        for m in range(2):
+            for n, (source, target) in enumerate(((tok_all, tok_v), (cot_all, cot_v))):
+                copies.append(
+                    pltpu.make_async_copy(
+                        source.at[m, there], target.at[slot, pl.ds(m * rows, rows)], in_sem.at[slot, 2 * m + n]
+                    )
+                )
+        return copies
+
+    def stores(group, slot):
+        there = pl.ds(pl.multiple_of(group * rows, rows), rows)
+        pairs = ((normed_v, normed_out), (activ_v, activ_out), (pre_v, pre_out), (four_v, four_out))
+        return [
+            pltpu.make_async_copy(
+                source.at[slot, pl.ds(m * rows, rows)], target.at[m, there], out_sem.at[slot, 4 * m + n]
+            )
+            for m in range(2)
+            for n, (source, target) in enumerate(pairs)
+        ]
+
+    def fetch(i):
+        dy, dx, j = GROUPS[i]
+        for (way, k), there in nearest[j]:
+            def wait(way=way, k=k):
+                for u in range(3):
+                    c = (dy, dx, way, k)
+                    arrive(u, c, c + ("core",), 1 - t)
+            when(there, wait)
+        for copy in loads(group_at(dy, dx, z_at(j)), i % 2):
+            copy.start()
+
     block = (y * 4 + l * 2 + x, (1 - y) * 4 + l * 2 + x)
-    pieces = []
     depth = w_1.shape[0]
-    for b, to in ((block[1], True), (block[0], False)):
-        row = pl.ds(pl.multiple_of(y * depth, depth), depth)
-        wide, narrow = w_1.shape[1] // 8, w_d.shape[0] // 8
-        pieces.append([
-            (w_1.at[:, pl.ds(pl.multiple_of(b * wide, wide), wide)], o_1.at[row]),
-            (w_2.at[pl.ds(pl.multiple_of(b * wide, wide), wide)], o_2.at[:, row]),
-            (w_q.at[:, :, pl.ds(pl.multiple_of(b * narrow, narrow), narrow)], q_out.at[:, row]),
-            (w_d.at[pl.ds(pl.multiple_of(b * narrow, narrow), narrow)], d_out.at[:, row]),
+    wide, narrow = w_1.shape[1] // 8, w_d.shape[0] // 8
+    row = pl.ds(pl.multiple_of(y * depth, depth), depth)
+
+    def pieces(b):
+        w = pl.ds(pl.multiple_of(b * wide, wide), wide)
+        n = pl.ds(pl.multiple_of(b * narrow, narrow), narrow)
+        return [
             (small, small_out.at[y]),
-        ])
-    locals_, weights = [], []
+            (w_1.at[:, w], o_1.at[row]),
+            (w_2.at[w], o_2.at[:, row]),
+            (w_q.at[:, :, n], q_out.at[:, row]),
+            (w_d.at[n], d_out.at[:, row]),
+        ]
+
     first = (0, 0, "up", 0)
-    for u in range(3):
-        up_down(u, first) if u else None
+    for u in (1, 2):
+        up_down(u, first)
     for u in range(3):
         onward(u, first, "y")
-    for i, (source, target) in enumerate(pieces[0]):
-        copy = pltpu.make_async_remote_copy(
-            src_ref=source, dst_ref=target, send_sem=send_sem.at[number(("w", i))],
-            recv_sem=recv_sem.at[number(("w", i))], device_id=other_y, device_id_type=MESH,
-        )
+    weights, locals_ = [], []
+    for i, (source, target) in enumerate(pieces(block[1])):
+        copy = link("w", source, target, (i,), other_y)
         copy.start()
         weights.append(copy)
     for u in range(3):
@@ -707,121 +811,169 @@
         copy = pltpu.make_async_copy(own(u), region(u, first, t), local_sem.at[len(locals_)])
         copy.start()
         locals_.append(copy)
-    for source, target in pieces[1]:
+    for source, target in pieces(block[0]):
         copy = pltpu.make_async_copy(source, target, local_sem.at[len(locals_)])
         copy.start()
         locals_.append(copy)
-
+    acc_1[...] = jnp.zeros_like(acc_1)
+    acc_2[...] = jnp.zeros_like(acc_2)
+    cot_sum[...] = jnp.zeros_like(cot_sum)
+    pre_sum[...] = jnp.zeros_like(pre_sum)
     got(0, (1, 0, "up", 0))
     onward(0, (1, 0, "up", 0), "x")
     up_down(0, first)
     up_down(0, (1, 0, "up", 0))
     to_core(0, (1, 0, "up", 0))
-
-    def rest_of_first():
-        for dy in (0, 1):
-            got(0, (dy, 1, "up", 0))
-            up_down(0, (dy, 1, "up", 0))
-            to_core(0, (dy, 1, "up", 0))
-
-    def z_step(s):
-        for u in (1, 2):
-            for way, k in steps[s]:
-                def act(u=u, c=(0, 0, way, k)):
-                    got(u, c)
-                    up_down(u, c) if c[3] < 3 else None
-                    onward(u, c, "y")
-                    onward(u, c, "x")
-                    to_core(u, c)
-                when(there_of(way, k), act)
-
-    def y_step(s):
-        for u in (1, 2):
-            for way, k in steps[s]:
-                def act(u=u, c=(1, 0, way, k)):
-                    got(u, c)
-                    onward(u, c, "x")
-                    to_core(u, c)
-                when(there_of(way, k), act)
-
-    def x_step(s):
-        for u in (1, 2):
-            for way, k in steps[s]:
-                def act(u=u, way=way, k=k):
-                    for dy in (0, 1):
-                        got(u, (dy, 1, way, k))
-                        to_core(u, (dy, 1, way, k))
-                when(there_of(way, k), act)
-
-    def first_step(s):
-        for way, k in steps[s]:
-            def act(way=way, k=k):
-                for dy in (0, 1):
-                    for dx in (0, 1):
-                        c = (dy, dx, way, k)
-                        got(0, c)
-                        up_down(0, c) if k < 3 else None
-                        to_core(0, c)
-            when(there_of(way, k), act)
-
     z_step(1)
-    rest_of_first()
-    y_step(0)
-    z_step(2)
-    y_step(1)
-    x_step(0)
-    first_step(1)
-    z_step(3)
-    y_step(2)
-    x_step(1)
-    first_step(2)
-    y_step(3)
-    x_step(2)
-    first_step(3)
-    x_step(3)
-    for u in range(3):
-        for dy in (0, 1):
-            for dx in (0, 1):
-                for s in range(4):
-                    for way, k in steps[s]:
-                        c = (dy, dx, way, k)
-                        when(there_of(way, k), lambda: arrive(u, c, c + ("core",), 1 - t))
+    for dy in (0, 1):
+        got(0, (dy, 1, "up", 0))
+        up_down(0, (dy, 1, "up", 0))
+        to_core(0, (dy, 1, "up", 0))
+    for event in ((y_step, 0), (z_step, 2), (y_step, 1), (x_step, 0, 0), (x_step, 0, 1)):
+        event[0](*event[1:])
     for copy in locals_:
         copy.wait()
+    fetch(0)
     for copy in weights:
+        copy.wait_recv()
+    into = []
+    for n, (source, target) in enumerate(
+        ((q_out, v_q), (d_out, v_d), (o_1, v_1), (o_2, v_2), (small_out, v_s))
+    ):
+        copy = pltpu.make_async_copy(source, target, local_sem.at[n])
+        copy.start()
+        into.append(copy)
+    for copy in into:
         copy.wait()
+    both = v_s[...].astype(jnp.float32)
+
+    def line(at):
+        n = half // 128
+        return jnp.concatenate([both[yy, at + r : at + r + 1, :] for yy in range(2) for r in range(n)], axis=1)
+
+    gain, shift = line(0), line(half // 128)
+    summed = both[0] + both[1]
+    base = 4 * half // 128
+    index = lax.broadcasted_iota(jnp.int32, summed.shape, 0)
+
+    def pick(values, at):
+        return jnp.sum(jnp.where(index == at, values, 0.0), axis=0, keepdims=True)
+
+    q_shift = [pick(summed, base + c * 8 + block[0]) for c in range(3)]
+    f_shift = jnp.concatenate(
+        [pick(both[yy], base + 24 + 2 * block[0] + r) for r in range(2) for yy in range(2)], axis=1
+    )
+    events = {
+        0: [(first_step, 1)],
+        1: [(z_step, 3)],
+        2: [(y_step, 2)],
+        3: [(x_step, 1, 0)],
+        4: [(x_step, 1, 1)],
+        5: [(first_step, 2)],
+        7: [(y_step, 3)],
+        8: [(x_step, 2, 0), (x_step, 2, 1)],
+        10: [(first_step, 3)],
+        12: [(x_step, 3, 0)],
+        14: [(x_step, 3, 1)],
+    }
+    count = len(GROUPS)
+
+    def chosen(step):
+        value = group_at(*GROUPS[-1][:2], z_at(GROUPS[-1][2]))
+        for i in range(count - 1):
+            dy, dx, j = GROUPS[i]
+            value = jnp.where(step == i, group_at(dy, dx, z_at(j)), value)
+        return value
+
+    f32, bf16 = jnp.float32, jnp.bfloat16
+
+    def work(step, carry):
+        slot = lax.rem(step, 2)
+        for i in range(count - 1):
+
+            @pl.when(step == i)
+            def _(i=i):
+                for event in events.get(i, []):
+                    event[0](*event[1:])
+                fetch(i + 1)
+
+        group = chosen(step)
+        for copy in loads(group, slot):
+            copy.wait()
+
+        @pl.when(step >= 2)
+        def _():
+            for copy in stores(chosen(step - 2), slot):
+                copy.wait()
+
+        values = tok_v[slot].astype(f32)
+        center = values - jnp.mean(values, axis=1, keepdims=True)
+        r = lax.rsqrt(jnp.mean(center * center, axis=1, keepdims=True) + EPSILON)
+        normed = (center * r * gain + shift).astype(bf16)
+        normed_v[slot] = normed
+        cots = cot_v[slot]
+        pre = dot(normed, v_1[...]) + f_shift
+        square = pre * pre
+        curve = jnp.tanh(ROOT * (pre + CUBE * pre * square))
+        activ = (0.5 * pre * (1.0 + curve)).astype(bf16)
+        slope = 0.5 * (1.0 + curve) + 0.5 * pre * (1.0 - curve * curve) * (ROOT * (1.0 + 3.0 * CUBE * square))
+        grad_pre = (dot(cots, v_2[...], NT) * slope).astype(bf16)
+        activ_v[slot] = activ
+        pre_v[slot] = grad_pre
+        for c in range(3):
+            at = slice(c * narrow, (c + 1) * narrow)
+            four_v[slot, :, at] = (dot(normed, v_q[c]) + q_shift[c]).astype(bf16)
+        four_v[slot, :, 3 * narrow :] = dot(cots, v_d[...], NT).astype(bf16)
+        acc_1[...] += dot(normed, grad_pre, TN)
+        acc_2[...] += dot(activ, cots, TN)
+        cot_sum[...] += jnp.sum(cots.astype(f32), axis=0, keepdims=True)
+        pre_sum[...] += jnp.sum(grad_pre.astype(f32), axis=0, keepdims=True)
+        for copy in stores(group, slot):
+            copy.start()
+        return carry
+
+    lax.fori_loop(0, count, work, 0)
+    g_1[...] = acc_1[...].astype(bf16)
+    g_2[...] = acc_2[...].astype(bf16)
+    for i in (count - 2, count - 1):
+        dy, dx, j = GROUPS[i]
+        for copy in stores(group_at(dy, dx, z_at(j)), i % 2):
+            copy.wait()
+    for copy in weights:
+        copy.wait_send()
     for unit, chunk, key, going in started:
         there = there_of(*chunk[2:])
         if going is not None:
             can = z < 3 if going == "up" else z > 0
             there = can if there is True else can & there
-        when(there, lambda: sent(unit, chunk, key))
+        when(there, lambda: sent(unit, key))
 
 
 def spread(tokens, cotangent, w_q, w_d, w_1, w_2, small):
     micro, rows, half = tokens.shape
-    everything = jax.ShapeDtypeStruct((micro, rows * 16, half * 2), tokens.dtype)
-    depth = w_1.shape[0] * 2
-    outs = [
-        everything,
-        everything,
-        jax.ShapeDtypeStruct((3, depth, w_q.shape[2] // 8), w_q.dtype),
-        jax.ShapeDtypeStruct((w_d.shape[0] // 8, depth), w_d.dtype),
-        jax.ShapeDtypeStruct((depth, w_1.shape[1] // 8), w_1.dtype),
-        jax.ShapeDtypeStruct((w_2.shape[0] // 8, depth), w_2.dtype),
-        jax.ShapeDtypeStruct((2,) + small.shape, small.dtype),
-    ]
+    total, deep = rows * 16, half * 2
+    wide, narrow = w_1.shape[1] // 8, w_d.shape[0] // 8
+    bf16, f32 = jnp.bfloat16, jnp.float32
+    shape = jax.ShapeDtypeStruct
+    weights = [(3, deep, narrow), (narrow, deep), (deep, wide), (wide, deep), (2,) + small.shape]
+    outs = [(micro, total, deep)] * 2 + weights
+    outs += [(micro, total, deep), (micro, total, wide), (micro, total, wide), (micro, total, 4 * narrow)]
+    both = micro * rows
+    any_, vmem = pl.BlockSpec(memory_space=pl.ANY), pl.BlockSpec(memory_space=pltpu.VMEM)
+    sem = pltpu.SemaphoreType.DMA
     return pl.pallas_call(
         spread_kernel,
-        out_shape=outs,
-        in_specs=[pl.BlockSpec(memory_space=pl.ANY)] * 7,
-        out_specs=[pl.BlockSpec(memory_space=pl.ANY)] * 7,
-        scratch_shapes=[
-            pltpu.SemaphoreType.DMA((8,)),
-            pltpu.SemaphoreType.DMA((176,)),
-            pltpu.SemaphoreType.DMA((176,)),
-        ],
-        compiler_params=pltpu.CompilerParams(collective_id=0, has_side_effects=True),
+        out_shape=[shape(s, bf16) for s in outs + [(deep, wide), (wide, deep)]]
+        + [shape((1, deep), f32), shape((1, wide), f32)],
+        in_specs=[any_] * 7,
+        out_specs=[any_] * len(outs) + [vmem] * 4,
+        scratch_shapes=[pltpu.VMEM(s, bf16) for s in weights]
+        + [pltpu.VMEM((deep, wide), f32), pltpu.VMEM((wide, deep), f32)]
+        + [pltpu.VMEM((2, both, w), bf16) for w in (deep, deep, deep, wide, wide, 4 * narrow)]
+        + [sem((8,)), sem((176,)), sem((176,)), sem((2, 4)), sem((2, 8))],
+        compiler_params=pltpu.CompilerParams(
+            collective_id=0, has_side_effects=True, vmem_limit_bytes=56 << 20
+        ),
         name="spread",
     )(tokens, cotangent, w_q, w_d, w_1, w_2, small)
 
@@ -919,15 +1071,6 @@
 def join_sems(count):
     sem = pltpu.SemaphoreType.DMA
     return [sem((count,)), sem((7 * count,)), sem((7 * count,))]
-
-
-NN = (((1,), (0,)), ((), ()))
-NT = (((1,), (1,)), ((), ()))
-TN = (((0,), (0,)), ((), ()))
-
-
-def dot(a, b, dims=NN):
-    return lax.dot_general(a, b, dims, preferred_element_type=jnp.float32)
 
 
 def fold_kernel(
@@ -1164,95 +1307,6 @@
         ),
         name="fold",
     )(activ, grad_pre, back, tok_all, g_q, g_d, g_b, cot, w_1, w_2, w_q, w_d, gain, out_shift)
-
-
-ROOT = 0.7978845608028654
-CUBE = 0.044715
-
-
-def rows_kernel(
-    tok, cot, w_1, w_2, w_q, w_d, gain, shift, f_shift, q_shift,
-    normed_out, activ_out, pre_out, four_out, g_1, g_2, cot_sum, pre_sum, acc_1, acc_2,
-):
-    step = pl.program_id(0)
-
-    @pl.when(step == 0)
-    def _():
-        acc_1[...] = jnp.zeros_like(acc_1)
-        acc_2[...] = jnp.zeros_like(acc_2)
-        cot_sum[...] = jnp.zeros_like(cot_sum)
-        pre_sum[...] = jnp.zeros_like(pre_sum)
-
-    f32, bf16 = jnp.float32, jnp.bfloat16
-    values = tok[0].astype(f32)
-    center = values - jnp.mean(values, axis=1, keepdims=True)
-    r = lax.rsqrt(jnp.mean(center * center, axis=1, keepdims=True) + EPSILON)
-    normed = (center * r * gain[...] + shift[...]).astype(bf16)
-    normed_out[0] = normed
-    cots = cot[0]
-    pre = dot(normed, w_1[...]) + f_shift[...]
-    square = pre * pre
-    curve = jnp.tanh(ROOT * (pre + CUBE * pre * square))
-    activ = (0.5 * pre * (1.0 + curve)).astype(bf16)
-    slope = 0.5 * (1.0 + curve) + 0.5 * pre * (1.0 - curve * curve) * (ROOT * (1.0 + 3.0 * CUBE * square))
-    grad_pre = (dot(cots, w_2[...], NT) * slope).astype(bf16)
-    activ_out[0] = activ
-    pre_out[0] = grad_pre
-    narrow = w_d.shape[0]
-    for c in range(3):
-        at = slice(c * narrow, (c + 1) * narrow)
-        four_out[0, :, at] = (dot(normed, w_q[c]) + q_shift[:, at]).astype(bf16)
-    four_out[0, :, 3 * narrow :] = dot(cots, w_d[...], NT).astype(bf16)
-    acc_1[...] += dot(normed, grad_pre, TN)
-    acc_2[...] += dot(activ, cots, TN)
-    cot_sum[...] += jnp.sum(cots.astype(f32), axis=0, keepdims=True)
-    pre_sum[...] += jnp.sum(grad_pre.astype(f32), axis=0, keepdims=True)
-
-    @pl.when(step == pl.num_programs(0) - 1)
-    def _():
-        g_1[...] = acc_1[...].astype(bf16)
-        g_2[...] = acc_2[...].astype(bf16)
-
-
-def row_work(tok_all, cot_all, w_1, w_2, w_q, w_d, gain, shift, f_shift, q_shift, size):
-    micro, total, width = tok_all.shape
-    per = total // size
-    wide = w_1.shape[1]
-    narrow = w_d.shape[0]
-    bf16, f32 = jnp.bfloat16, jnp.float32
-
-    def block(w):
-        return pl.BlockSpec((1, size, w), lambda i: (i // per, i % per, 0))
-
-    def whole(a):
-        return pl.BlockSpec(a.shape, lambda i: (0,) * len(a.shape), pipeline_mode=pl.Buffered(1))
-
-    def fixed(*s):
-        return pl.BlockSpec(s, lambda i: (0,) * len(s))
-
-    consts = (w_1, w_2, w_q, w_d, gain, shift, f_shift, q_shift)
-    return pl.pallas_call(
-        rows_kernel,
-        grid=(micro * per,),
-        out_shape=[
-            jax.ShapeDtypeStruct(tok_all.shape, bf16),
-            jax.ShapeDtypeStruct((micro, total, wide), bf16),
-            jax.ShapeDtypeStruct((micro, total, wide), bf16),
-            jax.ShapeDtypeStruct((micro, total, 4 * narrow), bf16),
-            jax.ShapeDtypeStruct(w_1.shape, bf16),
-            jax.ShapeDtypeStruct(w_2.shape, bf16),
-            jax.ShapeDtypeStruct((1, width), f32),
-            jax.ShapeDtypeStruct((1, wide), f32),
-        ],
-        in_specs=[block(width), block(width)] + [whole(a) for a in consts],
-        out_specs=[
-            block(width), block(wide), block(wide), block(4 * narrow),
-            fixed(*w_1.shape), fixed(*w_2.shape), fixed(1, width), fixed(1, wide),
-        ],
-        scratch_shapes=[pltpu.VMEM(w_1.shape, f32), pltpu.VMEM(w_2.shape, f32)],
-        compiler_params=pltpu.CompilerParams(vmem_limit_bytes=60 << 20),
-        name="row_work",
-    )(tok_all, cot_all, *consts)
 
 
 def swap_rotary(values):
@@ -1479,34 +1533,25 @@
     total = rows * 16
     pack_rows = rows * 8
     packs = total // pack_rows
-    block = y * 4 + l * 2 + x
-    wide = fc1_weight.shape[1] // 8
     narrow = dense_weight.shape[0] // 8
-    small = jnp.concatenate(
-        [a.reshape(-1) for a in (ln_gain, ln_bias, dense_bias, fc2_bias, qkv_bias, fc1_bias)]
-    )
-    small = jnp.pad(small, (0, 64 * 128 - small.shape[0])).reshape(64, 128)
-    tok_all, cot_all, w_q, w_d, w_1, w_2, small = spread(
+    flat = jnp.concatenate([a.reshape(-1, 128) for a in (ln_gain, ln_bias, dense_bias, fc2_bias)])
+    turned = qkv_bias.reshape(24, 2, 1, qkv_bias.shape[2])
+    at_y = jnp.arange(2)[None, None, :, None] == y
+    turned = jnp.where(at_y, turned, jnp.zeros_like(turned)).reshape(24, 128)
+    small = jnp.concatenate([flat, turned, fc1_bias])
+    small = jnp.pad(small, ((0, SMALL_ROWS - small.shape[0]), (0, 0)))
+    (
+        tok_all, cot_all, w_q, w_d, w_1, w_2, small, normed, activ, grad_pre, four, g_w1, g_w2, cot_sum, pre_sum,
+    ) = spread(
         tokens, cotangent, qkv_weight.transpose(1, 0, 2), dense_weight, fc1_weight, fc2_weight, small
     )
-    small = small.reshape(2, 64 * 128).astype(f32)
+    small = small.reshape(2, -1).astype(f32)
     gain = small[:, 0:share].reshape(1, width)
-    shift = small[:, share : 2 * share].reshape(1, width)
     out_shift = (small[:, 2 * share : 3 * share] + small[:, 3 * share : 4 * share]).reshape(1, width)
-    at = 4 * share
-    q_shift = small[:, at : at + qkv_bias.size].reshape((2,) + qkv_bias.shape)
-    q_shift = q_shift.transpose(1, 2, 0, 3).reshape(3, -1)
-    at += qkv_bias.size
-    f_shift = small[:, at : at + fc1_bias.size].reshape((2,) + fc1_bias.shape).transpose(1, 0, 2).reshape(-1)
-    q_shift = lax.dynamic_slice_in_dim(q_shift, block * narrow, narrow, 1).reshape(1, -1)
-    f_shift = lax.dynamic_slice_in_dim(f_shift, block * wide, wide, 0).reshape(1, -1)
 
     places = jnp.arange(pack_rows, dtype=jnp.int32)
     segment, position = jax.vmap(lambda row: segment_layout(row, places))(
         lengths.reshape(micro * packs, -1)
-    )
-    normed, activ, grad_pre, four, g_w1, g_w2, cot_sum, pre_sum = row_work(
-        tok_all, cot_all, w_1, w_2, w_q, w_d, gain, shift, f_shift, q_shift, 4 * rows
     )
     back, g_wd, g_wq, qkv_sum, j_1, j_2 = heads(
         four, permutation, segment, position, normed, cot_all, g_w1, g_w2, packs, 4 * rows

time: 638 us -> 595 us (0.933)
  Pallas kernels: 567 us -> 526 us
    pallas_call x2 -> x1, Pallas kernels: 259 us -> 218 us  [spread(): pl.pallas_call(spread_kernel, out_shape=[shape(s, bf16) for s in outs + [...]
where the time goes in v4:
time: 595 us; the launch traced here: 587 us
  Pallas kernels  526 us (88%)
  other arithmetic  40.1 us (7%)
  local copies, waits for them, and re-layouts  19.5 us (3%)
    pallas_call x1, Pallas kernels, spread(): pl.pallas_call(spread_kernel, out_shape=[shape(s, bf16) for s in outs + [...  218 us
    pallas_call x1, Pallas kernels, fold(): pl.pallas_call(fold_kernel, out_shape=[jax.ShapeDtypeStruct(cot.shape, co...  165 us
    pallas_call x1, Pallas kernels, heads(): pl.pallas_call(partial(heads_kernel, packs, all_packs), grid=(all_packs +...  143 us

profile of v4, /device:TPU:0, one launch (start us, length us, event | category | flops | bytes accessed | tf_op | source)
XLA Modules:
  0.0 587.0 jit_solution(4928870068928878390)
XLA Ops:
  1.4 0.8 select_reduce_fusion.1
  2.2 0.7 sub.23
  3.7 1.3 broadcast_in_dim.106.perm
  5.8 0.7 constant_dynamic-update-slice_fusion.4
  6.5 0.7 constant_dynamic-update-slice_fusion.3
  7.8 0.7 broadcast_in_dim.103
  8.7 0.7 constant_dynamic-update-slice_fusion
  10.6 1.5 convert_element_type.44.pos
  12.1 2.0 copy.36.seg_q
  14.0 2.0 copy.37.perm_c
  16.0 218.0 %spread.1 = (bf16[2,2048,2048]{2,1,0:T(8,128)(2,1)}, bf16[2,2048,2048]{2,1,0:T(8,128)(2,1)}, bf16[3,2048,128]{2,1,0:T(8,128)(2,1)}, bf16[128,2048]{1,0:T(8,128)(...) custom-call(bf16[2,128,1024]{2,1,0:T(8,128)(2,1)} %tok.1, ...), custom_call_target="tpu_custom_call" | custom-call | tf_op jit(solution)/shard_map/spread/pallas_call | solution.py:964
  234.0 0.7 constant_dynamic-slice_fusion
  234.7 0.8 convert_bitcast_fusion.1
  236.8 143.2 %heads.1 = (bf16[2,2048,512]{2,1,0:T(8,128)(2,1)}, bf16[128,2048]{1,0:T(8,128)(2,1)}, bf16[3,2048,128]{2,1,0:T(8,128)(2,1)}, f32[1,384]{1,0:T(1,128)}, bf16[1024...) custom-call(bf16[2,2048,512]{2,1,0:T(8,128)(2,1)} %get-tuple-element.41.four, s32[2,1,2048]{2,1,0:T(1,128)} %broadcast_in_dim.106.perm, ...), custom_call_target="tpu_custom_call" | custom-call | tf_op jit(solution)/shard_map/heads/pallas_call | solution.py:1480
  380.0 1.3 select_maximum_fusion.g_b
  381.2 165.2 %fold.1 = (bf16[2,128,1024]{2,1,0:T(8,128)(2,1)}, bf16[2,128,1024]{2,1,0:T(8,128)(2,1)}, f32[8,1024]{1,0:T(8,128)}, bf16[3,1024,1024]{2,1,0:T(8,128)(2,1)}, bf16...) custom-call(bf16[2,2048,512]{2,1,0:T(8,128)(2,1)} %get-tuple-element.39.activ, ...), custom_call_target="tpu_custom_call" | custom-call | tf_op jit(solution)/shard_map/fold/pallas_call | solution.py:1271
  546.5 1.4 fusion.5
  547.9 1.0 slice.35
  550.3 4.4 convert_element_type.48
  554.7 6.3 %convert_bitcast_fusion = f32[1024,3,1024]{2,0,1:T(8,128)} fusion(bf16[3,1024,1024]{2,1,0:T(8,128)(2,1)S(1)} %copy-done), kind=kLoop, calls=%fused_computation | loop fusion | flops 3145728 | bytes 18874368 | tf_op jit(solution)/shard_map/transpose | solution.py:1574
  561.0 11.8 %convert_element_type.49 = f32[1024,4096]{1,0:T(8,128)} convert(bf16[1024,4096]{1,0:T(8,128)(2,1)} %get-tuple-element.64) | non-fusion elementwise | flops 4194304 | bytes 25165824 | tf_op jit(solution)/shard_map/convert_element_type | solution.py:1578
  572.8 11.8 %convert_element_type.50 = f32[4096,1024]{1,0:T(8,128)} convert(bf16[4096,1024]{1,0:T(8,128)(2,1)} %get-tuple-element.65) | non-fusion elementwise | flops 4194304 | bytes 25165824 | tf_op jit(solution)/shard_map/convert_element_type | solution.py:1580
  585.2 0.8 copy.55
  586.0 0.8 copy.56
  (39 shorter events, 7.5 us)
Async XLA Ops:
  10.0 4.1 copy-start.3
  234.7 349.9 %copy-start.4 = (f32[1,1024]{1,0:T(1,128)}, f32[1,1024]{1,0:T(1,128)S(1)}, u32[]{:S(2)}) copy-start(f32[1,1024]{1,0:T(1,128)S(1)} %constant_dynamic-slice_fusion) | copy-start | bytes 12292
  236.8 143.2 %copy-start.5 = (f32[1,512]{1,0:T(1,128)S(1)}, f32[1,512]{1,0:T(1,128)}, u32[]{:S(2)}) copy-start(f32[1,512]{1,0:T(1,128)} %get-tuple-element.51) | copy-start | bytes 6148
  549.6 5.1 copy-start
  572.8 12.4 %copy-start.2 = (bf16[2,128,1024]{2,1,0:T(8,128)(2,1)S(1)}, bf16[2,128,1024]{2,1,0:T(8,128)(2,1)}, u32[]{:S(2)}) copy-start(bf16[2,128,1024]{2,1,0:T(8,128)(2,1)} %get-tuple-element.108) | copy-start | bytes 1572868
  572.8 13.2 %copy-start.1 = (bf16[2,128,1024]{2,1,0:T(8,128)(2,1)S(1)}, bf16[2,128,1024]{2,1,0:T(8,128)(2,1)}, u32[]{:S(2)}) copy-start(bf16[2,128,1024]{2,1,0:T(8,128)(2,1)} %get-tuple-element.109) | copy-start | bytes 1572868

commit v5 on v4

--- a/solution.py
+++ b/solution.py
@@ -588,6 +588,7 @@
 CUBE = 0.044715
 GROUPS = tuple((dy, dx, j) for j in range(4) for dx in (0, 1) for dy in (0, 1))
 SMALL_ROWS = 80
+SEQUENCES = 4
 
 
 def spread_kernel(
@@ -984,7 +985,7 @@
         self.local_sem, self.send_sem, self.recv_sem = local_sem, send_sem, recv_sem
         self.y, self.h, self.l, self.x, self.t = place()
         self.device = {"y": {"y": 1 - self.y}, "l": {"l": 1 - self.l}, "x": {"x": 1 - self.x}}
-        self.numbers, self.sends = {}, []
+        self.numbers, self.sends, self.met = {}, [], set()
         self.every = range(len(parts))
         self.first = [p[3] for p in parts]
         self.then = ["l" if p[3] == "x" else "x" for p in parts]
@@ -1043,19 +1044,23 @@
         for i in self.every:
             self.kept(i).start()
 
-    def far(self, side):
+    def far(self, side, axis=None):
         yy = 1 - self.y if side else self.y
         for i in self.every:
+            if axis not in (None, self.then[i]):
+                continue
             a = self.first[i]
             self.got(i, self.beside(i, a, yy), (side, a))
             self.send(i, self.beside(i, a, yy), self.beside(i, a, yy), (side, "far"), self.then[i])
 
-    def brought(self):
-        for i in self.every:
-            ref = self.own(i, 1 - self.y)
-            self.got(i, ref, ("y",))
-            self.send(i, ref, ref, (1, self.first[i]), self.first[i])
-            self.send(i, ref, ref, (1, self.then[i]), self.then[i])
+    def brought(self, *axes):
+        for n, axis in enumerate(axes):
+            for i in self.every:
+                ref = self.own(i, 1 - self.y)
+                if (i, "y") not in self.met:
+                    self.met.add((i, "y"))
+                    self.got(i, ref, ("y",))
+                self.send(i, ref, ref, (1, axis), axis)
 
     def end(self):
         for i in self.every:
@@ -1096,7 +1101,7 @@
         xx = 1 - x if dx else x
         return pl.ds(pl.multiple_of((yy * 8 + h * 4 + ll * 2 + xx) * rows, rows), rows)
 
-    owners = [(1, 1, 0), (1, 1, 1), (0, 1, 0), (0, 1, 1), (1, 0, 0), (1, 0, 1), (0, 0, 1), (0, 0, 0)]
+    owners = [(1, 1, 1), (1, 1, 0), (1, 0, 1), (1, 0, 0), (0, 1, 1), (0, 1, 0), (0, 0, 1), (0, 0, 0)]
     arrived = {}
     for o, owner in enumerate(owners):
         start = len(loads)
@@ -1111,10 +1116,12 @@
         load(tok_all.at[m, group_rows(0, 0, 0)], tok_v.at[pl.ds(m * rows, rows)])
     tok_loads = loads[start:]
     greet([(device[a], True) for a in ("t", "x", "y", "l", "h")])
-    parts = [(g_q, 1, 2, "x"), (g_d, 1, 0, "l"), (g_b, None, 0, "l")]
-    gather = Join(parts, (j_q, j_d, j_b), *join_sem)
+    two, three = pl.ds(0, 2), pl.ds(2, 1)
+    parts = [(g_q.at[two], 1, 2, "x"), (g_q.at[three], 1, 2, "l"), (g_d, 1, 0, "l"), (g_b, None, 0, "l")]
+    gather = Join(parts, (j_q.at[two], j_q.at[three], j_d, j_b), *join_sem)
     gather.bring()
     gather.offer("x")
+    gather.offer("l")
     gather.keep()
 
     def part(a, o, tt):
@@ -1140,7 +1147,7 @@
         )
         core[i].start()
 
-    hops = {0: ("l", "y", "x"), 1: ("y", "x", "l")}
+    hops = {0: ("y", "l", "x"), 1: ("y", "x", "l")}
     place_of = {"y": 0, "l": 1, "x": 2}
     slots, passed = {}, {}
 
@@ -1158,11 +1165,6 @@
             total += sum_in[n].astype(jnp.float32)
         return total
 
-    def stage_owners(a, stage):
-        done = [place_of[d] for d in hops[a][:stage]]
-        now = place_of[hops[a][stage]]
-        return [o for o, w in enumerate(owners) if all(w[d] == 0 for d in done) and w[now] == 1]
-
     def pass_on(a, o, stage):
         axis = hops[a][stage]
         seen = list(owners[o])
@@ -1175,28 +1177,22 @@
         )
         passed[n].start()
 
-    order = []
-    for stage in range(3):
-        for pair in zip(stage_owners(0, stage), stage_owners(1, stage)):
-            order += [(a, o, stage) for a, o in enumerate(pair)]
-    ahead = 2
-    queue = [(a, o) for a, o, _ in order] + [(0, 7), (1, 7)]
-    for a, o in queue[:ahead]:
+    queue = [(1, 0), (1, 2), (1, 1), (1, 3), (0, 0), (0, 1), (0, 2), (0, 3)]
+    for a, o in queue[:2]:
         offer(a, o)
-    for i, (a, o, stage) in enumerate(order):
-        if stage == 0:
-            offer(*queue[i + ahead])
-            pass_on(a, o, stage)
-            if i == 7:
-                gather.offer("l")
-                for item in queue[i + ahead + 1 :]:
-                    offer(*item)
-                gather.far(0)
-                gather.brought()
-        else:
-            pass_on(a, o, stage)
-            if i == 11:
-                gather.far(1)
+    for i, (a, o) in enumerate(queue):
+        if i + 2 < len(queue):
+            offer(*queue[i + 2])
+        pass_on(a, o, 0)
+    gather.brought("x", "l")
+    for a, o in [(1, 4), (1, 6), (1, 5), (1, 7), (0, 4), (0, 5), (0, 6), (0, 7)]:
+        offer(a, o)
+    pass_on(1, 4, 1)
+    pass_on(1, 6, 1)
+    gather.far(0, "x")
+    gather.far(0, "l")
+    pass_on(1, 5, 2)
+    gather.far(1)
     for copy in tok_loads:
         copy.wait()
     mine = pl.ds(pl.multiple_of(t * share, share), share)
@@ -1231,9 +1227,8 @@
         return copy
 
     first = swap(0, "h")
-    out = token + total_of(0, 7, 3) + out_shift[:, mine]
-    for m in range(2):
-        layer_out[m] = out[m * rows : (m + 1) * rows].astype(jnp.bfloat16)
+    pass_on(0, 4, 1)
+    pass_on(0, 5, 1)
     first.wait_recv()
     ln_v[1] = ln_v[0] + ln_in[0]
     second = swap(1, "l")
@@ -1246,9 +1241,15 @@
         grad_out[m] = (cot[m].astype(jnp.float32) + grad[m * rows : (m + 1) * rows]).astype(jnp.bfloat16)
     second.wait_recv()
     ln_v[2] = ln_v[1] + ln_in[1]
-    swap(2, "x").wait_recv()
+    third = swap(2, "x")
+    pass_on(0, 6, 2)
+    third.wait_recv()
     ln_v[3] = ln_v[2] + ln_in[2]
-    swap(3, "y").wait_recv()
+    fourth = swap(3, "y")
+    out = token + total_of(0, 7, 3) + out_shift[:, mine]
+    for m in range(2):
+        layer_out[m] = out[m * rows : (m + 1) * rows].astype(jnp.bfloat16)
+    fourth.wait_recv()
     ln_v[4] = ln_v[3] + ln_in[3]
     swap(4, "t").wait_recv()
     ln_out[...] = jnp.where(t == y, ln_v[4], ln_in[4])
@@ -1301,7 +1302,7 @@
             sem((6,)),
             sem((6,)),
         ]
-        + join_sems(3),
+        + join_sems(4),
         compiler_params=pltpu.CompilerParams(
             collective_id=3, has_side_effects=True, vmem_limit_bytes=60 << 20
         ),
@@ -1318,18 +1319,29 @@
     )
 
 
-def attend_pack(pack, four, perm, seg_q, seg_k, pos, freq, sign, back_ref, laid, gq, gk, gv, cos_v, sin_v):
+def attend_pack(pack, four, perm, lengths, freq, sign, back_ref, laid, gq, gk, gv, cos_v, sin_v):
     pack_rows, width = laid.shape[0], laid.shape[1] // 4
     bf16, f32 = jnp.bfloat16, jnp.float32
     scale = 64 ** (-0.5)
     lane = lax.broadcasted_iota(jnp.int32, (1, width), 1)
     total = four.shape[1]
+
+    def starts(shape, block):
+        row = lax.broadcasted_iota(jnp.int32, shape, 0) + block * BLOCK
+        begin, end = jnp.zeros(shape, jnp.int32), 0
+        for i in range(SEQUENCES):
+            length = lengths(i)
+            end = end + length
+            begin += jnp.where(row >= end, length, 0)
+        return row, begin
+
     for block in range(pack_rows // BLOCK):
         here = slice(block * BLOCK, (block + 1) * BLOCK)
         target = pack * pack_rows + block * BLOCK + lax.broadcasted_iota(jnp.int32, (BLOCK, total), 0)
         chosen = jnp.where(perm[0] == target, 1.0, 0.0).astype(bf16)
         got = dot(chosen, four[0])
-        angle = pos[0, here, :] * freq[...]
+        row, begin = starts((BLOCK, width), block)
+        angle = (row - begin).astype(f32) * freq[...]
         cos, sin = jnp.cos(angle), jnp.sin(angle) * sign[...]
         cos_v[here, :] = cos
         sin_v[here, :] = sin
@@ -1346,9 +1358,9 @@
         here = slice(block * BLOCK, high)
         keys = laid[low:high, width : 2 * width]
         values = laid[low:high, 2 * width : 3 * width]
-        row = lax.broadcasted_iota(jnp.int32, (BLOCK, high - low), 0) + block * BLOCK
+        row, begin = starts((BLOCK, high - low), block)
         column = lax.broadcasted_iota(jnp.int32, (BLOCK, high - low), 1) + low
-        allowed = (seg_q[0, here, :] == seg_k[0, :, low:high]) & (column <= row)
+        allowed = (column >= begin) & (column <= row)
         attended = None
         for head in range(2):
             mine = (lane // 64) == head
@@ -1382,7 +1394,7 @@
 
 
 def heads_kernel(
-    packs, all_packs, four, perm, seg_q, seg_k, pos, freq, sign, perm_c, normed, cot, g_1, g_2,
+    packs, all_packs, lengths, four, perm, freq, sign, normed, cot, g_1, g_2,
     back_out, g_d, g_q, qkv_sum, j_1, j_2,
     held, laid, gq, gk, gv, cos_v, sin_v, acc_d, acc_q, *join_sem,
 ):
@@ -1408,12 +1420,12 @@
 
     @pl.when(step == all_packs)
     def _():
-        gather.brought()
+        gather.brought("x", "l")
 
     @pl.when(step < all_packs)
     def _():
         attend_pack(
-            lax.rem(step, packs), four, perm, seg_q, seg_k, pos, freq, sign,
+            lax.rem(step, packs), four, perm, lambda i: lengths[step, i], freq, sign,
             held.at[step], laid, gq, gk, gv, cos_v, sin_v,
         )
 
@@ -1424,11 +1436,13 @@
         per = total // size
         pack_rows = held.shape[1]
         first = (step - all_packs) // per * packs
-        column = lax.broadcasted_iota(jnp.int32, (size, pack_rows), 1)
+        at = pl.ds(pl.multiple_of(lax.rem(step - all_packs, per) * size, size), size)
+        line = perm[0, :, at]
+        row = lax.broadcasted_iota(jnp.int32, (pack_rows, size), 0)
         back = None
         for k in range(packs):
-            chosen = jnp.where(perm_c[0] == column + k * pack_rows, 1.0, 0.0).astype(bf16)
-            part = dot(chosen, held[first + k])
+            chosen = jnp.where(line == row + k * pack_rows, 1.0, 0.0).astype(bf16)
+            part = dot(chosen, held[first + k], TN)
             back = part if back is None else back + part
         back = back.astype(bf16)
         back_out[0] = back
@@ -1447,7 +1461,7 @@
         gather.end()
 
 
-def heads(four, permutation, segment, position, normed, cot_all, g_1, g_2, packs, size):
+def heads(lengths, four, permutation, normed, cot_all, g_1, g_2, packs, size):
     micro, total, wide = four.shape
     pack_rows = total // packs
     width = wide // 4
@@ -1459,11 +1473,15 @@
     freq = jnp.where(lane < ROT, power, 0.0)[None, :]
     sign = jnp.where(lane < ROT // 2, -1.0, 1.0)[None, :]
 
-    def by_pack(*s):
-        return pl.BlockSpec((1,) + s, lambda i: (jnp.minimum(i, all_packs - 1), 0, 0))
-
-    def by_micro(*s):
-        return pl.BlockSpec((1,) + s, lambda i: (jnp.minimum(i, all_packs - 1) // packs, 0, 0))
+    def by_micro(*s, after=False):
+        def index(i):
+            if after:
+                i = jnp.where(i < all_packs, i // packs, (i - all_packs) // per)
+            else:
+                i = jnp.minimum(i, all_packs - 1) // packs
+            return (i, 0, 0)
+
+        return pl.BlockSpec((1,) + s, index)
 
     def block(w):
         def index(i):
@@ -1489,14 +1507,11 @@
             jax.ShapeDtypeStruct((g_2.shape[0] * 8, deep // 2), g_2.dtype),
         ],
         in_specs=[
+            pl.BlockSpec(memory_space=pltpu.SMEM),
             by_micro(total, wide),
-            by_micro(1, total),
-            by_pack(pack_rows, 1),
-            by_pack(1, pack_rows),
-            by_pack(pack_rows, 1),
+            by_micro(1, total, after=True),
             fixed(1, width),
             fixed(1, width),
-            block(1),
             block(deep),
             block(deep),
             any_,
@@ -1517,9 +1532,26 @@
         ),
         name="heads",
     )(
-        four, permutation[:, None, :], segment[:, :, None], segment[:, None, :],
-        position.astype(jnp.float32)[:, :, None], freq, sign, permutation[:, :, None], normed, cot_all, g_1, g_2,
-    )
+        lengths.reshape(all_packs, -1), four, permutation[:, None, :], freq, sign, normed, cot_all, g_1, g_2,
+    )
+
+
+def widen_kernel(source, target):
+    target[...] = source[...].astype(jnp.float32)
+
+
+def widen(value, size):
+    rows, columns = value.shape
+    block = pl.BlockSpec((size, columns), lambda i: (i, 0))
+    return pl.pallas_call(
+        widen_kernel,
+        grid=(rows // size,),
+        out_shape=jax.ShapeDtypeStruct(value.shape, jnp.float32),
+        in_specs=[block],
+        out_specs=block,
+        compiler_params=pltpu.CompilerParams(vmem_limit_bytes=56 << 20),
+        name="widen",
+    )(value)
 
 
 def fast_body(
@@ -1549,12 +1581,8 @@
     gain = small[:, 0:share].reshape(1, width)
     out_shift = (small[:, 2 * share : 3 * share] + small[:, 3 * share : 4 * share]).reshape(1, width)
 
-    places = jnp.arange(pack_rows, dtype=jnp.int32)
-    segment, position = jax.vmap(lambda row: segment_layout(row, places))(
-        lengths.reshape(micro * packs, -1)
-    )
     back, g_wd, g_wq, qkv_sum, j_1, j_2 = heads(
-        four, permutation, segment, position, normed, cot_all, g_w1, g_w2, packs, 4 * rows
+        lengths, four, permutation, normed, cot_all, g_w1, g_w2, packs, 4 * rows
     )
     g_bias = jnp.pad(jnp.concatenate([qkv_sum, pre_sum], 1), ((0, 7), (0, 0)))
     layer_out, grad_tokens, g_ln, j_q, j_d, j_b = fold(
@@ -1575,9 +1603,9 @@
         g_qb,
         j_d.astype(f32),
         cot_sum,
-        j_1.astype(f32),
+        widen(j_1, 128),
         g_fb,
-        j_2.astype(f32),
+        widen(j_2, 512),
         cot_sum,
     )
 

time: 595 us -> 552 us (0.928)
  other arithmetic: 40.1 us -> 13.3 us
  Pallas kernels: 526 us -> 516 us
    pallas_call x1, Pallas kernels: 165 us -> 135 us  [fold(): pl.pallas_call(fold_kernel, out_shape=[jax.ShapeDtypeStruct(cot.shape, co...]
    convert_element_type x3 -> x0, other arithmetic: 25.1 us -> none  [the longest x1 11.8 us: fast_body(): j_1.astype(f32)]
    pallas_call x0 -> x2, Pallas kernels: none -> 20.6 us  [widen(): pl.pallas_call(widen_kernel, grid=(rows // size,), out_shape=jax.ShapeDty...]
where the time goes in v5:
time: 552 us; the launch traced here: 545 us
  Pallas kernels  516 us (93%)
  local copies, waits for them, and re-layouts  14.3 us (3%)
  other arithmetic  13.3 us (2%)
    pallas_call x1, Pallas kernels, spread(): pl.pallas_call(spread_kernel, out_shape=[shape(s, bf16) for s in outs + [...  218 us
    pallas_call x1, Pallas kernels, heads(): pl.pallas_call(partial(heads_kernel, packs, all_packs), grid=(all_packs +...  143 us
    pallas_call x1, Pallas kernels, fold(): pl.pallas_call(fold_kernel, out_shape=[jax.ShapeDtypeStruct(cot.shape, co...  135 us
    pallas_call x2, Pallas kernels, widen(): pl.pallas_call(widen_kernel, grid=(rows // size,), out_shape=jax.ShapeDty...  20.6 us

profile of v5, /device:TPU:0, one launch (start us, length us, event | category | flops | bytes accessed | tf_op | source)
XLA Modules:
  0.0 544.6 jit_solution(1843732917628889549)
XLA Ops:
  1.3 1.3 broadcast_in_dim.58.perm
  2.7 0.7 constant_dynamic-update-slice_fusion.5
  3.4 0.7 constant_dynamic-update-slice_fusion.4
  4.1 0.7 constant_dynamic-update-slice_fusion.3
  4.7 0.7 constant_dynamic-update-slice_fusion.2
  5.4 0.7 broadcast_in_dim.55
  6.3 0.7 constant_dynamic-update-slice_fusion
  7.0 0.6 pad.8.small
  7.6 218.0 %spread.1 = (bf16[2,2048,2048]{2,1,0:T(8,128)(2,1)}, bf16[2,2048,2048]{2,1,0:T(8,128)(2,1)}, bf16[3,2048,128]{2,1,0:T(8,128)(2,1)}, bf16[128,2048]{1,0:T(8,128)(...) custom-call(bf16[2,128,1024]{2,1,0:T(8,128)(2,1)} %tok.1, ...), custom_call_target="tpu_custom_call" | custom-call | tf_op jit(solution)/shard_map/spread/pallas_call | solution.py:965
  225.6 0.7 constant_dynamic-slice_fusion.1
  226.3 0.8 convert_bitcast_fusion.1
  228.3 142.7 %heads.1 = (bf16[2,2048,512]{2,1,0:T(8,128)(2,1)}, bf16[128,2048]{1,0:T(8,128)(2,1)}, bf16[3,2048,128]{2,1,0:T(8,128)(2,1)}, f32[1,384]{1,0:T(1,128)}, bf16[1024...) custom-call(s32[4,4]{1,0:T(4,128)} %bitcast.49, bf16[2,2048,512]{2,1,0:T(8,128)(2,1)} %get-tuple-element.41.four, ...), custom_call_target="tpu_custom_call" | custom-call | tf_op jit(solution)/shard_map/heads/pallas_call | solution.py:1498
  371.0 1.2 select_maximum_fusion.g_b
  372.3 134.6 %fold.1 = (bf16[2,128,1024]{2,1,0:T(8,128)(2,1)}, bf16[2,128,1024]{2,1,0:T(8,128)(2,1)}, f32[8,1024]{1,0:T(8,128)}, bf16[3,1024,1024]{2,1,0:T(8,128)(2,1)}, bf16...) custom-call(bf16[2,2048,512]{2,1,0:T(8,128)(2,1)} %get-tuple-element.39.activ, ...), custom_call_target="tpu_custom_call" | custom-call | tf_op jit(solution)/shard_map/fold/pallas_call | solution.py:1272
  506.9 1.4 fusion.5
  508.3 1.0 slice.35
  509.3 0.6 constant_dynamic-slice_fusion
  510.0 0.7 constant_dynamic-slice_fusion.2
  510.7 4.4 convert_element_type.27
  515.1 6.3 %convert_bitcast_fusion = f32[1024,3,1024]{2,0,1:T(8,128)} fusion(bf16[3,1024,1024]{2,1,0:T(8,128)(2,1)S(1)} %copy-done), kind=kLoop, calls=%fused_computation | loop fusion | flops 3145728 | bytes 18874368 | tf_op jit(solution)/shard_map/transpose | solution.py:1602
  521.4 10.3 %widen.2 = f32[1024,4096]{1,0:T(8,128)} custom-call(bf16[1024,4096]{1,0:T(8,128)(2,1)} %get-tuple-element.64.source), custom_call_target="tpu_custom_call" | custom-call | tf_op jit(solution)/shard_map/widen/pallas_call | solution.py:1546
  531.7 10.4 %widen.3 = f32[4096,1024]{1,0:T(8,128)} custom-call(bf16[4096,1024]{1,0:T(8,128)(2,1)} %get-tuple-element.65.source), custom_call_target="tpu_custom_call" | custom-call | tf_op jit(solution)/shard_map/widen/pallas_call | solution.py:1546
  542.6 0.8 copy.43
  543.4 0.8 copy.44
  (26 shorter events, 2.8 us)
Async XLA Ops:
  226.3 315.7 %copy-start.3 = (f32[1,1024]{1,0:T(1,128)}, f32[1,1024]{1,0:T(1,128)S(1)}, u32[]{:S(2)}) copy-start(f32[1,1024]{1,0:T(1,128)S(1)} %constant_dynamic-slice_fusion.1) | copy-start | bytes 12292
  228.3 142.7 %copy-start.4 = (f32[1,512]{1,0:T(1,128)S(1)}, f32[1,512]{1,0:T(1,128)}, u32[]{:S(2)}) copy-start(f32[1,512]{1,0:T(1,128)} %get-tuple-element.51) | copy-start | bytes 6148
  510.0 5.1 copy-start
  531.7 11.0 %copy-start.2 = (bf16[2,128,1024]{2,1,0:T(8,128)(2,1)S(1)}, bf16[2,128,1024]{2,1,0:T(8,128)(2,1)}, u32[]{:S(2)}) copy-start(bf16[2,128,1024]{2,1,0:T(8,128)(2,1)} %get-tuple-element.108) | copy-start | bytes 1572868
  531.7 11.8 %copy-start.1 = (bf16[2,128,1024]{2,1,0:T(8,128)(2,1)S(1)}, bf16[2,128,1024]{2,1,0:T(8,128)(2,1)}, u32[]{:S(2)}) copy-start(bf16[2,128,1024]{2,1,0:T(8,128)(2,1)} %get-tuple-element.109) | copy-start | bytes 1572868

commit v6 on v5

--- a/solution.py
+++ b/solution.py
@@ -592,15 +592,15 @@
 
 
 def spread_kernel(
-    tok, cot, w_q, w_d, w_1, w_2, small,
-    tok_all, cot_all, q_out, d_out, o_1, o_2, small_out, normed_out, activ_out, pre_out, four_out,
+    own_rows, w_q, w_d, w_1, w_2, small,
+    all_rows, q_out, d_out, o_1, o_2, small_out, normed_out, activ_out, pre_out, four_out,
     g_1, g_2, cot_sum, pre_sum,
-    v_q, v_d, v_1, v_2, v_s, acc_1, acc_2, tok_v, cot_v, normed_v, activ_v, pre_v, four_v,
+    v_q, v_d, v_1, v_2, v_s, acc_1, acc_2, rows_v, normed_v, activ_v, pre_v, four_v,
     local_sem, send_sem, recv_sem, in_sem, out_sem,
 ):
     y, h, l, x, t = place()
     z = 2 * h + l
-    rows, half = tok.shape[1], tok.shape[2]
+    rows, half = own_rows.shape[1], own_rows.shape[2]
     other_y, other_x, other_t = {"y": 1 - y}, {"x": 1 - x}, {"t": 1 - t}
 
     def along(zz):
@@ -610,7 +610,7 @@
         [(other_y, True), (other_x, True), (other_t, True)]
         + [(along(lax.max(z - 1, 0)), z > 0), (along(lax.min(z + 1, 3)), z < 3)]
     )
-    units = [(tok, tok_all, 0, 1), (tok, tok_all, 1, 1), (cot, cot_all, 0, 2)]
+    units = [(0, 1), (1, 3)]
     numbers = {}
 
     def number(key):
@@ -622,18 +622,19 @@
         return yy * 8 + zz * 2 + xx
 
     def region(unit, chunk, core):
-        _, out, m, n = units[unit]
+        m, n = units[unit]
         dy, dx, way, k = chunk
-        group = group_at(dy, dx, z - k if way == "up" else z + k)
-        return out.at[
-            pl.ds(m, n),
-            pl.ds(pl.multiple_of(group * rows, rows), rows),
-            pl.ds(pl.multiple_of(core * half, half), half),
-        ]
+        zz = z - k if way == "up" else z + k
+        columns = pl.ds(pl.multiple_of(core * half, half), half)
+        if dy is None:
+            return all_rows.at[pl.ds(m, n), :, zz, :, columns]
+        yy = 1 - y if dy else y
+        xx = 1 - x if dx else x
+        return all_rows.at[pl.ds(m, n), yy, zz, pl.ds(pl.multiple_of(xx * rows, rows), rows), columns]
 
     def own(unit):
-        array, _, m, n = units[unit]
-        return array.at[pl.ds(m, n)]
+        m, n = units[unit]
+        return own_rows.at[pl.ds(m, n)]
 
     started = []
 
@@ -652,8 +653,9 @@
         ref = region(unit, chunk, core)
         link(unit, ref, ref, key, other_t).wait_recv()
 
-    def sent(unit, key):
-        link(unit, own(unit), own(unit), key, other_t).wait_send()
+    def sent(unit, chunk, key):
+        ref = region(unit, chunk, t)
+        link(unit, ref, ref, key, other_t).wait_send()
 
     def when(there, what):
         if there is True:
@@ -690,44 +692,38 @@
     steps = [[("up", 0)], [("up", 1), ("down", 1)], [("up", 2), ("down", 2)], [("up", 3), ("down", 3)]]
 
     def z_step(s):
-        for u in (1, 2):
-            for way, k in steps[s]:
-                def act(u=u, c=(0, 0, way, k)):
-                    got(u, c)
-                    if c[3] < 3:
-                        up_down(u, c)
-                    onward(u, c, "x")
-                    onward(u, c, "y")
-                    to_core(u, c)
-                when(there_of(way, k), act)
+        for way, k in steps[s]:
+            def act(c=(0, 0, way, k)):
+                got(1, c)
+                if c[3] < 3:
+                    up_down(1, c)
+                onward(1, c, "x")
+                onward(1, c, "y")
+                to_core(1, c)
+            when(there_of(way, k), act)
 
     def y_step(s):
-        for u in (1, 2):
-            for way, k in steps[s]:
-                def act(u=u, c=(1, 0, way, k)):
-                    got(u, c)
-                    onward(u, c, "x")
-                    to_core(u, c)
-                when(there_of(way, k), act)
+        for way, k in steps[s]:
+            def act(c=(1, 0, way, k)):
+                got(1, c)
+                onward(1, c, "x")
+                to_core(1, c)
+            when(there_of(way, k), act)
 
     def x_step(s, dy):
-        for u in (1, 2):
-            for way, k in steps[s]:
-                def act(u=u, c=(dy, 1, way, k)):
-                    got(u, c)
-                    to_core(u, c)
-                when(there_of(way, k), act)
+        for way, k in steps[s]:
+            def act(c=(dy, 1, way, k)):
+                got(1, c)
+                to_core(1, c)
+            when(there_of(way, k), act)
 
     def first_step(s):
         for way, k in steps[s]:
-            def act(way=way, k=k):
-                for dy in (0, 1):
-                    for dx in (0, 1):
-                        c = (dy, dx, way, k)
-                        got(0, c)
-                        if k < 3:
-                            up_down(0, c)
-                        to_core(0, c)
+            def act(c=(None, None, way, k)):
+                got(0, c)
+                if c[3] < 3:
+                    up_down(0, c)
+                to_core(0, c)
             when(there_of(way, k), act)
 
     nearest = [
@@ -746,26 +742,17 @@
             value = jnp.where(z == zz, options[zz][j], value)
         return value
 
-    def loads(group, slot):
-        there = pl.ds(pl.multiple_of(group * rows, rows), rows)
-        copies = []
-        for m in range(2):
-            for n, (source, target) in enumerate(((tok_all, tok_v), (cot_all, cot_v))):
-                copies.append(
-                    pltpu.make_async_copy(
-                        source.at[m, there], target.at[slot, pl.ds(m * rows, rows)], in_sem.at[slot, 2 * m + n]
-                    )
-                )
-        return copies
+    def load(group, slot):
+        here = pl.ds(pl.multiple_of(lax.rem(group, 2) * rows, rows), rows)
+        return pltpu.make_async_copy(
+            all_rows.at[:, group // 8, lax.rem(group // 2, 4), here], rows_v.at[slot], in_sem.at[slot]
+        )
 
     def stores(group, slot):
         there = pl.ds(pl.multiple_of(group * rows, rows), rows)
         pairs = ((normed_v, normed_out), (activ_v, activ_out), (pre_v, pre_out), (four_v, four_out))
         return [
-            pltpu.make_async_copy(
-                source.at[slot, pl.ds(m * rows, rows)], target.at[m, there], out_sem.at[slot, 4 * m + n]
-            )
-            for m in range(2)
+            pltpu.make_async_copy(source.at[slot], target.at[:, there], out_sem.at[slot, n])
             for n, (source, target) in enumerate(pairs)
         ]
 
@@ -773,12 +760,13 @@
         dy, dx, j = GROUPS[i]
         for (way, k), there in nearest[j]:
             def wait(way=way, k=k):
-                for u in range(3):
-                    c = (dy, dx, way, k)
+                chunks = [(1, (dy, dx, way, k))]
+                if not dy and not dx:
+                    chunks.append((0, (None, None, way, k)))
+                for u, c in chunks:
                     arrive(u, c, c + ("core",), 1 - t)
             when(there, wait)
-        for copy in loads(group_at(dy, dx, z_at(j)), i % 2):
-            copy.start()
+        load(group_at(dy, dx, z_at(j)), i % 2).start()
 
     block = (y * 4 + l * 2 + x, (1 - y) * 4 + l * 2 + x)
     depth = w_1.shape[0]
@@ -796,23 +784,20 @@
             (w_d.at[n], d_out.at[:, row]),
         ]
 
-    first = (0, 0, "up", 0)
-    for u in (1, 2):
-        up_down(u, first)
-    for u in range(3):
+    first, corner = (0, 0, "up", 0), (None, None, "up", 0)
+    up_down(1, first)
+    for u in range(2):
         onward(u, first, "y")
     weights, locals_ = [], []
     for i, (source, target) in enumerate(pieces(block[1])):
         copy = link("w", source, target, (i,), other_y)
         copy.start()
         weights.append(copy)
-    for u in range(3):
+    for u in range(2):
         onward(u, first, "x")
-        to_core(u, first)
-        copy = pltpu.make_async_copy(own(u), region(u, first, t), local_sem.at[len(locals_)])
-        copy.start()
-        locals_.append(copy)
-    for source, target in pieces(block[0]):
+    to_core(1, first)
+    pairs = [(own(u), region(u, first, t)) for u in range(2)] + pieces(block[0])
+    for source, target in pairs:
         copy = pltpu.make_async_copy(source, target, local_sem.at[len(locals_)])
         copy.start()
         locals_.append(copy)
@@ -822,17 +807,15 @@
     pre_sum[...] = jnp.zeros_like(pre_sum)
     got(0, (1, 0, "up", 0))
     onward(0, (1, 0, "up", 0), "x")
-    up_down(0, first)
-    up_down(0, (1, 0, "up", 0))
-    to_core(0, (1, 0, "up", 0))
     z_step(1)
     for dy in (0, 1):
         got(0, (dy, 1, "up", 0))
-        up_down(0, (dy, 1, "up", 0))
-        to_core(0, (dy, 1, "up", 0))
+    locals_[0].wait()
+    up_down(0, corner)
+    to_core(0, corner)
     for event in ((y_step, 0), (z_step, 2), (y_step, 1), (x_step, 0, 0), (x_step, 0, 1)):
         event[0](*event[1:])
-    for copy in locals_:
+    for copy in locals_[1:]:
         copy.wait()
     fetch(0)
     for copy in weights:
@@ -899,32 +882,31 @@
                 fetch(i + 1)
 
         group = chosen(step)
-        for copy in loads(group, slot):
-            copy.wait()
+        load(group, slot).wait()
 
         @pl.when(step >= 2)
         def _():
             for copy in stores(chosen(step - 2), slot):
                 copy.wait()
 
-        values = tok_v[slot].astype(f32)
+        values = rows_v[slot, 0:2].reshape(2 * rows, -1).astype(f32)
         center = values - jnp.mean(values, axis=1, keepdims=True)
         r = lax.rsqrt(jnp.mean(center * center, axis=1, keepdims=True) + EPSILON)
         normed = (center * r * gain + shift).astype(bf16)
-        normed_v[slot] = normed
-        cots = cot_v[slot]
+        normed_v[slot] = normed.reshape(2, rows, -1)
+        cots = rows_v[slot, 2:4].reshape(2 * rows, -1)
         pre = dot(normed, v_1[...]) + f_shift
         square = pre * pre
         curve = jnp.tanh(ROOT * (pre + CUBE * pre * square))
         activ = (0.5 * pre * (1.0 + curve)).astype(bf16)
         slope = 0.5 * (1.0 + curve) + 0.5 * pre * (1.0 - curve * curve) * (ROOT * (1.0 + 3.0 * CUBE * square))
         grad_pre = (dot(cots, v_2[...], NT) * slope).astype(bf16)
-        activ_v[slot] = activ
-        pre_v[slot] = grad_pre
+        activ_v[slot] = activ.reshape(2, rows, -1)
+        pre_v[slot] = grad_pre.reshape(2, rows, -1)
         for c in range(3):
             at = slice(c * narrow, (c + 1) * narrow)
-            four_v[slot, :, at] = (dot(normed, v_q[c]) + q_shift[c]).astype(bf16)
-        four_v[slot, :, 3 * narrow :] = dot(cots, v_d[...], NT).astype(bf16)
+            four_v[slot, :, :, at] = (dot(normed, v_q[c]) + q_shift[c]).astype(bf16).reshape(2, rows, -1)
+        four_v[slot, :, :, 3 * narrow :] = dot(cots, v_d[...], NT).astype(bf16).reshape(2, rows, -1)
         acc_1[...] += dot(normed, grad_pre, TN)
         acc_2[...] += dot(activ, cots, TN)
         cot_sum[...] += jnp.sum(cots.astype(f32), axis=0, keepdims=True)
@@ -947,40 +929,42 @@
         if going is not None:
             can = z < 3 if going == "up" else z > 0
             there = can if there is True else can & there
-        when(there, lambda: sent(unit, key))
-
-
-def spread(tokens, cotangent, w_q, w_d, w_1, w_2, small):
-    micro, rows, half = tokens.shape
+        when(there, lambda: sent(unit, chunk[:2] + first[2:], key))
+
+
+def spread(own_rows, w_q, w_d, w_1, w_2, small):
+    arrays, rows, half = own_rows.shape
+    micro = arrays // 2
     total, deep = rows * 16, half * 2
     wide, narrow = w_1.shape[1] // 8, w_d.shape[0] // 8
     bf16, f32 = jnp.bfloat16, jnp.float32
     shape = jax.ShapeDtypeStruct
     weights = [(3, deep, narrow), (narrow, deep), (deep, wide), (wide, deep), (2,) + small.shape]
-    outs = [(micro, total, deep)] * 2 + weights
+    outs = [(arrays, 2, 4, 2 * rows, deep)] + weights
     outs += [(micro, total, deep), (micro, total, wide), (micro, total, wide), (micro, total, 4 * narrow)]
-    both = micro * rows
     any_, vmem = pl.BlockSpec(memory_space=pl.ANY), pl.BlockSpec(memory_space=pltpu.VMEM)
     sem = pltpu.SemaphoreType.DMA
     return pl.pallas_call(
         spread_kernel,
         out_shape=[shape(s, bf16) for s in outs + [(deep, wide), (wide, deep)]]
         + [shape((1, deep), f32), shape((1, wide), f32)],
-        in_specs=[any_] * 7,
+        in_specs=[any_] * 6,
         out_specs=[any_] * len(outs) + [vmem] * 4,
         scratch_shapes=[pltpu.VMEM(s, bf16) for s in weights]
         + [pltpu.VMEM((deep, wide), f32), pltpu.VMEM((wide, deep), f32)]
-        + [pltpu.VMEM((2, both, w), bf16) for w in (deep, deep, deep, wide, wide, 4 * narrow)]
-        + [sem((8,)), sem((176,)), sem((176,)), sem((2, 4)), sem((2, 8))],
+        + [pltpu.VMEM((2, arrays, rows, deep), bf16)]
+        + [pltpu.VMEM((2, micro, rows, w), bf16) for w in (deep, wide, wide, 4 * narrow)]
+        + [sem((8,)), sem((96,)), sem((96,)), sem((2,)), sem((2, 4))],
         compiler_params=pltpu.CompilerParams(
             collective_id=0, has_side_effects=True, vmem_limit_bytes=56 << 20
         ),
         name="spread",
-    )(tokens, cotangent, w_q, w_d, w_1, w_2, small)
+    )(own_rows, w_q, w_d, w_1, w_2, small)
 
 
 class Join:
-    def __init__(self, parts, outs, local_sem, send_sem, recv_sem):
+    def __init__(self, parts, outs, local_sem, send_sem, recv_sem, here=()):
+        self.here = dict(here)
         self.parts, self.outs = parts, outs
         self.local_sem, self.send_sem, self.recv_sem = local_sem, send_sem, recv_sem
         self.y, self.h, self.l, self.x, self.t = place()
@@ -1029,6 +1013,8 @@
 
     def bring(self):
         for i in self.every:
+            if i in self.here:
+                continue
             self.send(i, self.half_of(i, 1 - self.y), self.own(i, self.y), ("y",), "y")
 
     def offer(self, axis):
@@ -1040,9 +1026,15 @@
     def kept(self, i):
         return pltpu.make_async_copy(self.half_of(i, self.y), self.own(i, self.y), self.local_sem.at[i])
 
+    def kept_here(self, i):
+        where = self.local_sem.at[len(self.parts) + i]
+        return pltpu.make_async_copy(self.here[i], self.own(i, 1 - self.y), where)
+
     def keep(self):
         for i in self.every:
             self.kept(i).start()
+        for i in self.here:
+            self.kept_here(i).start()
 
     def far(self, side, axis=None):
         yy = 1 - self.y if side else self.y
@@ -1057,10 +1049,10 @@
         for n, axis in enumerate(axes):
             for i in self.every:
                 ref = self.own(i, 1 - self.y)
-                if (i, "y") not in self.met:
-                    self.met.add((i, "y"))
+                if i not in self.here and i not in self.met:
+                    self.met.add(i)
                     self.got(i, ref, ("y",))
-                self.send(i, ref, ref, (1, axis), axis)
+                self.send(i, self.here.get(i, ref), ref, (1, axis), axis)
 
     def end(self):
         for i in self.every:
@@ -1069,17 +1061,19 @@
                 self.got(i, self.spot(i, yy, 1 - self.l, 1 - self.x), (side, "far"))
         for i in self.every:
             self.kept(i).wait()
+        for i in self.here:
+            self.kept_here(i).wait()
         for n, i, axis in self.sends:
             self.copy(n, self.own(i, self.y), self.own(i, self.y), axis).wait_send()
 
 
 def join_sems(count):
     sem = pltpu.SemaphoreType.DMA
-    return [sem((count,)), sem((7 * count,)), sem((7 * count,))]
+    return [sem((2 * count,)), sem((7 * count,)), sem((7 * count,))]
 
 
 def fold_kernel(
-    activ, grad_pre, back, tok_all, g_q, g_d, g_b, cot, w_1, w_2, w_q, w_d, gain, out_shift,
+    activ, grad_pre, back, tok_all, g_q, g_d, g_b, b_q, b_d, cot, w_1, w_2, w_q, w_d, gain, out_shift,
     layer_out, grad_out, ln_out, j_q, j_d, j_b, act_v, pre_v, back_v, tok_v, give, core_in, give_n, sum_in, stat_v, stat_in, ln_v, ln_in,
     load_sem, core_send, core_recv, hop_send, hop_recv, small_send, small_recv, *join_sem,
 ):
@@ -1118,7 +1112,9 @@
     greet([(device[a], True) for a in ("t", "x", "y", "l", "h")])
     two, three = pl.ds(0, 2), pl.ds(2, 1)
     parts = [(g_q.at[two], 1, 2, "x"), (g_q.at[three], 1, 2, "l"), (g_d, 1, 0, "l"), (g_b, None, 0, "l")]
-    gather = Join(parts, (j_q.at[two], j_q.at[three], j_d, j_b), *join_sem)
+    gather = Join(
+        parts, (j_q.at[two], j_q.at[three], j_d, j_b), *join_sem, here=enumerate((b_q.at[two], b_q.at[three], b_d))
+    )
     gather.bring()
     gather.offer("x")
     gather.offer("l")
@@ -1184,15 +1180,15 @@
         if i + 2 < len(queue):
             offer(*queue[i + 2])
         pass_on(a, o, 0)
-    gather.brought("x", "l")
+    gather.brought("l")
     for a, o in [(1, 4), (1, 6), (1, 5), (1, 7), (0, 4), (0, 5), (0, 6), (0, 7)]:
         offer(a, o)
     pass_on(1, 4, 1)
     pass_on(1, 6, 1)
+    gather.brought("x")
+    pass_on(1, 5, 2)
     gather.far(0, "x")
     gather.far(0, "l")
-    pass_on(1, 5, 2)
-    gather.far(1)
     for copy in tok_loads:
         copy.wait()
     mine = pl.ds(pl.multiple_of(t * share, share), share)
@@ -1228,6 +1224,7 @@
 
     first = swap(0, "h")
     pass_on(0, 4, 1)
+    gather.far(1)
     pass_on(0, 5, 1)
     first.wait_recv()
     ln_v[1] = ln_v[0] + ln_in[0]
@@ -1262,7 +1259,7 @@
     gather.end()
 
 
-def fold(activ, grad_pre, back, tok_all, g_q, g_d, g_b, cot, w_1, w_2, w_q, w_d, gain, out_shift):
+def fold(activ, grad_pre, back, tok_all, g_q, g_d, g_b, b_q, b_d, cot, w_1, w_2, w_q, w_d, gain, out_shift):
     micro, rows, share = cot.shape
     both = micro * rows
     narrow = w_d.shape[0]
@@ -1279,7 +1276,7 @@
             jax.ShapeDtypeStruct((share, share), g_d.dtype),
             jax.ShapeDtypeStruct((64, g_b.shape[1]), g_b.dtype),
         ],
-        in_specs=[any_] * 7 + [vmem] * 7,
+        in_specs=[any_] * 9 + [vmem] * 7,
         out_specs=[vmem] * 3 + [any_] * 3,
         scratch_shapes=[
             held(8, w_1.shape[1]),
@@ -1307,7 +1304,7 @@
             collective_id=3, has_side_effects=True, vmem_limit_bytes=60 << 20
         ),
         name="fold",
-    )(activ, grad_pre, back, tok_all, g_q, g_d, g_b, cot, w_1, w_2, w_q, w_d, gain, out_shift)
+    )(activ, grad_pre, back, tok_all, g_q, g_d, g_b, b_q, b_d, cot, w_1, w_2, w_q, w_d, gain, out_shift)
 
 
 def swap_rotary(values):
@@ -1395,8 +1392,8 @@
 
 def heads_kernel(
     packs, all_packs, lengths, four, perm, freq, sign, normed, cot, g_1, g_2,
-    back_out, g_d, g_q, qkv_sum, j_1, j_2,
-    held, laid, gq, gk, gv, cos_v, sin_v, acc_d, acc_q, *join_sem,
+    back_out, g_d, g_q, qkv_sum, j_1, j_2, b_q, b_d,
+    held, laid, gq, gk, gv, cos_v, sin_v, acc_d, acc_q, bring_send, bring_recv, *join_sem,
 ):
     step = pl.program_id(0)
     last = pl.num_programs(0) - 1
@@ -1457,11 +1454,23 @@
         g_d[...] = acc_d[...].astype(bf16)
         for c in range(3):
             g_q[c] = acc_q[:, c * narrow : (c + 1) * narrow].astype(bf16)
+        half = acc_q.shape[0] // 2
+        other = pl.ds(pl.multiple_of((1 - gather.y) * half, half), half)
+        copies = []
+        for i, (source, target) in enumerate(((g_q.at[:, other], b_q), (g_d.at[:, other], b_d))):
+            copy = pltpu.make_async_remote_copy(
+                src_ref=source, dst_ref=target, send_sem=bring_send.at[i], recv_sem=bring_recv.at[i],
+                device_id=gather.device["y"], device_id_type=MESH,
+            )
+            copy.start()
+            copies.append(copy)
         gather.far(1)
         gather.end()
-
-
-def heads(lengths, four, permutation, normed, cot_all, g_1, g_2, packs, size):
+        for copy in copies:
+            copy.wait()
+
+
+def heads(lengths, four, permutation, normed, all_rows, g_1, g_2, packs, size):
     micro, total, wide = four.shape
     pack_rows = total // packs
     width = wide // 4
@@ -1483,10 +1492,10 @@
 
         return pl.BlockSpec((1,) + s, index)
 
-    def block(w):
+    def block(w, skip=0):
         def index(i):
             n = jnp.maximum(i - all_packs, 0)
-            return (n // per, lax.rem(n, per), 0)
+            return (n // per + skip, lax.rem(n, per), 0)
 
         return pl.BlockSpec((1, size, w), index)
 
@@ -1505,6 +1514,8 @@
             jax.ShapeDtypeStruct((1, 3 * width), jnp.float32),
             jax.ShapeDtypeStruct((deep // 2, g_1.shape[1] * 8), g_1.dtype),
             jax.ShapeDtypeStruct((g_2.shape[0] * 8, deep // 2), g_2.dtype),
+            jax.ShapeDtypeStruct((3, deep // 2, width), jnp.bfloat16),
+            jax.ShapeDtypeStruct((width, deep // 2), jnp.bfloat16),
         ],
         in_specs=[
             pl.BlockSpec(memory_space=pltpu.SMEM),
@@ -1513,12 +1524,13 @@
             fixed(1, width),
             fixed(1, width),
             block(deep),
-            block(deep),
+            block(deep, micro),
             any_,
             any_,
         ],
         out_specs=[
-            block(wide), fixed(width, deep), fixed(3, deep, width), fixed(1, 3 * width), any_, any_,
+            block(wide), fixed(width, deep), fixed(3, deep, width), fixed(1, 3 * width),
+            any_, any_, any_, any_,
         ],
         scratch_shapes=[
             pltpu.VMEM((all_packs, pack_rows, wide), jnp.bfloat16),
@@ -1526,32 +1538,36 @@
         ]
         + [plane] * 5
         + [pltpu.VMEM((width, deep), jnp.float32), pltpu.VMEM((deep, 3 * width), jnp.float32)]
+        + [pltpu.SemaphoreType.DMA((2,))] * 2
         + join_sems(2),
         compiler_params=pltpu.CompilerParams(
             collective_id=1, has_side_effects=True, vmem_limit_bytes=56 << 20
         ),
         name="heads",
     )(
-        lengths.reshape(all_packs, -1), four, permutation[:, None, :], freq, sign, normed, cot_all, g_1, g_2,
-    )
-
-
-def widen_kernel(source, target):
-    target[...] = source[...].astype(jnp.float32)
-
-
-def widen(value, size):
-    rows, columns = value.shape
-    block = pl.BlockSpec((size, columns), lambda i: (i, 0))
+        lengths.reshape(all_packs, -1), four, permutation[:, None, :], freq, sign, normed, all_rows, g_1, g_2,
+    )
+
+
+def widen_kernel(*refs):
+    half = len(refs) // 2
+    for source, target in zip(refs[:half], refs[half:]):
+        target[...] = source[...].astype(jnp.float32)
+
+
+def widen(values, steps):
+    def block(value):
+        return pl.BlockSpec((value.shape[0] // steps, value.shape[1]), lambda i: (i, 0))
+
     return pl.pallas_call(
         widen_kernel,
-        grid=(rows // size,),
-        out_shape=jax.ShapeDtypeStruct(value.shape, jnp.float32),
-        in_specs=[block],
-        out_specs=block,
+        grid=(steps,),
+        out_shape=[jax.ShapeDtypeStruct(v.shape, jnp.float32) for v in values],
+        in_specs=[block(v) for v in values],
+        out_specs=[block(v) for v in values],
         compiler_params=pltpu.CompilerParams(vmem_limit_bytes=56 << 20),
         name="widen",
-    )(value)
+    )(*values)
 
 
 def fast_body(
@@ -1572,21 +1588,23 @@
     turned = jnp.where(at_y, turned, jnp.zeros_like(turned)).reshape(24, 128)
     small = jnp.concatenate([flat, turned, fc1_bias])
     small = jnp.pad(small, ((0, SMALL_ROWS - small.shape[0]), (0, 0)))
+    own_rows = jnp.concatenate([tokens, cotangent])
     (
-        tok_all, cot_all, w_q, w_d, w_1, w_2, small, normed, activ, grad_pre, four, g_w1, g_w2, cot_sum, pre_sum,
+        all_rows, w_q, w_d, w_1, w_2, small, normed, activ, grad_pre, four, g_w1, g_w2, cot_sum, pre_sum,
     ) = spread(
-        tokens, cotangent, qkv_weight.transpose(1, 0, 2), dense_weight, fc1_weight, fc2_weight, small
-    )
+        own_rows, qkv_weight.transpose(1, 0, 2), dense_weight, fc1_weight, fc2_weight, small
+    )
+    all_rows = all_rows.reshape(2 * micro, total, width)
     small = small.reshape(2, -1).astype(f32)
     gain = small[:, 0:share].reshape(1, width)
     out_shift = (small[:, 2 * share : 3 * share] + small[:, 3 * share : 4 * share]).reshape(1, width)
 
-    back, g_wd, g_wq, qkv_sum, j_1, j_2 = heads(
-        lengths, four, permutation, normed, cot_all, g_w1, g_w2, packs, 4 * rows
+    back, g_wd, g_wq, qkv_sum, j_1, j_2, b_q, b_d = heads(
+        lengths, four, permutation, normed, all_rows, g_w1, g_w2, packs, 4 * rows
     )
     g_bias = jnp.pad(jnp.concatenate([qkv_sum, pre_sum], 1), ((0, 7), (0, 0)))
     layer_out, grad_tokens, g_ln, j_q, j_d, j_b = fold(
-        activ, grad_pre, back, tok_all, g_wq, g_wd, g_bias, cotangent, w_1, w_2, w_q, w_d, gain, out_shift
+        activ, grad_pre, back, all_rows, g_wq, g_wd, g_bias, b_q, b_d, cotangent, w_1, w_2, w_q, w_d, gain, out_shift
     )
     g_bias = j_b.reshape(8, 8, -1)[:, 0]
     g_qb = g_bias[:, : 3 * narrow].reshape(8, 3, narrow).transpose(1, 0, 2).reshape(3, -1, 64)
@@ -1594,18 +1612,20 @@
     g_fb = g_bias[:, 3 * narrow :].reshape(fc1_bias.shape[0], -1)
     g_fb = lax.dynamic_slice_in_dim(g_fb, y * fc1_bias.shape[1], fc1_bias.shape[1], 1)
     cot_sum = lax.dynamic_slice_in_dim(cot_sum[0], y * share, share, 0)
+    j_1, j_2, j_q, j_d = widen([j_1, j_2, j_q.reshape(3 * share, share), j_d], 16)
+    j_q = j_q.reshape(3, share, share)
     return (
         layer_out,
         grad_tokens,
         g_ln[0],
         g_ln[1],
-        j_q.astype(f32).transpose(1, 0, 2),
+        j_q.transpose(1, 0, 2),
         g_qb,
-        j_d.astype(f32),
+        j_d,
         cot_sum,
-        widen(j_1, 128),
+        j_1,
         g_fb,
-        widen(j_2, 512),
+        j_2,
         cot_sum,
     )
 

time: 552 us -> 545 us (0.987)
  other arithmetic: 13.3 us -> 4.9 us
    transpose x1 -> x0, other arithmetic: 6.31 us -> none  [fast_body(): j_q.astype(f32).transpose(1, 0, 2)]
    pallas_call x2 -> x1, Pallas kernels: 20.6 us -> 26.6 us  [widen(): pl.pallas_call(widen_kernel, grid=(steps,), out_shape=[jax.ShapeDtypeStru...]
where the time goes in v6:
time: 545 us; the launch traced here: 538 us
  Pallas kernels  518 us (95%)
  local copies, waits for them, and re-layouts  14.3 us (3%)
    pallas_call x1, Pallas kernels, spread(): pl.pallas_call(spread_kernel, out_shape=[shape(s, bf16) for s in outs + [...  216 us
    pallas_call x1, Pallas kernels, heads(): pl.pallas_call(partial(heads_kernel, packs, all_packs), grid=(all_packs +...  144 us
    pallas_call x1, Pallas kernels, fold(): pl.pallas_call(fold_kernel, out_shape=[jax.ShapeDtypeStruct(cot.shape, co...  131 us
    pallas_call x1, Pallas kernels, widen(): pl.pallas_call(widen_kernel, grid=(steps,), out_shape=[jax.ShapeDtypeStru...  26.6 us

profile of v6, /device:TPU:0, one launch (start us, length us, event | category | flops | bytes accessed | tf_op | source)
XLA Modules:
  0.0 538.2 jit_solution(12519700217821529754)
XLA Ops:
  1.3 1.3 broadcast_in_dim.58.perm
  2.7 0.7 constant_dynamic-update-slice_fusion.5
  3.4 0.7 constant_dynamic-update-slice_fusion.4
  4.1 0.7 constant_dynamic-update-slice_fusion.3
  4.7 0.7 constant_dynamic-update-slice_fusion.2
  5.4 0.7 broadcast_in_dim.55
  6.3 0.7 constant_dynamic-update-slice_fusion
  7.0 0.6 pad.8.small
  7.6 2.3 pad_maximum_fusion.own_rows
  9.8 216.3 %spread.1 = (bf16[4,2,4,256,2048]{4,3,2,1,0:T(8,128)(2,1)}, bf16[3,2048,128]{2,1,0:T(8,128)(2,1)}, bf16[128,2048]{1,0:T(8,128)(2,1)}, bf16[2048,512]{1,0:T(8,128...) custom-call(bf16[4,128,1024]{2,1,0:T(8,128)(2,1)} %pad_maximum_fusio, ...), custom_call_target="tpu_custom_call" | custom-call | tf_op jit(solution)/shard_map/spread/pallas_call | solution.py:947
  226.2 0.7 constant_dynamic-slice_fusion.1
  226.9 0.8 convert_bitcast_fusion
  227.7 0.6 copy.29
  228.3 0.6 copy.28
  228.9 144.1 %heads.1 = (bf16[2,2048,512]{2,1,0:T(8,128)(2,1)}, bf16[128,2048]{1,0:T(8,128)(2,1)}, bf16[3,2048,128]{2,1,0:T(8,128)(2,1)}, f32[1,384]{1,0:T(1,128)}, bf16[1024...) custom-call(s32[4,4]{1,0:T(4,128)} %bitcast.55, ...), custom_call_target="tpu_custom_call" | custom-call | tf_op jit(solution)/shard_map/heads/pallas_call | solution.py:1507
  373.1 1.3 select_maximum_fusion.g_b
  374.4 130.8 %fold.1 = (bf16[2,128,1024]{2,1,0:T(8,128)(2,1)}, bf16[2,128,1024]{2,1,0:T(8,128)(2,1)}, f32[8,1024]{1,0:T(8,128)}, bf16[3,1024,1024]{2,1,0:T(8,128)(2,1)}, bf16...) custom-call(bf16[2,2048,512]{2,1,0:T(8,128)(2,1)} %get-tuple-element.44.activ, ...), custom_call_target="tpu_custom_call" | custom-call | tf_op jit(solution)/shard_map/fold/pallas_call | solution.py:1269
  505.2 1.4 fusion.5
  506.6 1.0 slice.35
  507.6 0.6 constant_dynamic-slice_fusion
  508.3 0.7 constant_dynamic-slice_fusion.2
  509.0 26.6 %widen.1 = (f32[1024,4096]{1,0:T(8,128)}, f32[4096,1024]{1,0:T(8,128)}, f32[3072,1024]{1,0:T(8,128)}, f32[1024,1024]{1,0:T(8,128)}) custom-call(bf16[1024,4096]{1,0:T(8,128)(2,1)} %get-tuple-element.66.refs_0_, bf16[4096,1024]{1,0:T(8,128)(2,1)} %get-tuple-element.67.refs_1_, bf16[3072,1024]{1,0:T(8,128)(2,1)} %bitcast.43, ...), custom_call_target="tpu_custom_call" | custom-call | tf_op jit(solution)/shard_map/widen/pallas_call | solution.py:1562
  536.1 0.8 copy.43
  536.9 0.8 copy.44
  (22 shorter events, 1.5 us)
Async XLA Ops:
  226.9 308.7 %copy-start.2 = (f32[1,1024]{1,0:T(1,128)}, f32[1,1024]{1,0:T(1,128)S(1)}, u32[]{:S(2)}) copy-start(f32[1,1024]{1,0:T(1,128)S(1)} %constant_dynamic-slice_fusion.1) | copy-start | bytes 12292
  228.9 144.1 %copy-start.3 = (f32[1,512]{1,0:T(1,128)S(1)}, f32[1,512]{1,0:T(1,128)}, u32[]{:S(2)}) copy-start(f32[1,512]{1,0:T(1,128)} %get-tuple-element.55) | copy-start | bytes 6148
  509.0 27.2 %copy-start.1 = (bf16[2,128,1024]{2,1,0:T(8,128)(2,1)S(1)}, bf16[2,128,1024]{2,1,0:T(8,128)(2,1)}, u32[]{:S(2)}) copy-start(bf16[2,128,1024]{2,1,0:T(8,128)(2,1)} %get-tuple-element.118) | copy-start | bytes 1572868
  509.0 28.0 %copy-start = (bf16[2,128,1024]{2,1,0:T(8,128)(2,1)S(1)}, bf16[2,128,1024]{2,1,0:T(8,128)(2,1)}, u32[]{:S(2)}) copy-start(bf16[2,128,1024]{2,1,0:T(8,128)(2,1)} %get-tuple-element.119) | copy-start | bytes 1572868

commit v7 on v6

--- a/solution.py
+++ b/solution.py
@@ -1612,7 +1612,7 @@
     g_fb = g_bias[:, 3 * narrow :].reshape(fc1_bias.shape[0], -1)
     g_fb = lax.dynamic_slice_in_dim(g_fb, y * fc1_bias.shape[1], fc1_bias.shape[1], 1)
     cot_sum = lax.dynamic_slice_in_dim(cot_sum[0], y * share, share, 0)
-    j_1, j_2, j_q, j_d = widen([j_1, j_2, j_q.reshape(3 * share, share), j_d], 16)
+    j_1, j_2, j_q, j_d = widen([j_1, j_2, j_q.reshape(3 * share, share), j_d], 8)
     j_q = j_q.reshape(3, share, share)
     return (
         layer_out,

time: 545 us -> 543 us (level)
  no operation moved by 1% of the time
where the time goes in v7:
time: 543 us; the launch traced here: 537 us
  Pallas kernels  516 us (95%)
  local copies, waits for them, and re-layouts  14.3 us (3%)
    pallas_call x1, Pallas kernels, spread(): pl.pallas_call(spread_kernel, out_shape=[shape(s, bf16) for s in outs + [...  216 us
    pallas_call x1, Pallas kernels, heads(): pl.pallas_call(partial(heads_kernel, packs, all_packs), grid=(all_packs +...  144 us
    pallas_call x1, Pallas kernels, fold(): pl.pallas_call(fold_kernel, out_shape=[jax.ShapeDtypeStruct(cot.shape, co...  131 us
    pallas_call x1, Pallas kernels, widen(): pl.pallas_call(widen_kernel, grid=(steps,), out_shape=[jax.ShapeDtypeStru...  25.1 us

profile of v7, /device:TPU:0, one launch (start us, length us, event | category | flops | bytes accessed | tf_op | source)
XLA Modules:
  0.0 536.8 jit_solution(3755921808048091562)
XLA Ops:
  1.3 1.3 broadcast_in_dim.58.perm
  2.7 0.7 constant_dynamic-update-slice_fusion.5
  3.4 0.7 constant_dynamic-update-slice_fusion.4
  4.1 0.7 constant_dynamic-update-slice_fusion.3
  4.7 0.7 constant_dynamic-update-slice_fusion.2
  5.4 0.7 broadcast_in_dim.55
  6.3 0.7 constant_dynamic-update-slice_fusion
  7.0 0.6 pad.8.small
  7.6 2.3 pad_maximum_fusion.own_rows
  9.8 216.3 %spread.1 = (bf16[4,2,4,256,2048]{4,3,2,1,0:T(8,128)(2,1)}, bf16[3,2048,128]{2,1,0:T(8,128)(2,1)}, bf16[128,2048]{1,0:T(8,128)(2,1)}, bf16[2048,512]{1,0:T(8,128...) custom-call(bf16[4,128,1024]{2,1,0:T(8,128)(2,1)} %pad_maximum_fusio, ...), custom_call_target="tpu_custom_call" | custom-call | tf_op jit(solution)/shard_map/spread/pallas_call | solution.py:947
  226.2 0.7 constant_dynamic-slice_fusion.1
  226.9 0.8 convert_bitcast_fusion
  227.7 0.6 copy.29
  228.3 0.6 copy.28
  228.9 144.1 %heads.1 = (bf16[2,2048,512]{2,1,0:T(8,128)(2,1)}, bf16[128,2048]{1,0:T(8,128)(2,1)}, bf16[3,2048,128]{2,1,0:T(8,128)(2,1)}, f32[1,384]{1,0:T(1,128)}, bf16[1024...) custom-call(s32[4,4]{1,0:T(4,128)} %bitcast.55, ...), custom_call_target="tpu_custom_call" | custom-call | tf_op jit(solution)/shard_map/heads/pallas_call | solution.py:1507
  373.1 1.3 select_maximum_fusion.g_b
  374.4 130.8 %fold.1 = (bf16[2,128,1024]{2,1,0:T(8,128)(2,1)}, bf16[2,128,1024]{2,1,0:T(8,128)(2,1)}, f32[8,1024]{1,0:T(8,128)}, bf16[3,1024,1024]{2,1,0:T(8,128)(2,1)}, bf16...) custom-call(bf16[2,2048,512]{2,1,0:T(8,128)(2,1)} %get-tuple-element.44.activ, ...), custom_call_target="tpu_custom_call" | custom-call | tf_op jit(solution)/shard_map/fold/pallas_call | solution.py:1269
  505.2 1.4 fusion.5
  506.6 1.0 slice.35
  507.6 0.6 constant_dynamic-slice_fusion
  508.3 0.7 constant_dynamic-slice_fusion.2
  509.0 25.1 %widen.1 = (f32[1024,4096]{1,0:T(8,128)}, f32[4096,1024]{1,0:T(8,128)}, f32[3072,1024]{1,0:T(8,128)}, f32[1024,1024]{1,0:T(8,128)}) custom-call(bf16[1024,4096]{1,0:T(8,128)(2,1)} %get-tuple-element.66.refs_0_, bf16[4096,1024]{1,0:T(8,128)(2,1)} %get-tuple-element.67.refs_1_, bf16[3072,1024]{1,0:T(8,128)(2,1)} %bitcast.43, ...), custom_call_target="tpu_custom_call" | custom-call | tf_op jit(solution)/shard_map/widen/pallas_call | solution.py:1562
  534.7 0.8 copy.43
  535.5 0.8 copy.44
  (22 shorter events, 1.5 us)
Async XLA Ops:
  226.9 307.2 %copy-start.2 = (f32[1,1024]{1,0:T(1,128)}, f32[1,1024]{1,0:T(1,128)S(1)}, u32[]{:S(2)}) copy-start(f32[1,1024]{1,0:T(1,128)S(1)} %constant_dynamic-slice_fusion.1) | copy-start | bytes 12292
  228.9 144.1 %copy-start.3 = (f32[1,512]{1,0:T(1,128)S(1)}, f32[1,512]{1,0:T(1,128)}, u32[]{:S(2)}) copy-start(f32[1,512]{1,0:T(1,128)} %get-tuple-element.55) | copy-start | bytes 6148
  509.0 25.8 %copy-start.1 = (bf16[2,128,1024]{2,1,0:T(8,128)(2,1)S(1)}, bf16[2,128,1024]{2,1,0:T(8,128)(2,1)}, u32[]{:S(2)}) copy-start(bf16[2,128,1024]{2,1,0:T(8,128)(2,1)} %get-tuple-element.118) | copy-start | bytes 1572868
  509.0 26.5 %copy-start = (bf16[2,128,1024]{2,1,0:T(8,128)(2,1)S(1)}, bf16[2,128,1024]{2,1,0:T(8,128)(2,1)}, u32[]{:S(2)}) copy-start(bf16[2,128,1024]{2,1,0:T(8,128)(2,1)} %get-tuple-element.119) | copy-start | bytes 1572868
